TPU v7x, 32 devices: a whole 2x2x4 slice. The times are simulated.
32 devices in a mesh: fsdp: 4 (over x, core), seq: 8 (over z, y).
Axes of the slice: x: 2, y: 2, z: 4, core: 2. Of those that a mesh axis runs over, the one named last changes fastest.
Arguments:
- tokens: bfloat16 [4096, 1024], P(('fsdp', 'seq')), may hold values from -6 to 6
- attn_gain: bfloat16 [1024], P('fsdp'), may hold values from 0.099609375 to 1.8984375
- w_query: bfloat16 [1024, 1024], P('fsdp'), may hold values from -0.375 to 0.375
- w_latent: bfloat16 [1024, 512], P('fsdp'), may hold values from -0.1875 to 0.1875
- w_key_up: bfloat16 [256, 1024], P(None, 'fsdp'), may hold values from -0.375 to 0.375
- w_value_up: bfloat16 [256, 1024], P(None, 'fsdp'), may hold values from -0.375 to 0.375
- w_out: bfloat16 [1024, 1024], P('fsdp'), may hold values from -0.75 to 0.75
- mlp_gain: bfloat16 [1024], P('fsdp'), may hold values from 0.099609375 to 1.8984375
- w_gate: bfloat16 [1024, 2816], P('fsdp'), may hold values from -0.1875 to 0.1875
- w_up: bfloat16 [1024, 2816], P('fsdp'), may hold values from -0.1875 to 0.1875
- w_down: bfloat16 [2816, 1024], P('fsdp'), may hold values from -0.109375 to 0.109375
- lengths: int32 [4, 4], P('fsdp'), may hold values from 1 to 1021, as said below
- cotangent: bfloat16 [4096, 1024], P(('fsdp', 'seq')), may hold values from -6 to 6
Outputs:
- output: bfloat16 [4096, 1024], P(('fsdp', 'seq'))
- tokens_grad: bfloat16 [4096, 1024], P(('fsdp', 'seq'))
- grad_attn_gain: float32 [1024], P(('fsdp', 'seq'))
- grad_query: float32 [1024, 1024], P('fsdp', 'seq')
- grad_latent: float32 [1024, 512], P('fsdp', 'seq')
- grad_key_up: float32 [256, 1024], P(None, ('fsdp', 'seq'))
- grad_value_up: float32 [256, 1024], P(None, ('fsdp', 'seq'))
- grad_out: float32 [1024, 1024], P('seq', 'fsdp')
- grad_mlp_gain: float32 [1024], P(('fsdp', 'seq'))
- grad_gate: float32 [1024, 2816], P('fsdp', 'seq')
- grad_up: float32 [1024, 2816], P('fsdp', 'seq')
- grad_down: float32 [2816, 1024], P('seq', 'fsdp')
Inputs may be any that keep to these rules, and one draw needn't show every extreme that they name: In each row, 4 document lengths that sum to 1024; the second document starts within the group's first 128 rows and ends within its last 128 rows.
All inputs are finite; a program needn't handle non-finite values.
Results may differ from a plain program's by a relative error of at most 0.018.
Values may be sent and summed in bfloat16 or wider, within the bound.
No kernel may reach another device: no remote copies, remote signals or barrier semaphores. Data moves between devices by JAX's collectives and lax.ppermute only.
A program may use at most 256 MiB of HBM per device.

v0:
```python
import jax
import jax.numpy as jnp
from jax import lax
from jax.sharding import PartitionSpec as P

HEADS = 16
HD = 64
GROUPS = 2
LAT_HEAD = 256
KEYBLK = 1024
QW = 1024
GQ = 8


epsilon = 1e-06


def normalize(values, gain):
    return values * lax.rsqrt(jnp.mean(values * values, axis=-1, keepdims=True) + epsilon) * gain


def doc_numbers(lengths_row, count):
    bounds = jnp.cumsum(lengths_row)
    places = jnp.arange(count, dtype=jnp.int32)
    return jnp.sum((places[:, None] >= bounds[None, :-1]).astype(jnp.int32), axis=1)


def contract_rows(left, right):
    return lax.dot_general(
        left, right, (((0,), (0,)), ((), ())), preferred_element_type=jnp.float32
    )


def contract_cols(left, right):
    return lax.dot_general(
        left, right, (((1,), (1,)), ((), ())), preferred_element_type=jnp.float32
    )


def split_parts(values):
    upper = values.astype(jnp.bfloat16)
    lower = (values - upper.astype(jnp.float32)).astype(jnp.bfloat16)
    return (upper, lower)


def gated_unit(gate_pre, upward):
    return jax.nn.silu(gate_pre) * upward


def body(
    tokens,
    attn_gain,
    w_query,
    w_latent,
    w_key_up,
    w_value_up,
    w_out,
    mlp_gain,
    w_gate,
    w_up,
    w_down,
    lengths,
    cotangent,
):
    attn_gain, w_query, w_latent, w_key_up, w_value_up, w_out, mlp_gain, w_gate, w_up, w_down = (
        lax.all_gather(attn_gain, "fsdp", axis=0, tiled=True),
        lax.all_gather(w_query, "fsdp", axis=0, tiled=True),
        lax.all_gather(w_latent, "fsdp", axis=0, tiled=True),
        lax.all_gather(w_key_up, "fsdp", axis=1, tiled=True),
        lax.all_gather(w_value_up, "fsdp", axis=1, tiled=True),
        lax.all_gather(w_out, "fsdp", axis=0, tiled=True),
        lax.all_gather(mlp_gain, "fsdp", axis=0, tiled=True),
        lax.all_gather(w_gate, "fsdp", axis=0, tiled=True),
        lax.all_gather(w_up, "fsdp", axis=0, tiled=True),
        lax.all_gather(w_down, "fsdp", axis=0, tiled=True),
    )
    row_count = tokens.shape[0]
    seq_rank = lax.axis_index("seq")
    stream_len = row_count * lax.axis_size("seq")
    head_width = GQ * HD
    doc_ids = doc_numbers(lengths[0], stream_len)
    row_start = seq_rank * row_count
    own_docs = lax.dynamic_slice_in_dim(doc_ids, row_start, row_count)
    own_places = row_start + jnp.arange(row_count, dtype=jnp.int32)
    block_count = (row_start + row_count - 1) // KEYBLK + 1
    tokens_f = tokens.astype(jnp.float32)
    gain_a = attn_gain.astype(jnp.float32)
    gain_m = mlp_gain.astype(jnp.float32)
    normed = normalize(tokens_f, gain_a).astype(jnp.bfloat16)
    queries = jnp.dot(normed, w_query, preferred_element_type=jnp.float32).astype(jnp.bfloat16)
    latent = jnp.dot(normed, w_latent, preferred_element_type=jnp.float32).astype(jnp.bfloat16)
    gathered = lax.all_gather(latent, "seq", axis=0, tiled=True)
    query_heads = queries.reshape(row_count, HEADS, HD)

    def key_block(source, block_idx, group_idx, with_values):
        latent_part = lax.dynamic_slice(
            source, (block_idx * KEYBLK, group_idx * LAT_HEAD), (KEYBLK, LAT_HEAD)
        )
        low_col = group_idx * head_width
        key_rows = (
            jnp.dot(
                latent_part,
                w_key_up[:, low_col : low_col + head_width],
                preferred_element_type=jnp.float32,
            )
            .astype(jnp.bfloat16)
            .reshape(KEYBLK, GQ, HD)
        )
        value_rows = None
        if with_values:
            value_rows = (
                jnp.dot(
                    latent_part,
                    w_value_up[:, low_col : low_col + head_width],
                    preferred_element_type=jnp.float32,
                )
                .astype(jnp.bfloat16)
                .reshape(KEYBLK, GQ, HD)
            )
        key_docs = lax.dynamic_slice_in_dim(doc_ids, block_idx * KEYBLK, KEYBLK)
        key_places = block_idx * KEYBLK + jnp.arange(KEYBLK, dtype=jnp.int32)
        allowed = (own_docs[:, None] == key_docs[None, :]) & (
            own_places[:, None] >= key_places[None, :]
        )
        return (latent_part, key_rows, value_rows, allowed)

    def block_scores(group_idx, key_rows):
        group_query = query_heads[:, group_idx * GQ : (group_idx + 1) * GQ]
        return (
            jnp.einsum("qhd,khd->hqk", group_query, key_rows, preferred_element_type=jnp.float32)
            * 0.125
        )

    def first_pass(block_idx, carried):
        row_max, row_total = carried
        max_list = []
        total_list = []
        for group_idx in range(GROUPS):
            _, key_rows, _, allowed = key_block(gathered, block_idx, group_idx, False)
            masked = jnp.where(allowed[None], block_scores(group_idx, key_rows), -1e30)
            old_max = row_max[group_idx * GQ : (group_idx + 1) * GQ]
            new_max = jnp.maximum(old_max, jnp.max(masked, axis=-1))
            row_mass = jnp.sum(
                jnp.where(allowed[None], jnp.exp(masked - new_max[:, :, None]), 0.0), axis=-1
            )
            max_list.append(new_max)
            total_list.append(
                row_total[group_idx * GQ : (group_idx + 1) * GQ] * jnp.exp(old_max - new_max)
                + row_mass
            )
        return (jnp.concatenate(max_list, axis=0), jnp.concatenate(total_list, axis=0))

    start_max = jnp.full((HEADS, row_count), -1e30, jnp.float32)
    start_total = jnp.zeros((HEADS, row_count), jnp.float32)
    row_max, row_total = lax.fori_loop(0, block_count, first_pass, (start_max, start_total))
    logsum = row_max + jnp.log(row_total)

    def block_probs(group_idx, key_rows, allowed):
        group_logsum = logsum[group_idx * GQ : (group_idx + 1) * GQ]
        return jnp.where(
            allowed[None],
            jnp.exp(block_scores(group_idx, key_rows) - group_logsum[:, :, None]),
            0.0,
        )

    def second_pass(block_idx, carried):
        rounded_sum, exact_sum = carried
        rounded_list = []
        exact_list = []
        for group_idx in range(GROUPS):
            _, key_rows, value_rows, allowed = key_block(gathered, block_idx, group_idx, True)
            attn_probs = block_probs(group_idx, key_rows, allowed)
            probs_upper, probs_lower = split_parts(attn_probs)
            rounded_part = jnp.einsum(
                "hqk,khd->qhd", probs_upper, value_rows, preferred_element_type=jnp.float32
            )
            rounded_list.append(rounded_part)
            exact_list.append(
                rounded_part
                + jnp.einsum(
                    "hqk,khd->qhd", probs_lower, value_rows, preferred_element_type=jnp.float32
                )
            )
        return (
            rounded_sum + jnp.concatenate(rounded_list, axis=1),
            exact_sum + jnp.concatenate(exact_list, axis=1),
        )

    head_zeros = jnp.zeros((row_count, HEADS, HD), jnp.float32)
    rounded_sum, exact_sum = lax.fori_loop(0, block_count, second_pass, (head_zeros, head_zeros))
    mixed = rounded_sum.reshape(row_count, QW).astype(jnp.bfloat16)
    resid = tokens_f + jnp.dot(mixed, w_out, preferred_element_type=jnp.float32)
    normed_m = normalize(resid, gain_m).astype(jnp.bfloat16)
    gate_pre = jnp.dot(normed_m, w_gate, preferred_element_type=jnp.float32)
    upward = jnp.dot(normed_m, w_up, preferred_element_type=jnp.float32)
    hidden = gated_unit(gate_pre, upward).astype(jnp.bfloat16)
    output = (resid + jnp.dot(hidden, w_down, preferred_element_type=jnp.float32)).astype(
        jnp.bfloat16
    )
    dhidden = contract_cols(cotangent, w_down).astype(jnp.bfloat16)
    _, pull_unit = jax.vjp(gated_unit, gate_pre, upward)
    dgate, dupward = pull_unit(dhidden.astype(jnp.float32))
    dgate = dgate.astype(jnp.bfloat16)
    dupward = dupward.astype(jnp.bfloat16)
    dnormed_m = contract_cols(dgate, w_gate) + contract_cols(dupward, w_up)
    _, pull_norm_m = jax.vjp(normalize, resid, gain_m)
    dresid_norm, grad_mlp_gain = pull_norm_m(dnormed_m)
    dresid = cotangent.astype(jnp.float32) + dresid_norm
    dattn = dresid.astype(jnp.bfloat16)
    dmixed = contract_cols(dattn, w_out).astype(jnp.bfloat16)
    grad_heads = dmixed.reshape(row_count, HEADS, HD)
    row_delta = jnp.einsum("qhd,qhd->hq", grad_heads.astype(jnp.float32), exact_sum)
    source = gathered

    def backward_pass(block_idx, carried):
        dqueries, dlatent, grad_ku, grad_vu = carried
        query_list = []
        fresh_latent = []
        for group_idx in range(GROUPS):
            latent_part, key_rows, value_rows, allowed = key_block(
                source, block_idx, group_idx, True
            )
            low_col = group_idx * head_width
            group_query = query_heads[:, group_idx * GQ : (group_idx + 1) * GQ]
            group_grad = grad_heads[:, group_idx * GQ : (group_idx + 1) * GQ]
            attn_probs = block_probs(group_idx, key_rows, allowed)
            prob_grad = jnp.einsum(
                "qhd,khd->hqk", group_grad, value_rows, preferred_element_type=jnp.float32
            )
            group_delta = row_delta[group_idx * GQ : (group_idx + 1) * GQ]
            score_grad = (attn_probs * (prob_grad - group_delta[:, :, None])).astype(jnp.bfloat16)
            query_list.append(
                jnp.einsum("hqk,khd->qhd", score_grad, key_rows, preferred_element_type=jnp.float32)
                * 0.125
            )
            key_grad = (
                jnp.einsum(
                    "hqk,qhd->khd", score_grad, group_query, preferred_element_type=jnp.float32
                )
                * 0.125
            ).reshape(KEYBLK, head_width)
            value_grad = jnp.einsum(
                "hqk,qhd->khd",
                attn_probs.astype(jnp.bfloat16),
                group_grad,
                preferred_element_type=jnp.float32,
            ).reshape(KEYBLK, head_width)
            key_upper, key_lower = split_parts(key_grad)
            value_upper, value_lower = split_parts(value_grad)
            key_weight = w_key_up[:, low_col : low_col + head_width]
            value_weight = w_value_up[:, low_col : low_col + head_width]
            latent_grad = (
                contract_cols(key_upper, key_weight)
                + contract_cols(key_lower, key_weight)
                + contract_cols(value_upper, value_weight)
                + contract_cols(value_lower, value_weight)
            )
            fresh_latent.append(
                lax.dynamic_update_slice_in_dim(
                    dlatent[group_idx], latent_grad, block_idx * KEYBLK, 0
                )
            )
            grad_ku = grad_ku.at[:, low_col : low_col + head_width].add(
                contract_rows(latent_part, key_upper) + contract_rows(latent_part, key_lower)
            )
            grad_vu = grad_vu.at[:, low_col : low_col + head_width].add(
                contract_rows(latent_part, value_upper) + contract_rows(latent_part, value_lower)
            )
        return (
            dqueries + jnp.concatenate(query_list, axis=1),
            tuple(fresh_latent),
            grad_ku,
            grad_vu,
        )

    latent_zeros = tuple(
        (jnp.zeros((stream_len, LAT_HEAD), jnp.float32) for group_idx in range(GROUPS))
    )
    weight_zeros = jnp.zeros((LAT_HEAD, QW), jnp.float32)
    dqueries, dlatent, grad_key_up, grad_value_up = lax.fori_loop(
        0, block_count, backward_pass, (head_zeros, latent_zeros, weight_zeros, weight_zeros)
    )
    dqueries = dqueries.reshape(row_count, QW).astype(jnp.bfloat16)
    shares = (
        lax.psum_scatter(dlatent[0], "seq", scatter_dimension=0, tiled=True),
        lax.psum_scatter(dlatent[1], "seq", scatter_dimension=0, tiled=True),
    )
    dlatent_own = jnp.concatenate(shares, axis=1).astype(jnp.bfloat16)
    dnormed = contract_cols(dqueries, w_query) + contract_cols(dlatent_own, w_latent)
    _, pull_norm_a = jax.vjp(normalize, tokens_f, gain_a)
    dtokens_norm, grad_attn_gain = pull_norm_a(dnormed)
    tokens_grad = (dresid + dtokens_norm).astype(jnp.bfloat16)
    normed_all, normed_m_all, cotangent_all, dattn_all = (
        lax.all_gather(normed, "seq", axis=0, tiled=True),
        lax.all_gather(normed_m, "seq", axis=0, tiled=True),
        lax.all_gather(cotangent, "seq", axis=0, tiled=True),
        lax.all_gather(dattn, "seq", axis=0, tiled=True),
    )
    hidden_cols, dgate_cols, dupward_cols, mixed_cols, dquery_cols, dlatent_cols = (
        lax.all_to_all(hidden, "seq", split_axis=1, concat_axis=0, tiled=True),
        lax.all_to_all(dgate, "seq", split_axis=1, concat_axis=0, tiled=True),
        lax.all_to_all(dupward, "seq", split_axis=1, concat_axis=0, tiled=True),
        lax.all_to_all(mixed, "seq", split_axis=1, concat_axis=0, tiled=True),
        lax.all_to_all(dqueries, "seq", split_axis=1, concat_axis=0, tiled=True),
        lax.all_to_all(dlatent_own, "seq", split_axis=1, concat_axis=0, tiled=True),
    )
    part_query = contract_rows(normed_all, dquery_cols)
    part_latent = contract_rows(normed_all, dlatent_cols)
    part_out = contract_rows(mixed_cols, dattn_all)
    part_gate = contract_rows(normed_m_all, dgate_cols)
    part_up = contract_rows(normed_m_all, dupward_cols)
    part_down = contract_rows(hidden_cols, cotangent_all)
    grad_query, grad_latent, grad_out, grad_gate, grad_up, grad_down = (
        lax.psum_scatter(
            part_query.astype(jnp.bfloat16), "fsdp", scatter_dimension=0, tiled=True
        ).astype(jnp.float32),
        lax.psum_scatter(
            part_latent.astype(jnp.bfloat16), "fsdp", scatter_dimension=0, tiled=True
        ).astype(jnp.float32),
        lax.psum_scatter(
            part_out.astype(jnp.bfloat16), "fsdp", scatter_dimension=1, tiled=True
        ).astype(jnp.float32),
        lax.psum_scatter(
            part_gate.astype(jnp.bfloat16), "fsdp", scatter_dimension=0, tiled=True
        ).astype(jnp.float32),
        lax.psum_scatter(
            part_up.astype(jnp.bfloat16), "fsdp", scatter_dimension=0, tiled=True
        ).astype(jnp.float32),
        lax.psum_scatter(
            part_down.astype(jnp.bfloat16), "fsdp", scatter_dimension=1, tiled=True
        ).astype(jnp.float32),
    )
    small_sent = (
        lax.psum_scatter(grad_attn_gain, ("fsdp", "seq"), scatter_dimension=0, tiled=True),
        lax.psum_scatter(grad_key_up, ("fsdp", "seq"), scatter_dimension=1, tiled=True),
        lax.psum_scatter(grad_value_up, ("fsdp", "seq"), scatter_dimension=1, tiled=True),
        lax.psum_scatter(grad_mlp_gain, ("fsdp", "seq"), scatter_dimension=0, tiled=True),
    )
    return (
        output,
        tokens_grad,
        small_sent[0],
        grad_query,
        grad_latent,
        small_sent[1],
        small_sent[2],
        grad_out,
        small_sent[3],
        grad_gate,
        grad_up,
        grad_down,
    )


def solution(mesh):
    in_specs = (
        P(("fsdp", "seq"), None),
        P("fsdp"),
        P("fsdp", None),
        P("fsdp", None),
        P(None, "fsdp"),
        P(None, "fsdp"),
        P("fsdp", None),
        P("fsdp"),
        P("fsdp", None),
        P("fsdp", None),
        P("fsdp", None),
        P("fsdp", None),
        P(("fsdp", "seq"), None),
    )
    out_specs = (
        P(("fsdp", "seq"), None),
        P(("fsdp", "seq"), None),
        P(("fsdp", "seq")),
        P("fsdp", "seq"),
        P("fsdp", "seq"),
        P(None, ("fsdp", "seq")),
        P(None, ("fsdp", "seq")),
        P("seq", "fsdp"),
        P(("fsdp", "seq")),
        P("fsdp", "seq"),
        P("fsdp", "seq"),
        P("seq", "fsdp"),
    )
    return jax.shard_map(body, mesh=mesh, in_specs=in_specs, out_specs=out_specs, check_vma=False)
```

profile of v0, /device:TPU:0, one launch (start us, length us, event | category | flops | bytes accessed | tf_op | source)
XLA Modules:
  0.0 1104.4 jit_solution(1975361463680358151)
XLA Ops:
  17.6 11.4 %all-gather.14.cloned.1.call-done = bf16[1024,512]{1,0:T(8,128)(2,1)} async-done(((bf16[256,512]{1,0:T(8,128)(2,1)}), bf16[1024,512]{1,0:T(8,128)(2,1)}) %all-gather.14.cloned.1.call-update) | async-done | bytes 1048592 | tf_op jit(solution)/shard_map/all_gather | solution.py:68
  34.4 7.6 all_gather.48
  42.4 10.5 all_gather.49
  60.2 39.0 %all-gather.16.cloned.1.call-done = bf16[1024,512]{1,0:T(8,128)(2,1)} async-done(((bf16[128,512]{1,0:T(8,128)(2,1)}), bf16[1024,512]{1,0:T(8,128)(2,1)}) %all-gather.16.cloned.1.call-update) | async-done | bytes 1048592 | tf_op jit(solution)/shard_map/all_gather | solution.py:92
  107.5 34.6 %while.54 = (s32[]{:T(128)}, f32[128,16,64]{0,2,1:T(8,128)}, f32[128,16,64]{0,2,1:T(8,128)}, s32[]{:T(128)}, bf16[1024,512]{1,0:T(8,128)(2,1)}, /*index=5*/bf16[...) while((s32[]{:T(128)}, f32[128,16,64]{0,2,1:T(8,128)}, ...), condition=%wide.region_10.11_spmd.clone, body=%wide.region_9.10_spmd.clone.sunk | while | flops 1905263744 | bytes 73840464 | solution.py:190
  145.6 21.3 %all-gather.22.cloned.1.call-done = bf16[1024,2816]{1,0:T(8,128)(2,1)} async-done(((bf16[256,2816]{1,0:T(8,128)(2,1)}), bf16[1024,2816]{1,0:T(8,128)(2,1)}) %all-gather.22.cloned.1.call-update) | async-done | bytes 5767184 | tf_op jit(solution)/shard_map/all_gather | solution.py:73
  171.5 40.2 %all-gather.24.cloned.1.call-done = bf16[1024,2816]{1,0:T(8,128)(2,1)} async-done(((bf16[256,2816]{1,0:T(8,128)(2,1)}), bf16[1024,2816]{1,0:T(8,128)(2,1)}) %all-gather.24.cloned.1.call-update) | async-done | bytes 5767184 | tf_op jit(solution)/shard_map/all_gather | solution.py:74
  216.4 40.3 %all-gather.26.cloned.1.call-done = bf16[2816,1024]{1,0:T(8,128)(2,1)} async-done(((bf16[704,1024]{1,0:T(8,128)(2,1)}), bf16[2816,1024]{1,0:T(8,128)(2,1)}) %all-gather.26.cloned.1.call-update) | async-done | bytes 5767184 | tf_op jit(solution)/shard_map/all_gather | solution.py:75
  256.7 6.6 multiply_convert_fusion
  281.5 37.0 %while.55 = (s32[]{:T(128)}, f32[128,16,64]{0,2,1:T(8,128)}, f32[1024,256]{1,0:T(8,128)}, f32[1024,256]{1,0:T(8,128)}, f32[256,1024]{0,1:T(8,128)}, /*index=5*/f...) while((s32[]{:T(128)}, f32[128,16,64]{0,2,1:T(8,128)}, ...), condition=%wide.region_16.17_spmd.clone, body=%wide.region_14.16_spmd.clone.sunk | while | flops 6747325440 | bytes 164304816 | solution.py:280
  332.7 53.6 %reduce-scatter.13.cloned.1.call-done = f32[128,256]{0,1:T(8,128)} async-done(((f32[1024,256]{0,1:T(8,128)}), f32[128,256]{0,1:T(8,128)}) %reduce-scatter.13.cloned.1.call-update) | async-done | bytes 131088 | tf_op jit(solution)/shard_map/reduce_scatter | solution.py:286
  387.3 65.9 %reduce-scatter.11.cloned.1.call-done = f32[128,256]{0,1:T(8,128)} async-done(((f32[1024,256]{0,1:T(8,128)}), f32[128,256]{0,1:T(8,128)}) %reduce-scatter.11.cloned.1.call-update) | async-done | bytes 131088 | tf_op jit(solution)/shard_map/reduce_scatter | solution.py:285
  470.4 40.0 %all-gather.28.cloned.1.call-done = bf16[1024,1024]{1,0:T(8,128)(2,1)} async-done(((bf16[128,1024]{1,0:T(8,128)(2,1)}), bf16[1024,1024]{1,0:T(8,128)(2,1)}) %all-gather.28.cloned.1.call-update) | async-done | bytes 2097168 | tf_op jit(solution)/shard_map/all_gather | solution.py:294
  519.8 50.7 %all-gather.32.cloned.1.call-done = bf16[1024,1024]{1,0:T(8,128)(2,1)} async-done(((bf16[128,1024]{1,0:T(8,128)(2,1)}), bf16[1024,1024]{1,0:T(8,128)(2,1)}) %all-gather.32.cloned.1.call-update) | async-done | bytes 2097168 | tf_op jit(solution)/shard_map/all_gather | solution.py:295
  582.5 47.1 %all-gather.34.cloned.1.call-done = bf16[1024,1024]{1,0:T(8,128)(2,1)} async-done(((bf16[128,1024]{1,0:T(8,128)(2,1)}), bf16[1024,1024]{1,0:T(8,128)(2,1)}) %all-gather.34.cloned.1.call-update) | async-done | bytes 2097168 | tf_op jit(solution)/shard_map/all_gather | solution.py:296
  633.0 15.6 %all_to_all.105 = bf16[128,8,128]{0,2,1:T(8,128)(2,1)} all-to-all(bf16[128,8,128]{0,2,1:T(8,128)(2,1)S(1)} %bitcast.439), channel_id=1, replica_groups=mesh['fsdp'=4,'seq'=8] {'seq'}, dimensions={1} | all-to-all | bytes 524288 | tf_op jit(solution)/shard_map/all_to_all | solution.py:303
  650.4 31.5 %all-gather.30.cloned.1.call-done = bf16[1024,1024]{1,0:T(8,128)(2,1)} async-done(((bf16[128,1024]{1,0:T(8,128)(2,1)}), bf16[1024,1024]{1,0:T(8,128)(2,1)}) %all-gather.30.cloned.1.call-update) | async-done | bytes 2097168 | tf_op jit(solution)/shard_map/all_gather | solution.py:297
  693.4 10.0 reduce-scatter.15.cloned.1.call-done
  706.6 39.5 %all-reduce.2 = (f32[1024]{0:T(1024)S(1)}, f32[1024]{0:T(1024)S(1)}) all-reduce(f32[1024]{0:T(1024)S(1)} %get-tuple-element.644, f32[1024]{0:T(1024)S(1)} %copy-done.44), channel_id=4, replica_groups=mesh['fsdp'=4,'seq'=8] {'fsdp','seq'}, use_global_device_ids=true, to_apply=%region_21.22.clone | all-reduce | flops 2048 | bytes 16384
  753.0 23.8 %reduce-scatter.27.cloned.1.call-done = bf16[256,352]{0,1:T(8,128)(2,1)} async-done(((bf16[1024,352]{0,1:T(8,128)(2,1)}), bf16[256,352]{0,1:T(8,128)(2,1)}) %reduce-scatter.27.cloned.1.call-update) | async-done | bytes 180240 | tf_op jit(solution)/shard_map/reduce_scatter | solution.py:326
  778.5 23.6 %reduce-scatter.29.cloned.1.call-done = bf16[352,256]{1,0:T(8,128)(2,1)} async-done(((bf16[352,1024]{1,0:T(8,128)(2,1)}), bf16[352,256]{1,0:T(8,128)(2,1)}) %reduce-scatter.29.cloned.1.call-update) | async-done | bytes 180240 | tf_op jit(solution)/shard_map/reduce_scatter | solution.py:329
  803.7 21.0 %reduce-scatter.23.cloned.1.call-done = bf16[128,256]{1,0:T(8,128)(2,1)} async-done(((bf16[128,1024]{1,0:T(8,128)(2,1)}), bf16[128,256]{1,0:T(8,128)(2,1)}) %reduce-scatter.23.cloned.1.call-update) | async-done | bytes 65552 | tf_op jit(solution)/shard_map/reduce_scatter | solution.py:320
  826.2 136.6 %reduce-scatter.19.cloned.1.call-done = f32[256,32]{0,1:T(8,128)} async-done(((f32[256,1024]{0,1:T(8,128)}), f32[256,32]{0,1:T(8,128)}) %reduce-scatter.19.cloned.1.call-update) | async-done | bytes 32784 | tf_op jit(solution)/shard_map/reduce_scatter | solution.py:335
  962.8 134.4 %reduce-scatter.21.cloned.1.call-done = f32[256,32]{0,1:T(8,128)} async-done(((f32[256,1024]{0,1:T(8,128)}), f32[256,32]{0,1:T(8,128)}) %reduce-scatter.21.cloned.1.call-update) | async-done | bytes 32784 | tf_op jit(solution)/shard_map/reduce_scatter | solution.py:336
  (304 shorter events, 207.7 us)
Async XLA Ops:
  7.9 50.0 %all-gather.18.cloned.1.call-start = ((), (), s32[]{:S(2)}) async-start(), calls=%async_computation.18 | async-start | bytes 2621440 | tf_op jit(solution)/shard_map/all_gather | solution.py:67
  8.7 90.5 %all-gather.16.cloned.1.call-start = ((), (), s32[]{:S(2)}) async-start(), calls=%async_computation.17 | async-start | bytes 1179648 | tf_op jit(solution)/shard_map/all_gather | solution.py:92
  31.3 111.9 %all-gather.20.cloned.1.call-start = ((), (), s32[]{:S(2)}) async-start(), calls=%async_computation.19 | async-start | bytes 2621440 | tf_op jit(solution)/shard_map/all_gather | solution.py:71
  31.8 135.0 %all-gather.22.cloned.1.call-start = ((), (), s32[]{:S(2)}) async-start(), calls=%async_computation.20 | async-start | bytes 7208960 | tf_op jit(solution)/shard_map/all_gather | solution.py:73
  32.4 179.3 %all-gather.24.cloned.1.call-start = ((), (), s32[]{:S(2)}) async-start(), calls=%async_computation.21 | async-start | bytes 7208960 | tf_op jit(solution)/shard_map/all_gather | solution.py:74
  33.0 223.7 %all-gather.26.cloned.1.call-start = ((), (), s32[]{:S(2)}) async-start(), calls=%async_computation.22 | async-start | bytes 7208960 | tf_op jit(solution)/shard_map/all_gather | solution.py:75
  33.7 352.6 %reduce-scatter.13.cloned.1.call-start = ((), (), s32[]{:S(2)}) async-start(), calls=%async_computation.24 | async-start | bytes 1179648 | tf_op jit(solution)/shard_map/reduce_scatter | solution.py:286
  321.1 132.1 %reduce-scatter.11.cloned.1.call-start = ((), (), s32[]{:S(2)}) async-start(), calls=%async_computation.23 | async-start | bytes 1179648 | tf_op jit(solution)/shard_map/reduce_scatter | solution.py:285
  323.8 186.5 %all-gather.28.cloned.1.call-start = ((), (), s32[]{:S(2)}) async-start(), calls=%async_computation.25 | async-start | bytes 2359296 | tf_op jit(solution)/shard_map/all_gather | solution.py:294
  324.4 246.1 %all-gather.32.cloned.1.call-start = ((), (), s32[]{:S(2)}) async-start(), calls=%async_computation.32 | async-start | bytes 2359296 | tf_op jit(solution)/shard_map/all_gather | solution.py:295
  325.1 304.4 %all-gather.34.cloned.1.call-start = ((), (), s32[]{:S(2)}) async-start(), calls=%async_computation.35 | async-start | bytes 2359296 | tf_op jit(solution)/shard_map/all_gather | solution.py:296
  325.7 356.3 %all-gather.30.cloned.1.call-start = ((), (), s32[]{:S(2)}) async-start(), calls=%async_computation.30 | async-start | bytes 2359296 | tf_op jit(solution)/shard_map/all_gather | solution.py:297
  327.2 127.6 %all-to-all-start = ((bf16[128,8,128]{0,2,1:T(8,128)(2,1)}), bf16[128,8,128]{0,2,1:T(8,128)(2,1)S(1)}, u32[]{:S(2)}, u32[]{:S(2)}) async-start(bf16[128,8,128]{0,2,1:T(8,128)(2,1)} %bitcast.12), calls=%async_computation.2 | async-start | bytes 524288 | tf_op jit(solution)/shard_map/all_to_all | solution.py:304
  466.0 50.1 %all-to-all-start.3 = ((bf16[128,8,352]{0,2,1:T(8,128)(2,1)}), bf16[128,8,352]{0,2,1:T(8,128)(2,1)}, u32[]{:S(2)}, u32[]{:S(2)}) async-start(bf16[128,8,352]{0,2,1:T(8,128)(2,1)} %bitcast.21), calls=%async_computation.10 | async-start | bytes 1441792 | tf_op jit(solution)/shard_map/all_to_all | solution.py:301
  470.2 233.2 %reduce-scatter.15.cloned.1.call-start = ((), (), s32[]{:S(2)}) async-start(), calls=%async_computation.26 | async-start | bytes 327680 | tf_op jit(solution)/shard_map/reduce_scatter | solution.py:314
  513.6 234.7 %reduce-scatter.17.cloned.1.call-start = ((), (), s32[]{:S(2)}) async-start(), calls=%async_computation.27 | async-start | bytes 163840 | tf_op jit(solution)/shard_map/reduce_scatter | solution.py:317
  516.0 59.3 %all-to-all-start.4 = ((bf16[128,8,352]{0,2,1:T(8,128)(2,1)}), bf16[128,8,352]{0,2,1:T(8,128)(2,1)S(1)}, u32[]{:S(2)}, u32[]{:S(2)}) async-start(bf16[128,8,352]{0,2,1:T(8,128)(2,1)} %bitcast.437), calls=%async_computation.12 | async-start | bytes 1441792 | tf_op jit(solution)/shard_map/all_to_all | solution.py:302
  519.7 231.6 %reduce-scatter.25.cloned.1.call-start = ((), (), s32[]{:S(2)}) async-start(), calls=%async_computation.33 | async-start | bytes 901120 | tf_op jit(solution)/shard_map/reduce_scatter | solution.py:323
  575.4 54.2 %all-to-all-start.5 = ((bf16[128,8,352]{0,2,1:T(8,128)(2,1)}), bf16[128,8,352]{0,2,1:T(8,128)(2,1)S(1)}, u32[]{:S(2)}, u32[]{:S(2)}) async-start(bf16[128,8,352]{0,2,1:T(8,128)(2,1)} %bitcast.25), calls=%async_computation.14 | async-start | bytes 1441792 | tf_op jit(solution)/shard_map/all_to_all | solution.py:300
  578.9 197.9 %reduce-scatter.27.cloned.1.call-start = ((), (), s32[]{:S(2)}) async-start(), calls=%async_computation.34 | async-start | bytes 901120 | tf_op jit(solution)/shard_map/reduce_scatter | solution.py:326
  582.4 219.6 %reduce-scatter.29.cloned.1.call-start = ((), (), s32[]{:S(2)}) async-start(), calls=%async_computation.36 | async-start | bytes 901120 | tf_op jit(solution)/shard_map/reduce_scatter | solution.py:329
  632.9 191.8 %reduce-scatter.23.cloned.1.call-start = ((), (), s32[]{:S(2)}) async-start(), calls=%async_computation.31 | async-start | bytes 327680 | tf_op jit(solution)/shard_map/reduce_scatter | solution.py:320
  684.9 277.9 %reduce-scatter.19.cloned.1.call-start = ((), (), s32[]{:S(2)}) async-start(), calls=%async_computation.28 | async-start | bytes 1081344 | tf_op jit(solution)/shard_map/reduce_scatter | solution.py:335
  685.5 411.8 %reduce-scatter.21.cloned.1.call-start = ((), (), s32[]{:S(2)}) async-start(), calls=%async_computation.29 | async-start | bytes 1081344 | tf_op jit(solution)/shard_map/reduce_scatter | solution.py:336
  (57 other events, 1824.5 us)
Sparse Core Ops, SparseCore 0:
  9.6 19.4 all-gather.13
  30.6 25.6 all-gather.17
  59.0 40.1 all-gather.15
  100.6 21.3 all-gather.19
  123.4 43.3 all-gather.21
  168.3 43.3 all-gather.23
  213.3 43.3 all-gather.25
  321.2 65.0 reduce-scatter.12
  390.2 62.9 reduce-scatter.10
  455.7 54.5 all-gather.27
  512.5 57.9 all-gather.31
  572.5 57.0 all-gather.33
  632.2 49.6 all-gather.29
  684.9 18.4 reduce-scatter.14
  706.4 19.5 reduce-scatter.16
  728.4 22.8 reduce-scatter.24
  753.8 22.9 reduce-scatter.26
  779.2 22.8 reduce-scatter.28
  804.7 20.0 reduce-scatter.22
  827.4 135.3 reduce-scatter.18
  965.7 131.4 reduce-scatter.20
where the time goes:
time: 1110 us; the launch traced here: 1100 us
  waiting for transfers between devices  806 us (73%)
  matrix products  111 us (10%)
  blocking collectives  84.1 us (8%)
  local copies, waits for them, and re-layouts  25.5 us (2%)
  other arithmetic  23.5 us (2%)
  starting transfers between devices  21.5 us (2%)
  loops' own time  17.8 us (2%)
  between operations  15.3 us (1%)
    reduce_scatter x1, waiting for transfers between devices, body(): lax.psum_scatter(grad_key_up, ('fsdp', 'seq'), scatter_dimension=1, tiled...  137 us
    reduce_scatter x1, waiting for transfers between devices, body(): lax.psum_scatter(grad_value_up, ('fsdp', 'seq'), scatter_dimension=1, til...  134 us
    reduce_scatter x1, waiting for transfers between devices, body(): lax.psum_scatter(dlatent[0], 'seq', scatter_dimension=0, tiled=True)  65.9 us
    reduce_scatter x1, waiting for transfers between devices, body(): lax.psum_scatter(dlatent[1], 'seq', scatter_dimension=0, tiled=True)  53.6 us
    all_gather x1, waiting for transfers between devices, body(): lax.all_gather(normed_m, 'seq', axis=0, tiled=True)  50.7 us
    all_gather x1, waiting for transfers between devices, body(): lax.all_gather(cotangent, 'seq', axis=0, tiled=True)  47.1 us
    all_gather x1, waiting for transfers between devices, body(): lax.all_gather(w_down, 'fsdp', axis=0, tiled=True)  40.3 us
    all_gather x1, waiting for transfers between devices, body(): lax.all_gather(w_up, 'fsdp', axis=0, tiled=True)  40.2 us
  transfers between devices with their start and end apart: 26, of which 19 were waited for; matrix products, arithmetic and copies ran while one was open for 8% of the time, Pallas kernels for 0%

commit v1 on v0

--- a/solution.py
+++ b/solution.py
@@ -1,6 +1,11 @@
+import functools
+
 import jax
 import jax.numpy as jnp
 from jax import lax
+from jax.experimental import pallas as pl
+from jax.experimental.pallas import tpu as pltpu
+from jax.sharding import Mesh
 from jax.sharding import PartitionSpec as P
 
 HEADS = 16
@@ -352,7 +357,734 @@
     )
 
 
+BF = jnp.bfloat16
+F32 = jnp.float32
+NEG = -1e30
+SCALE = 0.125
+RING = (0, 2, 4, 6, 7, 5, 3, 1)
+MIB = 2**20
+
+FS, ZS, Y0, Y1, ZH0, ZH1, ZL, ROW0 = 8, 12, 16, 17, 18, 19, 20, 21
+
+
+def dot_nn(left, right):
+    return lax.dot_general(left, right, (((1,), (0,)), ((), ())), preferred_element_type=F32)
+
+
+def fold(total):
+    return lax.rsqrt(jnp.mean(total * total, axis=-1, keepdims=True) + epsilon)
+
+
+def at(index, size):
+    return pl.ds(pl.multiple_of(index * size, size), size)
+
+
+class Lazy:
+    def __init__(self, ref, copy):
+        self.ref, self.copy, self.shape = ref, copy, ref.shape
+
+    def __getitem__(self, index):
+        if self.copy is not None:
+            self.copy.wait()
+            self.copy = None
+        return self.ref[index]
+
+
+class Late:
+    def __init__(self, ref, out, sem):
+        self.ref, self.out, self.sem, self.shape, self.copy = ref, out, sem, ref.shape, None
+
+    def __getitem__(self, index):
+        return self.ref[index]
+
+    def __setitem__(self, index, value):
+        self.ref[index] = value
+
+    def flush(self):
+        self.copy = pltpu.make_async_copy(self.ref, self.out, self.sem)
+        self.copy.start()
+
+
+def call(kernel, n_smem, outs, scratch=(), limit=16, flops=1, far_in=(), far_out=()):
+    far_in, far_out = tuple(far_in), tuple(far_out)
+    n_out, n_far = len(outs), len(far_in) + len(far_out)
+
+    def run(*args, deps=()):
+        n_in = len(args) - n_smem
+
+        def body(*refs):
+            smem, ins, results = refs[:n_smem], list(refs[n_smem : n_smem + n_in]), list(refs[n_smem + n_in + len(deps) : n_smem + n_in + len(deps) + n_out])
+            rest = refs[n_smem + n_in + len(deps) + n_out :]
+            sems = rest[-1]
+            far, own = rest[len(scratch) : len(scratch) + n_far], rest[: len(scratch)]
+            for k, i in enumerate(far_in):
+                copy = pltpu.make_async_copy(ins[i], far[k], sems.at[k])
+                copy.start()
+                ins[i] = Lazy(far[k], copy)
+            late = []
+            for k, i in enumerate(far_out):
+                results[i] = Late(far[len(far_in) + k], results[i], sems.at[len(far_in) + k])
+                late.append(results[i])
+            kernel(*smem, *ins, *results, *own)
+            for i in far_in:
+                if ins[i].copy is not None:
+                    ins[i].copy.wait()
+            for v in late:
+                if v.copy is None:
+                    v.flush()
+            for v in late:
+                v.copy.wait()
+
+        spec = lambda i, far: pl.BlockSpec(memory_space=pl.ANY if i in far else pltpu.VMEM)
+        shapes = [pltpu.VMEM(shape, dtype) for shape, dtype in scratch]
+        shapes += [pltpu.VMEM(args[n_smem + i].shape, args[n_smem + i].dtype) for i in far_in]
+        shapes += [pltpu.VMEM(*outs[i]) for i in far_out]
+        return pl.pallas_call(
+            body,
+            in_specs=[pl.BlockSpec(memory_space=pltpu.SMEM)] * n_smem + [spec(i, far_in) for i in range(n_in)] + [pl.BlockSpec(memory_space=pl.ANY)] * len(deps),
+            out_specs=[spec(i, far_out) for i in range(n_out)],
+            out_shape=[jax.ShapeDtypeStruct(shape, dtype) for shape, dtype in outs],
+            scratch_shapes=shapes + [pltpu.SemaphoreType.DMA((max(1, n_far),))],
+            compiler_params=pltpu.CompilerParams(vmem_limit_bytes=limit * MIB),
+            cost_estimate=pl.CostEstimate(flops=flops, bytes_accessed=0, transcendentals=0),
+        )(*args, *deps)
+
+    return run
+
+
+def attend_kernel(idx, lens, *refs):
+    tok, wl, wb = refs[0:8], refs[8:12], refs[12:18]
+    mixed_ref, probs_ref, out_ref, qs_ref, q_ref, na_ref, lat_ref, wq_ref, wk_ref, wv_ref, wlt_ref, bias_ref = refs[18:30]
+    rows, d = tok[0].shape
+    keys = 8 * rows
+    part = wl[0].shape[0]
+    width = GQ * rows
+    for k in range(4):
+        here = at(idx[FS + k], part)
+        wlt_ref[:, here] = wl[k][...].T
+        if k < 2:
+            wq_ref[here, :] = wb[k][:, 0:QW]
+            wk_ref[:, here] = wb[k][:, QW : QW + LAT_HEAD]
+            wv_ref[:, here] = wb[k][:, QW + LAT_HEAD : QW + 2 * LAT_HEAD]
+        else:
+            first, second = wb[2 * k - 2], wb[2 * k - 1]
+            cut = first.shape[1]
+            wq_ref[here, 0:cut] = first[...]
+            wq_ref[here, cut:QW] = second[:, 0 : QW - cut]
+            wk_ref[:, here] = second[:, QW - cut : QW - cut + LAT_HEAD]
+            wv_ref[:, here] = second[:, QW - cut + LAT_HEAD : QW - cut + 2 * LAT_HEAD]
+    for i in range(8):
+        values = tok[i][...].astype(F32)
+        normed = (values * fold(values)).astype(BF)
+        na_ref[at(idx[i], rows), :] = normed
+        if i == 0:
+            q_ref[...] = dot_nn(normed, wq_ref[...]).astype(BF)
+    lat_ref[...] = contract_cols(na_ref[...], wlt_ref[...]).astype(BF)
+    for ref in (wq_ref, wk_ref, wv_ref, wlt_ref, q_ref, na_ref, lat_ref):
+        ref.flush()
+    place = lax.broadcasted_iota(jnp.int32, (rows, keys), 1)
+    own = idx[ROW0] + lax.broadcasted_iota(jnp.int32, (rows, keys), 0)
+    first = jnp.zeros((rows, keys), jnp.int32)
+    edge = 0
+    for i in range(lens.shape[1] - 1):
+        edge = edge + lens[0, i]
+        first = jnp.where(own >= edge, edge, first)
+    bias = jnp.where((place >= first) & (place <= own), 0.0, NEG)
+    bias_ref[0:rows, :] = bias
+    bias_ref[rows : 2 * rows, :] = bias
+    low = lax.broadcasted_iota(jnp.int32, (rows, 2 * HD), 1) < HD
+    for p in range(HEADS // 2):
+        cols = slice(p * 2 * HD, (p + 1) * 2 * HD)
+        q = q_ref[:, cols]
+        none = jnp.zeros_like(q)
+        for j, own_q in enumerate((jnp.where(low, q, none), jnp.where(low, none, q))):
+            qs_ref[(2 * p + j) * rows : (2 * p + j + 1) * rows, :] = (contract_cols(own_q, wk_ref[:, cols]) * SCALE).astype(BF)
+    for g in range(GROUPS):
+        lat = lat_ref[:, g * LAT_HEAD : (g + 1) * LAT_HEAD]
+        for r in range(0, width, 2 * rows):
+            band = slice(g * width + r, g * width + r + 2 * rows)
+            scores = contract_cols(qs_ref[band, :], lat) + bias_ref[...]
+            mass = jnp.exp(scores - jnp.max(scores, axis=-1, keepdims=True))
+            probs_ref[band, :] = (mass * (1.0 / jnp.sum(mass, axis=-1, keepdims=True))).astype(BF)
+        band = slice(g * width, (g + 1) * width)
+        out_ref[band, :] = dot_nn(probs_ref[band, :], lat).astype(BF)
+    for ref in (probs_ref, qs_ref, out_ref):
+        ref.flush()
+    for p in range(HEADS // 2):
+        cols = slice(p * 2 * HD, (p + 1) * 2 * HD)
+        a, b = (dot_nn(out_ref[(2 * p + j) * rows : (2 * p + j + 1) * rows, :], wv_ref[:, cols]) for j in range(2))
+        mixed_ref[:, cols] = jnp.where(low, a, b).astype(BF)
+
+
+def attend(idx, lens, blocks, w_lats, w_bigs, deps=()):
+    rows, d = blocks[0].shape
+    keys, n_lat = 8 * rows, GROUPS * LAT_HEAD
+    outs = [(rows, QW), (HEADS * rows, keys), (HEADS * rows, LAT_HEAD), (HEADS * rows, LAT_HEAD), (rows, QW)]
+    outs += [(keys, d), (keys, n_lat), (d, QW), (LAT_HEAD, QW), (LAT_HEAD, QW), (n_lat, d)]
+    macs = 2 * HEADS * rows * keys * LAT_HEAD + keys * d * n_lat
+    return call(
+        attend_kernel, 2, [(v, BF) for v in outs], [((2 * rows, keys), F32)], limit=60,
+        far_in=range(18), far_out=range(1, 11),
+    )(
+        idx, lens, *blocks, *w_lats, *w_bigs, deps=deps
+    )
+
+
+def quarters(idx, parts):
+    own, near, far, diag, other, last = parts
+    half = far.shape[0]
+    yield own, at(idx[FS], 2 * half)
+    yield near, at(idx[FS + 1], 2 * half)
+    yield far, at(idx[FS + 2] * 2 + idx[Y0], half)
+    yield diag, at(idx[FS + 3] * 2 + idx[Y0], half)
+    yield other, at(idx[FS + 2] * 2 + idx[Y1], half)
+    yield last, at(idx[FS + 3] * 2 + idx[Y1], half)
+
+
+def project_kernel(idx, mixed, tok, *refs):
+    parts, (cot, cot_up, cot_far, gu_c, resid_ref, normed_ref, pack_ref, corner_ref) = refs[:4], refs[4:]
+    total = tok[...].astype(F32)
+    for k, w in enumerate(parts):
+        total = total + dot_nn(mixed[:, at(idx[FS + k], w.shape[0])], w[...])
+    resid_ref[...] = total
+    normed = (total * fold(total)).astype(BF)
+    normed_ref[...] = normed
+    rows = normed.shape[0]
+    corner_ref[0:rows, :] = normed
+    corner_ref[rows:, :] = cot[...]
+    pack_ref[0:rows, :] = normed
+    pack_ref[rows : 2 * rows, :] = cot_up[...]
+    pack_ref[2 * rows : 3 * rows, :] = cot_far[...]
+    pack_ref[3 * rows :, 0 : gu_c.shape[1]] = gu_c[...]
+    pack_ref[3 * rows :, gu_c.shape[1] :] = jnp.zeros((rows, pack_ref.shape[1] - gu_c.shape[1]), BF)
+
+
+def columns_kernel(idx, gate_ref, up_ref, gain_ref, own_ref, near_ref, far_ref, other_ref, all_ref):
+    gain = gain_ref[...].astype(F32)
+    n, rows, two = all_ref.shape
+    cols = gate_ref.shape[1] // n
+    gap = jnp.zeros((rows, two // 2 - cols), BF)
+    for j in range(n):
+        for part, ref in enumerate((gate_ref, up_ref)):
+            block = (ref[:, j * cols : (j + 1) * cols].astype(F32) * gain).astype(BF)
+            all_ref[j, :, part * (two // 2) : (part + 1) * (two // 2)] = jnp.concatenate([block, gap], axis=1)
+    band = at(idx[Y0], rows // 2)
+    own_ref[...] = all_ref[2 * idx[FS] + idx[ZL]]
+    near_ref[...] = all_ref[2 * idx[FS + 1] + idx[ZL]]
+    far_ref[...] = all_ref[2 * idx[FS + 2] + idx[ZL], band, :]
+    other_ref[...] = all_ref[2 * idx[FS + 3] + idx[ZL], band, :]
+
+
+def assemble_kernel(idx, *refs):
+    parts, (down, gu_ref, dn_ref) = refs[:6], refs[6:]
+    n = gu_ref.shape[1]
+    for i, (w, where) in enumerate(quarters(idx, parts)):
+        gu_ref[where, :] = w[-parts[2].shape[0] :, :n] if i == 3 else w[...]
+    n = down.shape[0] // 2
+    dn_ref[0:n, :] = down[at(idx[ZL], n), :]
+    dn_ref[n:, :] = jnp.zeros((dn_ref.shape[0] - n, dn_ref.shape[1]), BF)
+
+
+def rows_of(ref, where, rows):
+    return ref[where : where + rows, :]
+
+
+def unit_kernel(places, n0, n1, c0, c1, w_gu, w_dn, hid_ref, both_ref, dkeep, dsend, okeep, osend):
+    rows = dkeep.shape[0]
+    wide = w_dn.shape[0]
+    n0, n1, c0, c1 = (rows_of(ref, p, rows) for ref, p in zip((n0, n1, c0, c1), places))
+    both = dot_nn(jnp.concatenate([n0, n1], 0), w_gu[...])
+    gate, upward = both[:, :wide], both[:, wide:]
+    dhid = contract_cols(jnp.concatenate([c0, c1], 0), w_dn[...]).astype(BF).astype(F32)
+    sig = jax.nn.sigmoid(gate)
+    act = gate * sig
+    hid = (act * upward).astype(BF)
+    hid_ref[...] = hid
+    both_ref[:, :wide] = (dhid * upward * sig * (1.0 + gate * (1.0 - sig))).astype(BF)
+    both_ref[:, wide:] = (dhid * act).astype(BF)
+    dn = contract_cols(both_ref[...], w_gu[...])
+    dkeep[...] = dn[:rows]
+    dsend[...] = dn[rows:].astype(BF)
+    out = dot_nn(hid, w_dn[...])
+    okeep[...] = out[:rows]
+    osend[...] = out[rows:].astype(BF)
+
+
+def relative_columns(idx, shard):
+    return [at(2 * idx[yy] + idx[zz], shard) for yy in (Y1, Y0) for zz in (ZH1, ZH0)]
+
+
+def grow_kernel(places, idx, hid, both, n0, n1, c0, c1, *refs):
+    down_ref, gu_ref = refs[-2:]
+    shard = n0.shape[1] // 4
+    rows = hid.shape[0] // 2
+    for j, cols in enumerate(relative_columns(idx, shard)):
+        here = slice(j * shard, (j + 1) * shard)
+        v0, v1, t0, t1 = (ref[p : p + rows, cols] for ref, p in zip((n0, n1, c0, c1), places))
+        down = contract_rows(hid[...], jnp.concatenate([t0, t1], 0))
+        gu = contract_rows(both[...], jnp.concatenate([v0, v1], 0))
+        if len(refs) == 4:
+            down, gu = down + refs[0][:, here], gu + refs[1][:, here]
+        down_ref[:, here] = down
+        gu_ref[:, here] = gu
+
+
+def last_kernel(ff8, places, idx, hid, both, n0, n1, c0, c1, down_ref, gu_ref, send1, keep1, send2, keep2):
+    shard = n0.shape[1] // 4
+    rows = hid.shape[0] // 2
+    wide = (ff8 + 127) // 128 * 128
+    for j, cols in enumerate(relative_columns(idx, shard)):
+        here = slice(j * shard, (j + 1) * shard)
+        there = slice(j % 2 * shard, (j % 2 + 1) * shard)
+        v0, v1, t0, t1 = (ref[p : p + rows, cols] for ref, p in zip((n0, n1, c0, c1), places))
+        down = down_ref[:, here] + contract_rows(hid[...], jnp.concatenate([t0, t1], 0))
+        gu = gu_ref[:, here] + contract_rows(both[...], jnp.concatenate([v0, v1], 0))
+        one, two = (send1, send2) if j < 2 else (keep1, keep2)
+        one[0:ff8, there] = down[0:ff8].astype(BF)
+        one[ff8:, there] = gu[0:ff8].astype(BF)
+        two[:, there] = gu[wide : wide + ff8].astype(BF)
+
+
+def middle_kernel(idx, dkeep, near, far, up, diag, resid_ref, cot, *refs):
+    parts, (dresid_ref, dattn_ref, dmixed_ref, sum_ref) = refs[:4], refs[4:]
+    e = dkeep[...]
+    for v in (near, far, up, diag):
+        e = e + v[...].astype(F32)
+    resid = resid_ref[...]
+    rms = fold(resid)
+    n = resid * rms
+    en = e * n
+    dresid = cot[...].astype(F32) + rms * (e - n * jnp.mean(en, axis=-1, keepdims=True))
+    dresid_ref[...] = dresid
+    dattn = dresid.astype(BF)
+    dattn_ref[...] = dattn
+    sum_ref[...] = jnp.broadcast_to(jnp.sum(en, axis=0, keepdims=True), sum_ref.shape)
+    for k, w in enumerate(parts):
+        dmixed_ref[:, at(idx[FS + k], w.shape[0])] = contract_cols(dattn, w[...]).astype(BF)
+
+
+def outer_out_kernel(idx, mixed, dattn, send, keep):
+    rows = mixed.shape[0]
+    shard = send.shape[2]
+    for out, ks in ((send, (1, 3)), (keep, (0, 2))):
+        for i, k in enumerate(ks):
+            right = dattn[:, at(idx[FS + k], shard)]
+            for j, yy in enumerate((Y1, Y0)):
+                for kz in range(4):
+                    left = mixed[:, at(2 * idx[ZS + kz] + idx[yy], rows)]
+                    out[i, (4 * j + kz) * rows : (4 * j + kz + 1) * rows, :] = contract_rows(left, right).astype(BF)
+
+
+def attend_back_kernel(idx, dm_ref, q_ref, lat_ref, wk_ref, wv_ref, probs_ref, out_ref, qs_ref, dlat_ref, send, keep, dq_ref, up_ref, ds_ref, do_ref, dqs_ref):
+    rows = dm_ref.shape[0]
+    width = GQ * rows
+    half = HD // 2
+    low = lax.broadcasted_iota(jnp.int32, (rows, 2 * HD), 1) < HD
+    for p in range(HEADS // 2):
+        cols = slice(p * 2 * HD, (p + 1) * 2 * HD)
+        dm = dm_ref[:, cols]
+        none = jnp.zeros_like(dm)
+        for j, own in enumerate((jnp.where(low, dm, none), jnp.where(low, none, dm))):
+            do_ref[(2 * p + j) * rows : (2 * p + j + 1) * rows, :] = contract_cols(own, wv_ref[:, cols]).astype(BF)
+    for g in range(GROUPS):
+        lat = lat_ref[:, g * LAT_HEAD : (g + 1) * LAT_HEAD]
+        for r in range(0, width, 2 * rows):
+            band = slice(g * width + r, g * width + r + 2 * rows)
+            do = do_ref[band, :]
+            delta = jnp.sum(do.astype(F32) * out_ref[band, :].astype(F32), axis=-1, keepdims=True)
+            ds_ref[band, :] = (probs_ref[band, :].astype(F32) * (contract_cols(do, lat) - delta)).astype(BF)
+        band = slice(g * width, (g + 1) * width)
+        dlat_ref[:, g * LAT_HEAD : (g + 1) * LAT_HEAD] = (
+            contract_rows(ds_ref[band, :], qs_ref[band, :]) + contract_rows(probs_ref[band, :], do_ref[band, :])
+        ).astype(BF)
+        dqs_ref[band, :] = (dot_nn(ds_ref[band, :], lat) * SCALE).astype(BF)
+    for p in range(HEADS // 2):
+        cols = slice(p * 2 * HD, (p + 1) * 2 * HD)
+        bands = [slice((2 * p + j) * rows, (2 * p + j + 1) * rows) for j in range(2)]
+        a, b = (dot_nn(dqs_ref[band, :], wk_ref[:, cols]) for band in bands)
+        dq_ref[:, cols] = jnp.where(low, a, b).astype(BF)
+        f, s = divmod(4 * p, 8)
+        for j, band in enumerate(bands):
+            gk = contract_rows(q_ref[:, cols], dqs_ref[band, :]).astype(BF)
+            gv = contract_rows(dm_ref[:, cols], out_ref[band, :]).astype(BF)
+            for i in range(2):
+                piece = slice((2 * j + i) * half, (2 * j + i + 1) * half)
+                up_ref[f, s + 2 * j + i, 0:half, :] = gk[piece, :]
+                up_ref[f, s + 2 * j + i, half:HD, :] = gv[piece, :]
+    for k in range(4):
+        for out, yy in ((send, Y1), (keep, Y0)):
+            block = 2 * idx[ZS + k] + idx[yy]
+            n = dlat_ref.shape[1]
+            out[k * rows : (k + 1) * rows, 0:n] = dlat_ref[at(block, rows), :]
+            out[k * rows : (k + 1) * rows, n:] = dq_ref[:, at(block, 2 * HD)]
+
+
+def bundle_kernel(idx, dlat, na, wlt, dq, wq, ups, sum_ref, e_ref, send, keep, part_ref, sums_ref):
+    rows = dq.shape[0]
+    e = contract_cols(dq[...], wq[...])
+    e_ref[...] = e
+    total = jnp.sum(na[at(idx[ROW0] // rows, rows), :].astype(F32) * e, axis=0, keepdims=True)
+    for g in range(GROUPS):
+        band = slice(g * LAT_HEAD, (g + 1) * LAT_HEAD)
+        part = contract_rows(dlat[:, band], na[...])
+        part_ref[band, :] = part.astype(BF)
+        total = total + jnp.sum(part * wlt[band, :].astype(F32), axis=0, keepdims=True)
+    line = lax.broadcasted_iota(jnp.int32, (16, total.shape[1]), 0)
+    sums_ref[...] = jnp.where(line == 0, total, jnp.where(line == 1, sum_ref[0:1, :], 0.0)).astype(BF)
+    shard = send.shape[3]
+    n_lat = part_ref.shape[0] // 8
+    for out, ks in ((send, (1, 3)), (keep, (0, 2))):
+        for i, k in enumerate(ks):
+            cols = at(idx[FS + k], shard)
+            for j, yy in enumerate((Y1, Y0)):
+                for kz in range(4):
+                    s = 2 * idx[ZS + kz] + idx[yy]
+                    out[i, 4 * j + kz, 0:HD, :] = ups[idx[FS + k], s]
+                    out[i, 4 * j + kz, HD : HD + n_lat, :] = part_ref[at(s, n_lat), cols]
+                    out[i, 4 * j + kz, HD + n_lat :, :] = sums_ref[:, cols]
+
+
+def outer_query_kernel(idx, na, p0, p1, p2, p3, send, keep, total_ref):
+    rows = p0.shape[0]
+    wide = 2 * HD
+    total = None
+    for k, piece in enumerate((p0, p1, p2, p3)):
+        first = piece.shape[1] - 2 * wide
+        for j, yy in enumerate((Y0, Y1)):
+            right = piece[:, first + j * wide : first + (j + 1) * wide]
+            term = contract_rows(na[at(2 * idx[ZS + k] + idx[yy], rows), :], right)
+            total = term if total is None else total + term
+    total_ref[...] = total.astype(BF)
+    shard = send.shape[1]
+    for out, ks in ((send, (1, 3)), (keep, (0, 2))):
+        for i, k in enumerate(ks):
+            out[i, :, :] = total_ref[at(idx[FS + k], shard), :]
+
+
+def tokens_kernel(p0, p1, p2, p3, e_ref, wlt, tok, dresid, out_ref):
+    n = wlt.shape[0]
+    dlat = wide_sum(p0[:, 0:n], p1[:, 0:n]) + wide_sum(p2[:, 0:n], p3[:, 0:n])
+    e = e_ref[...] + dot_nn(dlat.astype(BF), wlt[...])
+    values = tok[...].astype(F32)
+    rms = fold(values)
+    n = values * rms
+    out_ref[...] = (dresid[...] + rms * (e - n * jnp.mean(e * n, axis=-1, keepdims=True))).astype(BF)
+
+
+def wide_sum(left, right):
+    return left.astype(F32) + right.astype(F32)
+
+
+def pass_kernel(*refs):
+    n = len(refs) // 2
+    for src, dst in zip(refs[:n], refs[n:]):
+        dst[...] = src[...]
+
+
+def through(values, deps):
+    return call(pass_kernel, 0, [(v.shape, v.dtype) for v in values])(*values, deps=deps)
+
+
+def pairs_kernel(*refs):
+    n = len(refs) // 3
+    for i in range(n):
+        refs[2 * n + i][...] = wide_sum(refs[2 * i][...], refs[2 * i + 1][...]).astype(BF)
+
+
+def add_pairs(pairs, deps=()):
+    return call(pairs_kernel, 0, [(a.shape, BF) for a, _ in pairs])(*[v for pair in pairs for v in pair], deps=deps)
+
+
+def halves_kernel(*refs):
+    n = len(refs) // 4
+    for i in range(n):
+        total = wide_sum(refs[2 * i][...], refs[2 * i + 1][...]).astype(BF)
+        first, second = refs[2 * n + 2 * i : 2 * n + 2 * i + 2]
+        cut = first.shape[1]
+        first[...] = total[:, :cut]
+        second[...] = total[:, cut:]
+
+
+def two_kernel(keep, there, own, far):
+    own[...] = wide_sum(keep[0], there[0]).astype(BF)
+    far[...] = wide_sum(keep[1], there[1]).astype(BF)
+
+
+def eleventh_kernel(up_keep, up_there, go_keep, go_there, up_a, go_own, cross):
+    n, shard = up_a.shape
+    total = wide_sum(up_keep[...], up_there[...]).astype(BF)
+    up_a[...] = total[:, shard:]
+    cross[0:n, :] = total[:, :shard]
+    go_own[...] = wide_sum(go_keep[0], go_there[0]).astype(BF)
+    cross[n:, :] = wide_sum(go_keep[1], go_there[1]).astype(BF)
+
+
+def exchange_kernel(keep, there, go_own, cross, b_keep, b_there, p0, p1, p2, p3, go_all, b_own, b_far, up_b):
+    two_kernel(b_keep, b_there, b_own, b_far)
+    rows, wide = p0.shape
+    n = wide - 4 * HD
+    for k, out in enumerate((p0, p1, p2, p3)):
+        band = slice(k * rows, (k + 1) * rows)
+        out[:, 0:n] = wide_sum(keep[band, 0:n], there[band, 0:n]).astype(BF)
+        out[:, n : n + 2 * HD] = keep[band, n:]
+        out[:, n + 2 * HD :] = there[band, n:]
+    n = up_b.shape[0]
+    up_b[...] = cross[0:n, :]
+    go_all[...] = wide_sum(go_own[...], cross[n:, :]).astype(BF)
+
+
+def later_kernel(b_own, b_far, go_all, send, keep):
+    half, tall = b_own.shape[0] // 2, b_own.shape[1]
+    n = go_all.shape[0] // 2
+    for out, h in ((send, 0), (keep, 1)):
+        for i in range(half):
+            out[i * tall : (i + 1) * tall, :] = wide_sum(b_own[h * half + i], b_far[h * half + i]).astype(BF)
+        out[half * tall :, :] = go_all[h * n : (h + 1) * n, :]
+
+
+def quarters_kernel(rows, keep, there, q_keep, q_there, *outs):
+    two_kernel(q_keep, q_there, outs[4], outs[5])
+    tall = outs[0].shape[0] - rows
+    for k in range(4):
+        for lo, n, into in ((k * tall, tall, 0), (4 * tall + k * rows, rows, tall)):
+            outs[k][into : into + n, :] = wide_sum(keep[lo : lo + n, :], there[lo : lo + n, :]).astype(BF)
+
+
+def stack_kernel(*refs):
+    out = refs[-1]
+    rows = refs[0].shape[0]
+    for i, ref in enumerate(refs[:-1]):
+        out[i * rows : (i + 1) * rows, :] = ref[...]
+
+
+def outputs_kernel(k0, k1, k2, k3, there, own, *outs):
+    rows = own.shape[0]
+    own[...] = wide_sum(k0[...], there[0:rows, :])
+    for i, (keep, out) in enumerate(zip((k1, k2, k3), outs)):
+        out[...] = wide_sum(keep[...], there[(i + 1) * rows : (i + 2) * rows, :]).astype(BF)
+
+
+def swap(value, axis):
+    return lax.ppermute(value, axis, [(0, 1), (1, 0)])
+
+
+def hop(value, k):
+    return lax.ppermute(value, "z", [(i, i ^ k) for i in range(4)])
+
+
+def corner(value):
+    return lax.ppermute(value, ("x", "z"), [(i, i ^ 5) for i in range(8)])
+
+
+def plus(left, right):
+    return left.astype(F32) + right.astype(F32)
+
+
+def fast_body(tokens, attn_gain, w_query, w_latent, w_key_up, w_value_up, w_out, mlp_gain, w_gate, w_up, w_down, lengths, cotangent):
+    x, c, z, y = (lax.axis_index(a) for a in ("x", "c", "z", "y"))
+    f, s, zl, zh = 2 * x + c, 2 * z + y, lax.rem(z, 2), z // 2
+    rows, d = tokens.shape
+    shard = d // 4
+    half = shard // 2
+    ff8 = w_gate.shape[1] // 8
+    wide = (ff8 + 127) // 128 * 128
+    n_lat = GROUPS * LAT_HEAD
+    keys = 8 * rows
+
+    cw = [(RING[i], RING[(i + 1) % 8]) for i in range(8)]
+    ccw = [(b, a) for a, b in cw]
+    place = jnp.where(y == 0, z, 7 - z)
+
+    def owner(p):
+        p = lax.rem(p + 8, 8)
+        return jnp.where(p < 4, 2 * p, 15 - 2 * p)
+
+    def ring(value, pairs):
+        return lax.ppermute(value, ("z", "y"), pairs)
+
+    def fold_into(gain, weight):
+        return (weight.astype(F32) * gain).astype(BF)
+
+    owners = [s, owner(place - 1), owner(place + 1), owner(place - 2), owner(place + 2), owner(place - 3), owner(place + 3), owner(place - 4)]
+    idx = jnp.stack(owners + [f, f ^ 1, f ^ 2, f ^ 3, z, z ^ 1, z ^ 2, z ^ 3, y, y ^ 1, zh, zh ^ 1, zl, s * rows]).astype(jnp.int32)
+    gain_a = attn_gain.astype(F32)[:, None]
+    gain_m = mlp_gain.astype(F32)[:, None]
+
+    a1, b1 = ring(tokens, cw), ring(tokens, ccw)
+    wl_own = fold_into(gain_a, w_latent)
+    wl_far, wl_near = swap(wl_own, "x"), swap(wl_own, "c")
+    cut = QW * 3 // 4
+    a1, b1 = through((a1, b1), (wl_far,))
+    a2, b2 = ring(a1, cw), ring(b1, ccw)
+    wl_diag = swap(wl_far, "c")
+    wb_own = jnp.concatenate([fold_into(gain_a, w_query), w_key_up, w_value_up], axis=1)
+    wb_own, wb_a, wb_b = through((wb_own, wb_own[:, :cut], wb_own[:, cut:]), (a1,))
+    wb_near, wb_far = swap(wb_own, "c"), [swap(wb_a, "x")]
+    gu_shapes = [((shard, 2 * wide), BF)] * 2 + [((half, 2 * wide), BF)] * 2
+    gu_own, gu_near, gu_far, gu_other = call(columns_kernel, 1, gu_shapes, [((8, shard, 2 * wide), BF)], limit=16)(
+        idx, w_gate, w_up, mlp_gain[:, None], deps=(a1,)
+    )
+    gu_near = swap(gu_near, "c")
+    a2, b2 = through((a2, b2), (wb_far[0], gu_own))
+    a3, b3 = ring(a2, cw), ring(b2, ccw)
+    wb_far.append(swap(through((wb_b,), (a2,))[0], "x"))
+    a3, wo_own = through((a3, w_out), (b3, wb_far[1]))
+    a4 = ring(a3, cw)
+    wo_far, wo_near = swap(wo_own, "x"), swap(wo_own, "c")
+    wb_diag = [swap(v, "c") for v in wb_far]
+
+    a4, gu_far, gu_other, cot = through((a4, gu_far, gu_other, cotangent), (wo_far,))
+    wo_diag = swap(wo_far, "c")
+    gu_far, gu_other = swap(gu_far, "x"), swap(gu_other, "x")
+    cot_far, cot_up, cot_near = swap(cot, "x"), hop(cot, 1), swap(cot, "c")
+    mixed, probs, outs, qs, queries, na_all, lat_all, w_q, w_key, w_value, w_lat_t = attend(
+        idx, lengths, (tokens, a1, b1, a2, b2, a3, b3, a4), (wl_own, wl_near, wl_far, wl_diag), (wb_own, wb_near, *wb_far, *wb_diag)
+    )
+    w_os = (w_out, wo_near, wo_far, wo_diag)
+    resid, normed, pack, corner_rows = call(
+        project_kernel, 1, [((rows, d), F32), ((rows, d), BF), ((4 * rows, d), BF), ((2 * rows, d), BF)]
+    )(idx, mixed, tokens, *w_os, cot, cot_up, cot_far, gu_other, deps=(gu_far,))
+
+    pack = swap(pack, "c")
+    nm_far, nm_up, diag_rows = swap(normed, "x"), hop(normed, 1), corner(corner_rows)
+    gu_y, gu_yc = through((gu_far, gu_other), (normed,))
+    gu_y = swap(gu_y, "y")
+    gu_yc = lax.ppermute(gu_yc, ("c", "y"), [(i, i ^ 3) for i in range(4)])
+    nm_up2, nm_far2, diag_rows2 = swap(nm_up, "c"), swap(nm_far, "c"), swap(diag_rows, "c")
+    w_gu, w_dn = call(assemble_kernel, 1, [((d, 2 * wide), BF), ((wide, d), BF)])(
+        idx, gu_own, gu_near, gu_far, pack, gu_y, gu_yc, w_down, deps=(nm_far, nm_up, diag_rows)
+    )
+
+    def unit(places, *args, deps=()):
+        shapes = [((2 * rows, wide), BF), ((2 * rows, 2 * wide), BF), ((rows, d), F32), ((rows, d), BF), ((rows, d), F32), ((rows, d), BF)]
+        return call(functools.partial(unit_kernel, places), 0, shapes)(*args, w_gu, w_dn, deps=deps)
+
+    def grow(places, *args, deps=()):
+        return call(functools.partial(grow_kernel, places), 1, [((wide, d), F32), ((2 * wide, d), F32)], limit=12)(idx, *args, deps=deps)
+
+    at_own, at_up, at_far, at_diag = (0, 0, 0, 0), (0, 0, 0, rows), (0, 0, 0, 2 * rows), (0, 0, rows, rows)
+    own_rows, up_rows, far_rows = (normed, pack, cot, cot_near), (nm_up, nm_up2, cot_up, pack), (nm_far, nm_far2, cot_far, pack)
+    diag_rows = (diag_rows, diag_rows2, diag_rows, diag_rows2)
+    own = unit(at_own, *own_rows)
+    sums = grow(at_own, *own[:2], *own_rows)
+    up = unit(at_up, *up_rows, deps=(sums[0],))
+    far = unit(at_far, *far_rows, deps=(up[0],))
+    diag = unit(at_diag, *diag_rows, deps=(far[0],))
+    d_near2, d_up2, d_far2, d_diag2 = (swap(v[3], "c") for v in (own, up, far, diag))
+    early = add_pairs([(up[2], d_up2), (far[2], d_far2), (diag[2], d_diag2)], deps=(d_near2,))
+    d_up, d_far, d_diag = hop(early[0], 1), swap(early[1], "x"), corner(early[2])
+    sums = grow(at_up, *up[:2], *up_rows, *sums, deps=early)
+    sums = grow(at_far, *far[:2], *far_rows, *sums)
+    shapes = [((2 * ff8, 2 * shard), BF)] * 2 + [((ff8, 2 * shard), BF)] * 2
+    y1_send, y1_keep, y2_send, y2_keep = call(functools.partial(last_kernel, ff8, at_diag), 1, shapes)(idx, *diag[:2], *diag_rows, *sums)
+    y1_there = swap(y1_send, "y")
+    dresid, dattn, dmixed, v_m = call(middle_kernel, 1, [((rows, d), F32), ((rows, d), BF), ((rows, QW), BF), ((8, d), F32)])(
+        idx, own[2], d_near2, d_far, d_up, d_diag, resid, cotangent, *w_os, deps=(y1_there,)
+    )
+
+    def home(value, flip, m):
+        pairs = []
+        for i in range(32):
+            xx, cc, zz, yy = i // 16, i // 8 % 2, i // 2 % 4, i % 2
+            pairs.append((i, ((yy * 2 + (zz // 2 ^ m)) * 4 + 2 * (xx ^ flip) + cc) * 2 + zz % 2))
+        return lax.ppermute(value, ("x", "c", "z", "y"), pairs)
+
+    go_send, go_keep = call(outer_out_kernel, 1, [((2, QW, shard), BF)] * 2)(idx, mixed, dattn)
+    go_there = swap(go_send, "c")
+    f1_b, f1_a = call(halves_kernel, 0, [((2 * ff8, shard), BF)] * 2)(y1_keep, y1_there, deps=(go_send,))
+    f1_a, f1_b = home(f1_a, 0, 0), swap(f1_b, "x")
+    y2_there = swap(through((y2_send,), (go_send,))[0], "y")
+    dlat, p_send, p_keep, dq, ups = call(
+        attend_back_kernel,
+        1,
+        [((keys, n_lat), BF)] + [((4 * rows, n_lat + 2 * HD), BF)] * 2 + [((rows, QW), BF), ((4, 8, HD, LAT_HEAD), BF)],
+        [((HEADS * rows, keys), BF), ((HEADS * rows, LAT_HEAD), BF), ((HEADS * rows, LAT_HEAD), BF)],
+        limit=40,
+        far_in=range(1, 8),
+    )(idx, dmixed, queries, lat_all, w_key, w_value, probs, outs, qs, deps=(y1_there, go_send))
+    tall = HD + n_lat // 8 + 16
+    e_q, b_send, b_keep = call(
+        bundle_kernel,
+        1,
+        [((rows, d), F32), ((2, 8, tall, shard), BF), ((2, 8, tall, shard), BF)],
+        [((n_lat, d), BF), ((16, d), BF)],
+        limit=24,
+        far_in=(1, 2, 4),
+    )(idx, dlat, na_all, w_lat_t, dq, w_q, ups, v_m)
+    f2_a, go_own, cross = call(eleventh_kernel, 0, [((ff8, shard), BF), ((QW, shard), BF), ((ff8 + QW, shard), BF)])(
+        y2_keep, y2_there, go_keep, go_there, deps=(b_send, f1_a)
+    )
+    f1_b, b_send, p_send = through((f1_b, b_send, p_send), (cross,))
+    p_there = swap(p_send, "y")
+    f2_a, f1_b2 = home(f2_a, 0, 0), home(f1_b, 1, 1)
+    cross, b_there = swap(cross, "x"), swap(b_send, "c")
+    shapes = [((rows, n_lat + 4 * HD), BF)] * 4 + [((QW, shard), BF)] + [((8, tall, shard), BF)] * 2 + [((ff8, shard), BF)]
+    p0, p1, p2, p3, go_all, b_own, b_sum, f2_b = call(exchange_kernel, 0, shapes)(
+        p_keep, p_there, go_own, cross, b_keep, b_there, deps=(f2_a, f1_b2)
+    )
+    pieces = (p0, hop(p1, 1), hop(p2, 2), hop(p3, 3))
+    b_far = swap(b_sum, "x")
+    o_there = swap(call(stack_kernel, 0, [((4 * rows, d), BF)])(*[v[5] for v in (own, up, far, diag)], deps=(b_sum,))[0], "c")
+    flat = ((4 * (tall + rows), shard), BF)
+    yz_send, yz_keep = call(later_kernel, 0, [flat] * 2)(b_own, b_far, go_all, deps=pieces[1:])
+    gq_send, gq_keep = call(outer_query_kernel, 1, [((2, shard, 2 * HD), BF)] * 2, [((d, 2 * HD), BF)], far_in=(0,))(idx, na_all, *pieces, deps=(yz_send,))
+    o_own, o_up, o_far, o_diag = call(outputs_kernel, 0, [((rows, d), F32)] + [((rows, d), BF)] * 3)(
+        *[v[4] for v in (own, up, far, diag)], o_there, deps=(yz_send,)
+    )
+    f2_b2 = home(through((f2_b,), (yz_send,))[0], 1, 1)
+    yz_there, gq_there = swap(yz_send, "y"), swap(gq_send, "c")
+    o_up, o_far, o_diag = hop(o_up, 1), swap(o_far, "x"), corner(o_diag)
+    tokens_grad = call(tokens_kernel, 0, [((rows, d), BF)])(*pieces, e_q, w_lat_t, tokens, dresid, deps=(o_own,))[0]
+    shapes = [((tall + rows, shard), BF)] * 4 + [((shard, 2 * HD), BF)] * 2
+    z0, z1, z2, z3, gq_own, gq_sum = call(functools.partial(quarters_kernel, rows), 0, shapes)(
+        yz_keep, yz_there, gq_keep, gq_there, deps=(tokens_grad, o_up, o_far, o_diag)
+    )
+    last = z0.astype(F32) + hop(z1, 1) + hop(z2, 2) + hop(z3, 3)
+    gq_far = swap(gq_sum, "x")
+
+    grad_query = plus(gq_own, gq_far) * gain_a
+    output = (resid + o_own + o_up + o_far + o_diag).astype(BF)
+    grad_down = plus(f1_a[:ff8], f1_b2[:ff8])
+    grad_gate = plus(f1_a[ff8:], f1_b2[ff8:]).T * gain_m
+    grad_up = plus(f2_a, f2_b2).T * gain_m
+    grad_out = last[tall:]
+    eighth = HD // 2
+    n_small = n_lat // 8
+    grad_key_up = last[:eighth].T
+    grad_value_up = last[eighth:HD].T
+    grad_latent = last[HD : HD + n_small].T * gain_a
+    own_gain = shard // 8
+    pair = lax.dynamic_slice(last, (HD + n_small, s * own_gain), (2, own_gain))
+    grad_attn_gain = pair[0] / lax.dynamic_slice_in_dim(gain_a[:, 0], s * own_gain, own_gain)
+    grad_mlp_gain = pair[1] / lax.dynamic_slice_in_dim(gain_m[:, 0], s * own_gain, own_gain)
+    return (
+        output,
+        tokens_grad,
+        grad_attn_gain,
+        grad_query,
+        grad_latent,
+        grad_key_up,
+        grad_value_up,
+        grad_out,
+        grad_mlp_gain,
+        grad_gate,
+        grad_up,
+        grad_down,
+    )
+
+
+def fast_solution(mesh):
+    mesh = Mesh(mesh.devices.reshape(2, 2, 4, 2), ("x", "c", "z", "y"))
+    f, s = ("x", "c"), ("z", "y")
+    a = f + s
+    in_specs = (P(a, None), P(f), P(f, None), P(f, None), P(None, f), P(None, f), P(f, None), P(f), P(f, None), P(f, None), P(f, None), P(f, None), P(a, None))
+    out_specs = (P(a, None), P(a, None), P(a), P(f, s), P(f, s), P(None, a), P(None, a), P(s, f), P(a), P(f, s), P(f, s), P(s, f))
+    return jax.shard_map(fast_body, mesh=mesh, in_specs=in_specs, out_specs=out_specs, check_vma=False)
+
+
 def solution(mesh):
+    if mesh.shape["fsdp"] == 4 and mesh.shape["seq"] == 8:
+        return fast_solution(mesh)
     in_specs = (
         P(("fsdp", "seq"), None),
         P("fsdp"),

time: 1110 us -> 267 us (0.24)
  waiting for transfers between devices: 806 us -> 97.9 us
  matrix products: 111 us -> 0 us
  blocking collectives: 84.1 us -> 0 us
  Pallas kernels: 0 us -> 59.7 us
  starting transfers between devices: 21.5 us -> 81.1 us
  loops' own time: 17.8 us -> 0 us
  other arithmetic: 23.5 us -> 7.84 us
  between operations: 15.3 us -> 2.28 us
  local copies, waits for them, and re-layouts: 25.5 us -> 14.4 us
    reduce_scatter x10 -> x0, waiting for transfers between devices: 471 us -> none  [the longest x1 137 us: body(): lax.psum_scatter(grad_key_up, ('fsdp', 'seq'), scatter_dimension=1, tiled...]
    all_gather x11 -> x0, waiting for transfers between devices: 321 us -> none  [the longest x1 50.7 us: body(): lax.all_gather(normed_m, 'seq', axis=0, tiled=True)]
    dot_general x62 -> x0, matrix products: 111 us -> none  [the longest x14 27.2 us: contract_cols(): lax.dot_general(left, right, (((1,), (1,)), ((), ())), preferred_element_...]
    ppermute x0 -> x65, waiting for transfers between devices: none -> 97.9 us  [the longest x40 23.4 us: swap(): return lax.ppermute(value, axis, [(0, 1), (1, 0)])]
    ppermute x0 -> x65, starting transfers between devices: none -> 81.1 us  [the longest x40 40.4 us: swap(): return lax.ppermute(value, axis, [(0, 1), (1, 0)])]
    pallas_call x0 -> x36, Pallas kernels: none -> 59.7 us  [run(): pl.pallas_call(body, in_specs=[pl.BlockSpec(memory_space=pltpu.SMEM)] * n...]
    unnamed x1 -> x0, blocking collectives: 39.5 us -> none
    all_gather x4 -> x0, blocking collectives: 29.1 us -> none  [the longest x1 10.5 us: body(): lax.all_gather(w_key_up, 'fsdp', axis=1, tiled=True)]
  transfers between devices with their start and end apart: 26 -> 65, of which waited for: 19 -> 24; matrix products, arithmetic and copies ran while one was open for 8% -> 3% of each run, Pallas kernels for 0% -> 18%
where the time goes in v1:
time: 267 us; the launch traced here: 263 us
  waiting for transfers between devices  97.9 us (37%)
  starting transfers between devices  81.1 us (30%)
  Pallas kernels  59.7 us (22%)
  local copies, waits for them, and re-layouts  14.4 us (5%)
  other arithmetic  7.84 us (3%)
    pallas_call x36, Pallas kernels, run(): pl.pallas_call(body, in_specs=[pl.BlockSpec(memory_space=pltpu.SMEM)] * n...  59.7 us
    ppermute x40, starting transfers between devices, swap(): return lax.ppermute(value, axis, [(0, 1), (1, 0)])  40.4 us
    ppermute x40, waiting for transfers between devices, swap(): return lax.ppermute(value, axis, [(0, 1), (1, 0)])  23.4 us
    ppermute x10, waiting for transfers between devices, hop(): return lax.ppermute(value, 'z', [(i, i ^ k) for i in range(4)])  22.3 us
    ppermute x4, waiting for transfers between devices, home(): return lax.ppermute(value, ('x', 'c', 'z', 'y'), pairs)  19.3 us
    ppermute x3, waiting for transfers between devices, corner(): return lax.ppermute(value, ('x', 'z'), [(i, i ^ 5) for i in range(8)])  15 us
    ppermute x10, starting transfers between devices, hop(): return lax.ppermute(value, 'z', [(i, i ^ k) for i in range(4)])  14.6 us
    ppermute x7, waiting for transfers between devices, ring(): return lax.ppermute(value, ('z', 'y'), pairs)  13 us
  transfers between devices with their start and end apart: 65, of which 24 were waited for; matrix products, arithmetic and copies ran while one was open for 3% of the time, Pallas kernels for 18%

profile of v1, /device:TPU:0, one launch (start us, length us, event | category | flops | bytes accessed | tf_op | source)
XLA Modules:
  0.0 263.2 jit_solution(7897105040990184764)
XLA Ops:
  0.7 3.1 %collective-permute-start = (bf16[128,1024]{1,0:T(8,128)(2,1)}, bf16[128,1024]{1,0:T(8,128)(2,1)S(1)}, u32[]{:S(2)}, u32[]{:S(2)}) collective-permute-start(bf16[128,1024]{1,0:T(8,128)(2,1)} %refs_6_.1), channel_id=1, source_target_pairs={{0,2},{2,4},{4,6},{6,7},{7,5},{5,3},{3,1},{1,0},{8,10},{10,12},{12... | collective-permute-start | bytes 786440 | tf_op jit(solution)/shard_map/ppermute | solution.py:903
  8.9 4.5 %collective-permute-done.2.refs_2_.refs_12_ = bf16[256,512]{1,0:T(8,128)(2,1)S(1)} collective-permute-done((bf16[256,512]{1,0:T(8,128)(2,1)S(1)}, bf16[256,512]{1,0:T(8,128)(2,1)S(1)}, u32[]{:S(2)}, u32[]{:S(2)}) %collective-permute-start.2) | collective-permute-done | bytes 262176 | tf_op jit(solution)/shard_map/ppermute | solution.py:868
  27.8 4.3 %collective-permute-done.6.refs_0_ = bf16[128,1024]{1,0:T(8,128)(2,1)S(1)} collective-permute-done((bf16[128,1024]{1,0:T(8,128)(2,1)S(1)}, bf16[128,1024]{1,0:T(8,128)(2,1)S(1)}, u32[]{:S(2)}, u32[]{:S(2)}) %collective-permute-start.6) | collective-permute-done | bytes 262176 | tf_op jit(solution)/shard_map/ppermute | solution.py:903
  38.1 5.9 %collective-permute-done.9.refs_0_ = bf16[128,1024]{1,0:T(8,128)(2,1)S(1)} collective-permute-done((bf16[128,1024]{1,0:T(8,128)(2,1)S(1)}, bf16[128,1024]{1,0:T(8,128)(2,1)S(1)}, u32[]{:S(2)}, u32[]{:S(2)}) %collective-permute-start.9) | collective-permute-done | bytes 262176 | tf_op jit(solution)/shard_map/ppermute | solution.py:903
  50.7 14.4 %shard_map.227 = (bf16[128,1024]{1,0:T(8,128)(2,1)}, bf16[2048,1024]{1,0:T(8,128)(2,1)}, bf16[2048,256]{1,0:T(8,128)(2,1)}, bf16[2048,256]{1,0:T(8,128)(2,1)}, b...) custom-call(s32[22]{0:T(128)} %copy-done.72, ...), custom_call_target="tpu_custom_call" | custom-call | flops 1 | tf_op jit(solution)/shard_map/pallas_call | solution.py:442
  74.3 10.4 %collective-permute-done.29.refs_10_.refs_0_.refs_2_.refs_3_.refs_5_ = bf16[256,1024]{1,0:T(8,128)(2,1)S(1)} collective-permute-done((bf16[256,1024]{1,0:T(8,128)(2,1)S(1)}, bf16[256,1024]{1,0:T(8,128)(2,1)S(1)}, u32[]{:S(2)}, u32[]{:S(2)}) %collective-permute-start.29) | collective-permute-done | bytes 524320 | tf_op jit(solution)/shard_map/ppermute | solution.py:876
  86.3 4.9 %collective-permute-done.26.refs_6_ = bf16[128,768]{1,0:T(8,128)(2,1)S(1)} collective-permute-done((bf16[128,768]{1,0:T(8,128)(2,1)S(1)}, bf16[128,768]{1,0:T(8,128)(2,1)S(1)}, u32[]{:S(2)}, u32[]{:S(2)}) %collective-permute-start.26) | collective-permute-done | bytes 196640 | tf_op jit(solution)/shard_map/ppermute | solution.py:952
  114.8 4.8 %collective-permute-done.37.refs_3_ = bf16[128,1024]{1,0:T(8,128)(2,1)S(1)} collective-permute-done((bf16[128,1024]{1,0:T(8,128)(2,1)S(1)}, bf16[128,1024]{1,0:T(8,128)(2,1)S(1)}, u32[]{:S(2)}, u32[]{:S(2)}) %collective-permute-start.37) | collective-permute-done | bytes 262176 | tf_op jit(solution)/shard_map/ppermute | solution.py:868
  121.6 4.6 %collective-permute-done.39.refs_5_ = bf16[128,1024]{1,0:T(8,128)(2,1)S(1)} collective-permute-done((bf16[128,1024]{1,0:T(8,128)(2,1)S(1)}, bf16[128,1024]{1,0:T(8,128)(2,1)S(1)}, u32[]{:S(2)}, u32[]{:S(2)}) %collective-permute-start.39) | collective-permute-done | bytes 262176 | tf_op jit(solution)/shard_map/ppermute | solution.py:876
  135.8 4.4 %collective-permute-start.41 = (bf16[704,256]{1,0:T(8,128)(2,1)}, bf16[704,256]{1,0:T(8,128)(2,1)S(1)}, u32[]{:S(2)}, u32[]{:S(2)}) collective-permute-start(bf16[704,256]{1,0:T(8,128)(2,1)} %get-tuple-element.201), channel_id=1, source_target_pairs={{0,16},{16,0},{1,17},{17,1},{2,18},{18,2},{3,19},{19,3},{4,20},{20... | collective-permute-start | bytes 1081352 | tf_op jit(solution)/shard_map/ppermute | solution.py:868
  140.3 8.9 %shard_map.242 = (bf16[1024,512]{1,0:T(8,128)(2,1)S(1)}, bf16[512,640]{1,0:T(8,128)(2,1)S(1)}, bf16[512,640]{1,0:T(8,128)(2,1)S(1)}, bf16[128,1024]{1,0:T(8,128)(2,1)S(1)}, bf16[4,8,64,256]{3,2,1,0:T(8,128)(2,1)S(1)}) custom-call(s32[22]{0:T(128)S(1)} %copy-done.73, bf16[128,1024]{1,0:T(8,128)(2,1)S(1)} %get-tuple-element.189.refs_1_, ...), custom_call_target="tpu_custom_call" | custom-call | flops 1 | tf_op jit(solution)/shard_map/pallas_call | solution.py:442
  149.3 3.6 %shard_map.244 = (f32[128,1024]{1,0:T(8,128)S(1)}, bf16[2,8,144,256]{3,2,1,0:T(8,128)(2,1)S(1)}, bf16[2,8,144,256]{3,2,1,0:T(8,128)(2,1)S(1)}) custom-call(s32[22]{0:T(128)S(1)} %copy-done.73, bf16[1024,512]{1,0:T(8,128)(2,1)S(1)} %get-tuple-element.202.refs_1_, bf16[1024,1024]{1,0:T(8,128)(2,1)S(1)} %copy-done, bf16[512,1024]{1,0:T(8,128)(2,1)S(1)} %copy-done.3, ...), custom_call_target="tpu_custom_call" | custom-call | flops 1 | tf_op jit(solution)/shard_map/pallas_call | solution.py:442
  156.8 5.9 %collective-permute-start.46 = (bf16[1376,256]{1,0:T(8,128)(2,1)S(1)}, bf16[1376,256]{1,0:T(8,128)(2,1)S(1)}, u32[]{:S(2)}, u32[]{:S(2)}) collective-permute-start(bf16[1376,256]{1,0:T(8,128)(2,1)S(1)} %get-tuple-element.215.refs_3_), channel_id=1, source_target_pairs={{0,16},{16,0},{1,17},{17,1},{2,18},{18,2},{3,19},{19,3},{4,20},{20... | collective-permute-start | bytes 2113544 | tf_op jit(solution)/shard_map/ppermute | solution.py:868
  162.6 2.8 %collective-permute-start.45 = (bf16[512,640]{1,0:T(8,128)(2,1)S(1)}, bf16[512,640]{1,0:T(8,128)(2,1)S(1)}, u32[]{:S(2)}, u32[]{:S(2)}) collective-permute-start(bf16[512,640]{1,0:T(8,128)(2,1)S(1)} %get-tuple-element.216), channel_id=1, source_target_pairs={{0,1},{1,0},{2,3},{3,2},{4,5},{5,4},{6,7},{7,6},{8,9},{9,8},{10,11... | collective-permute-start | bytes 1966088 | tf_op jit(solution)/shard_map/ppermute | solution.py:868
  168.0 18.9 %collective-permute-done.49.refs_7_ = bf16[704,256]{1,0:T(8,128)(2,1)S(1)} collective-permute-done((bf16[704,256]{1,0:T(8,128)(2,1)S(1)}, bf16[704,256]{1,0:T(8,128)(2,1)S(1)}, u32[]{:S(2)}, u32[]{:S(2)}) %collective-permute-start.49) | collective-permute-done | bytes 360480 | tf_op jit(solution)/shard_map/ppermute | solution.py:990
  186.9 4.4 %collective-permute-done.45.refs_1_ = bf16[512,640]{1,0:T(8,128)(2,1)S(1)} collective-permute-done((bf16[512,640]{1,0:T(8,128)(2,1)S(1)}, bf16[512,640]{1,0:T(8,128)(2,1)S(1)}, u32[]{:S(2)}, u32[]{:S(2)}) %collective-permute-start.45) | collective-permute-done | bytes 655392 | tf_op jit(solution)/shard_map/ppermute | solution.py:868
  193.4 3.2 %collective-permute-start.50 = (bf16[512,1024]{1,0:T(8,128)(2,1)}, bf16[512,1024]{1,0:T(8,128)(2,1)}, u32[]{:S(2)}, u32[]{:S(2)}) collective-permute-start(bf16[512,1024]{1,0:T(8,128)(2,1)} %shard_map.249), channel_id=1, source_target_pairs={{0,8},{8,0},{1,9},{9,1},{2,10},{10,2},{3,11},{11,3},{4,12},{12,4},... | collective-permute-start | bytes 3145736 | tf_op jit(solution)/shard_map/ppermute | solution.py:868
  197.9 3.1 %collective-permute-start.54 = (bf16[128,768]{1,0:T(8,128)(2,1)S(1)}, bf16[128,768]{1,0:T(8,128)(2,1)S(1)}, u32[]{:S(2)}, u32[]{:S(2)}) collective-permute-start(bf16[128,768]{1,0:T(8,128)(2,1)S(1)} %get-tuple-element.227), channel_id=1, source_target_pairs={{0,6},{2,4},{4,2},{6,0},{1,7},{3,5},{5,3},{7,1},{8,14},{10,12},{12... | collective-permute-start | bytes 589832 | tf_op jit(solution)/shard_map/ppermute | solution.py:872
  201.0 6.3 %collective-permute-done.52.refs_3_.refs_1_ = bf16[128,768]{1,0:T(8,128)(2,1)S(1)} collective-permute-done((bf16[128,768]{1,0:T(8,128)(2,1)S(1)}, bf16[128,768]{1,0:T(8,128)(2,1)S(1)}, u32[]{:S(2)}, u32[]{:S(2)}) %collective-permute-start.52) | collective-permute-done | bytes 196640 | tf_op jit(solution)/shard_map/ppermute | solution.py:872
  207.2 6.5 %collective-permute-done.53.refs_4_.refs_2_ = bf16[128,768]{1,0:T(8,128)(2,1)S(1)} collective-permute-done((bf16[128,768]{1,0:T(8,128)(2,1)S(1)}, bf16[128,768]{1,0:T(8,128)(2,1)S(1)}, u32[]{:S(2)}, u32[]{:S(2)}) %collective-permute-start.53) | collective-permute-done | bytes 196640 | tf_op jit(solution)/shard_map/ppermute | solution.py:872
  214.8 5.2 %collective-permute-start.64 = (bf16[352,256]{1,0:T(8,128)(2,1)}, bf16[352,256]{1,0:T(8,128)(2,1)}, u32[]{:S(2)}, u32[]{:S(2)}) collective-permute-start(bf16[352,256]{1,0:T(8,128)(2,1)} %shard_map.255), channel_id=1, source_target_pairs={{0,12},{1,28},{2,13},{3,29},{4,4},{5,20},{6,5},{7,21},{8,14},{9,30... | collective-permute-start | bytes 540680 | tf_op jit(solution)/shard_map/ppermute | solution.py:990
  236.7 5.9 %collective-permute-done.56.refs_6_ = bf16[128,1024]{1,0:T(8,128)(2,1)S(1)} collective-permute-done((bf16[128,1024]{1,0:T(8,128)(2,1)S(1)}, bf16[128,1024]{1,0:T(8,128)(2,1)S(1)}, u32[]{:S(2)}, u32[]{:S(2)}) %collective-permute-start.56) | collective-permute-done | bytes 262176 | tf_op jit(solution)/shard_map/ppermute | solution.py:868
  246.6 3.5 %collective-permute-start.61 = (bf16[272,256]{1,0:T(8,128)(2,1)S(1)}, bf16[272,256]{1,0:T(8,128)(2,1)S(1)}, u32[]{:S(2)}, u32[]{:S(2)}) collective-permute-start(bf16[272,256]{1,0:T(8,128)(2,1)S(1)} %get-tuple-element.241), channel_id=1, source_target_pairs={{0,4},{2,6},{4,0},{6,2},{1,5},{3,7},{5,1},{7,3},{8,12},{10,14},{12... | collective-permute-start | bytes 417800 | tf_op jit(solution)/shard_map/ppermute | solution.py:872
  252.9 7.5 %collective-permute-done.61 = bf16[272,256]{1,0:T(8,128)(2,1)S(1)} collective-permute-done((bf16[272,256]{1,0:T(8,128)(2,1)S(1)}, bf16[272,256]{1,0:T(8,128)(2,1)S(1)}, u32[]{:S(2)}, u32[]{:S(2)}) %collective-permute-start.61) | collective-permute-done | bytes 139296 | tf_op jit(solution)/shard_map/ppermute | solution.py:872
  (332 shorter events, 114.1 us)
Async XLA Ops:
  27.8 19.9 %collective-permute-start.13 = (bf16[256,1536]{1,0:T(8,128)(2,1)}, bf16[256,1536]{1,0:T(8,128)(2,1)S(1)}, u32[]{:S(2)}, u32[]{:S(2)}) collective-permute-start(bf16[256,1536]{1,0:T(8,128)(2,1)} %get-tuple-element.141.refs_14_), channel_id=1, source_target_pairs={{0,8},{8,0},{1,9},{9,1},{2,10},{10,2},{3,11},{11,3},{4,12},{12,4},... | collective-permute-start | bytes 2359304 | tf_op jit(solution)/shard_map/ppermute | solution.py:868
  44.4 21.4 %collective-permute-start.17 = (bf16[256,1024]{1,0:T(8,128)(2,1)S(1)}, bf16[256,1024]{1,0:T(8,128)(2,1)S(1)}, u32[]{:S(2)}, u32[]{:S(2)}) collective-permute-start(bf16[256,1024]{1,0:T(8,128)(2,1)S(1)} %collective-permute-done.10.refs_4_.refs_5_.refs_10_), channel_id=1, source_target_pairs={{0,8},{8,0},{1,9},{9,1},{2,10},{10,2},{3,11},{11,3},{4,12},{12,4},... | collective-permute-start | bytes 1572872 | tf_op jit(solution)/shard_map/ppermute | solution.py:868
  46.1 19.7 %collective-permute-start.18 = (bf16[128,1024]{1,0:T(8,128)(2,1)S(1)}, bf16[128,1024]{1,0:T(8,128)(2,1)S(1)}, u32[]{:S(2)}, u32[]{:S(2)}) collective-permute-start(bf16[128,1024]{1,0:T(8,128)(2,1)S(1)} %get-tuple-element.143.refs_7_.refs_2_.refs_5_), channel_id=1, source_target_pairs={{0,2},{2,0},{4,6},{6,4},{1,3},{3,1},{5,7},{7,5},{8,10},{10,8},{12,... | collective-permute-start | bytes 786440 | tf_op jit(solution)/shard_map/ppermute | solution.py:872
  47.7 18.1 %collective-permute-start.19 = (bf16[128,1024]{1,0:T(8,128)(2,1)S(1)}, bf16[128,1024]{1,0:T(8,128)(2,1)S(1)}, u32[]{:S(2)}, u32[]{:S(2)}) collective-permute-start(bf16[128,1024]{1,0:T(8,128)(2,1)S(1)} %get-tuple-element.143.refs_7_.refs_2_.refs_5_), channel_id=1, source_target_pairs={{0,16},{16,0},{1,17},{17,1},{2,18},{18,2},{3,19},{19,3},{4,20},{20... | collective-permute-start | bytes 786440 | tf_op jit(solution)/shard_map/ppermute | solution.py:868
  48.6 16.5 %collective-permute-start.20 = (bf16[128,768]{1,0:T(8,128)(2,1)}, bf16[128,768]{1,0:T(8,128)(2,1)S(1)}, u32[]{:S(2)}, u32[]{:S(2)}) collective-permute-start(bf16[128,768]{1,0:T(8,128)(2,1)} %get-tuple-element.144), channel_id=1, source_target_pairs={{0,16},{16,0},{1,17},{17,1},{2,18},{18,2},{3,19},{19,3},{4,20},{20... | collective-permute-start | bytes 589832 | tf_op jit(solution)/shard_map/ppermute | solution.py:868
  49.7 16.1 %collective-permute-start.21 = (bf16[128,768]{1,0:T(8,128)(2,1)}, bf16[128,768]{1,0:T(8,128)(2,1)S(1)}, u32[]{:S(2)}, u32[]{:S(2)}) collective-permute-start(bf16[128,768]{1,0:T(8,128)(2,1)} %get-tuple-element.145), channel_id=1, source_target_pairs={{0,16},{16,0},{1,17},{17,1},{2,18},{18,2},{3,19},{19,3},{4,20},{20... | collective-permute-start | bytes 589832 | tf_op jit(solution)/shard_map/ppermute | solution.py:868
  68.8 23.4 %collective-permute-start.22 = (bf16[512,1024]{1,0:T(8,128)(2,1)S(1)}, bf16[512,1024]{1,0:T(8,128)(2,1)S(1)}, u32[]{:S(2)}, u32[]{:S(2)}) collective-permute-start(bf16[512,1024]{1,0:T(8,128)(2,1)S(1)} %get-tuple-element.148), channel_id=1, source_target_pairs={{0,8},{8,0},{1,9},{9,1},{2,10},{10,2},{3,11},{11,3},{4,12},{12,4},... | collective-permute-start | bytes 3145736 | tf_op jit(solution)/shard_map/ppermute | solution.py:868
  71.8 19.9 %collective-permute-start.28 = (bf16[128,1024]{1,0:T(8,128)(2,1)S(1)}, bf16[128,1024]{1,0:T(8,128)(2,1)S(1)}, u32[]{:S(2)}, u32[]{:S(2)}) collective-permute-start(bf16[128,1024]{1,0:T(8,128)(2,1)S(1)} %get-tuple-element.147.refs_2_.refs_0_.refs_3_), channel_id=1, source_target_pairs={{0,2},{2,0},{4,6},{6,4},{1,3},{3,1},{5,7},{7,5},{8,10},{10,8},{12,... | collective-permute-start | bytes 786440 | tf_op jit(solution)/shard_map/ppermute | solution.py:872
  73.4 18.4 %collective-permute-start.27 = (bf16[128,1024]{1,0:T(8,128)(2,1)S(1)}, bf16[128,1024]{1,0:T(8,128)(2,1)S(1)}, u32[]{:S(2)}, u32[]{:S(2)}) collective-permute-start(bf16[128,1024]{1,0:T(8,128)(2,1)S(1)} %get-tuple-element.147.refs_2_.refs_0_.refs_3_), channel_id=1, source_target_pairs={{0,16},{16,0},{1,17},{17,1},{2,18},{18,2},{3,19},{19,3},{4,20},{20... | collective-permute-start | bytes 786440 | tf_op jit(solution)/shard_map/ppermute | solution.py:868
  84.7 16.3 %collective-permute-start.32 = (bf16[256,1024]{1,0:T(8,128)(2,1)S(1)}, bf16[256,1024]{1,0:T(8,128)(2,1)S(1)}, u32[]{:S(2)}, u32[]{:S(2)}) collective-permute-start(bf16[256,1024]{1,0:T(8,128)(2,1)S(1)} %collective-permute-done.29.refs_10_.refs_0_.refs_2_.refs_3_.refs_5_), channel_id=1, source_target_pairs={{0,8},{8,0},{1,9},{9,1},{2,10},{10,2},{3,11},{11,3},{4,12},{12,4},... | collective-permute-start | bytes 1572872 | tf_op jit(solution)/shard_map/ppermute | solution.py:868
  109.7 18.3 %collective-permute-start.40 = (bf16[704,512]{1,0:T(8,128)(2,1)S(1)}, bf16[704,512]{1,0:T(8,128)(2,1)S(1)}, u32[]{:S(2)}, u32[]{:S(2)}) collective-permute-start(bf16[704,512]{1,0:T(8,128)(2,1)S(1)} %get-tuple-element.188), channel_id=1, source_target_pairs={{0,1},{1,0},{2,3},{3,2},{4,5},{5,4},{6,7},{7,6},{8,9},{9,8},{10,11... | collective-permute-start | bytes 2162696 | tf_op jit(solution)/shard_map/ppermute | solution.py:868
  131.1 21.9 %collective-permute-start.43 = (bf16[2,1024,256]{2,1,0:T(8,128)(2,1)S(1)}, bf16[2,1024,256]{2,1,0:T(8,128)(2,1)}, u32[]{:S(2)}, u32[]{:S(2)}) collective-permute-start(bf16[2,1024,256]{2,1,0:T(8,128)(2,1)S(1)} %get-tuple-element.198.refs_10_.refs_2_.refs_1_), channel_id=1, source_target_pairs={{0,8},{8,0},{1,9},{9,1},{2,10},{10,2},{3,11},{11,3},{4,12},{12,4},... | collective-permute-start | bytes 3145736 | tf_op jit(solution)/shard_map/ppermute | solution.py:868
  131.2 21.7 %collective-permute-start.42 = (bf16[352,512]{1,0:T(8,128)(2,1)S(1)}, bf16[352,512]{1,0:T(8,128)(2,1)S(1)}, u32[]{:S(2)}, u32[]{:S(2)}) collective-permute-start(bf16[352,512]{1,0:T(8,128)(2,1)S(1)} %shard_map.245), channel_id=1, source_target_pairs={{0,1},{1,0},{2,3},{3,2},{4,5},{5,4},{6,7},{7,6},{8,9},{9,8},{10,11... | collective-permute-start | bytes 1081352 | tf_op jit(solution)/shard_map/ppermute | solution.py:868
  133.8 19.1 %collective-permute-start.44 = (bf16[704,256]{1,0:T(8,128)(2,1)}, bf16[704,256]{1,0:T(8,128)(2,1)S(1)}, u32[]{:S(2)}, u32[]{:S(2)}) collective-permute-start(bf16[704,256]{1,0:T(8,128)(2,1)} %get-tuple-element.214), channel_id=1, source_target_pairs={{0,0},{1,16},{2,1},{3,17},{4,8},{5,24},{6,9},{7,25},{8,2},{9,18},{... | collective-permute-start | bytes 1081352 | tf_op jit(solution)/shard_map/ppermute | solution.py:990
  135.8 19.0 %collective-permute-start.41 = (bf16[704,256]{1,0:T(8,128)(2,1)}, bf16[704,256]{1,0:T(8,128)(2,1)S(1)}, u32[]{:S(2)}, u32[]{:S(2)}) collective-permute-start(bf16[704,256]{1,0:T(8,128)(2,1)} %get-tuple-element.201), channel_id=1, source_target_pairs={{0,16},{16,0},{1,17},{17,1},{2,18},{18,2},{3,19},{19,3},{4,20},{20... | collective-permute-start | bytes 1081352 | tf_op jit(solution)/shard_map/ppermute | solution.py:868
  155.0 36.4 %collective-permute-start.47 = (bf16[2,8,144,256]{3,2,1,0:T(8,128)(2,1)S(1)}, bf16[2,8,144,256]{3,2,1,0:T(8,128)(2,1)S(1)}, u32[]{:S(2)}, u32[]{:S(2)}) collective-permute-start(bf16[2,8,144,256]{3,2,1,0:T(8,128)(2,1)S(1)} %get-tuple-element.219), channel_id=1, source_target_pairs={{0,8},{8,0},{1,9},{9,1},{2,10},{10,2},{3,11},{11,3},{4,12},{12,4},... | collective-permute-start | bytes 3538952 | tf_op jit(solution)/shard_map/ppermute | solution.py:868
  156.8 34.6 %collective-permute-start.46 = (bf16[1376,256]{1,0:T(8,128)(2,1)S(1)}, bf16[1376,256]{1,0:T(8,128)(2,1)S(1)}, u32[]{:S(2)}, u32[]{:S(2)}) collective-permute-start(bf16[1376,256]{1,0:T(8,128)(2,1)S(1)} %get-tuple-element.215.refs_3_), channel_id=1, source_target_pairs={{0,16},{16,0},{1,17},{17,1},{2,18},{18,2},{3,19},{19,3},{4,20},{20... | collective-permute-start | bytes 2113544 | tf_op jit(solution)/shard_map/ppermute | solution.py:868
  162.6 28.7 %collective-permute-start.45 = (bf16[512,640]{1,0:T(8,128)(2,1)S(1)}, bf16[512,640]{1,0:T(8,128)(2,1)S(1)}, u32[]{:S(2)}, u32[]{:S(2)}) collective-permute-start(bf16[512,640]{1,0:T(8,128)(2,1)S(1)} %get-tuple-element.216), channel_id=1, source_target_pairs={{0,1},{1,0},{2,3},{3,2},{4,5},{5,4},{6,7},{7,6},{8,9},{9,8},{10,11... | collective-permute-start | bytes 1966088 | tf_op jit(solution)/shard_map/ppermute | solution.py:868
  165.4 21.5 %collective-permute-start.49 = (bf16[704,256]{1,0:T(8,128)(2,1)S(1)}, bf16[704,256]{1,0:T(8,128)(2,1)S(1)}, u32[]{:S(2)}, u32[]{:S(2)}) collective-permute-start(bf16[704,256]{1,0:T(8,128)(2,1)S(1)} %get-tuple-element.221), channel_id=1, source_target_pairs={{0,12},{1,28},{2,13},{3,29},{4,4},{5,20},{6,5},{7,21},{8,14},{9,30... | collective-permute-start | bytes 1081352 | tf_op jit(solution)/shard_map/ppermute | solution.py:990
  193.4 31.9 %collective-permute-start.50 = (bf16[512,1024]{1,0:T(8,128)(2,1)}, bf16[512,1024]{1,0:T(8,128)(2,1)}, u32[]{:S(2)}, u32[]{:S(2)}) collective-permute-start(bf16[512,1024]{1,0:T(8,128)(2,1)} %shard_map.249), channel_id=1, source_target_pairs={{0,8},{8,0},{1,9},{9,1},{2,10},{10,2},{3,11},{11,3},{4,12},{12,4},... | collective-permute-start | bytes 3145736 | tf_op jit(solution)/shard_map/ppermute | solution.py:868
  196.6 17.1 %collective-permute-start.51 = (bf16[8,144,256]{2,1,0:T(8,128)(2,1)S(1)}, bf16[8,144,256]{2,1,0:T(8,128)(2,1)S(1)}, u32[]{:S(2)}, u32[]{:S(2)}) collective-permute-start(bf16[8,144,256]{2,1,0:T(8,128)(2,1)S(1)} %get-tuple-element.222.refs_4_), channel_id=1, source_target_pairs={{0,16},{16,0},{1,17},{17,1},{2,18},{18,2},{3,19},{19,3},{4,20},{20... | collective-permute-start | bytes 1769480 | tf_op jit(solution)/shard_map/ppermute | solution.py:868
  196.6 17.1 %collective-permute-start.53 = (bf16[128,768]{1,0:T(8,128)(2,1)S(1)}, bf16[128,768]{1,0:T(8,128)(2,1)S(1)}, u32[]{:S(2)}, u32[]{:S(2)}) collective-permute-start(bf16[128,768]{1,0:T(8,128)(2,1)S(1)} %get-tuple-element.226), channel_id=1, source_target_pairs={{0,4},{2,6},{4,0},{6,2},{1,5},{3,7},{5,1},{7,3},{8,12},{10,14},{12... | collective-permute-start | bytes 589832 | tf_op jit(solution)/shard_map/ppermute | solution.py:872
  213.9 22.8 %collective-permute-start.58 = (bf16[1088,256]{1,0:T(8,128)(2,1)S(1)}, bf16[1088,256]{1,0:T(8,128)(2,1)}, u32[]{:S(2)}, u32[]{:S(2)}) collective-permute-start(bf16[1088,256]{1,0:T(8,128)(2,1)S(1)} %get-tuple-element.228.refs_5_.refs_6_.refs_1_), channel_id=1, source_target_pairs={{0,1},{1,0},{2,3},{3,2},{4,5},{5,4},{6,7},{7,6},{8,9},{9,8},{10,11... | collective-permute-start | bytes 1671176 | tf_op jit(solution)/shard_map/ppermute | solution.py:868
  214.8 15.9 %collective-permute-start.64 = (bf16[352,256]{1,0:T(8,128)(2,1)}, bf16[352,256]{1,0:T(8,128)(2,1)}, u32[]{:S(2)}, u32[]{:S(2)}) collective-permute-start(bf16[352,256]{1,0:T(8,128)(2,1)} %shard_map.255), channel_id=1, source_target_pairs={{0,12},{1,28},{2,13},{3,29},{4,4},{5,20},{6,5},{7,21},{8,14},{9,30... | collective-permute-start | bytes 540680 | tf_op jit(solution)/shard_map/ppermute | solution.py:990
  (127 other events, 967.0 us)

commit v2 on v1

--- a/solution.py
+++ b/solution.py
@@ -364,7 +364,7 @@
 RING = (0, 2, 4, 6, 7, 5, 3, 1)
 MIB = 2**20
 
-FS, ZS, Y0, Y1, ZH0, ZH1, ZL, ROW0 = 8, 12, 16, 17, 18, 19, 20, 21
+FS, ZS, Y0, Y1, ZH0, ZH1, ZL, ROW0, BLOCK, X0, X1 = 8, 12, 16, 17, 18, 19, 20, 21, 22, 23, 24
 
 
 def dot_nn(left, right):
@@ -530,19 +530,8 @@
     )
 
 
-def quarters(idx, parts):
-    own, near, far, diag, other, last = parts
-    half = far.shape[0]
-    yield own, at(idx[FS], 2 * half)
-    yield near, at(idx[FS + 1], 2 * half)
-    yield far, at(idx[FS + 2] * 2 + idx[Y0], half)
-    yield diag, at(idx[FS + 3] * 2 + idx[Y0], half)
-    yield other, at(idx[FS + 2] * 2 + idx[Y1], half)
-    yield last, at(idx[FS + 3] * 2 + idx[Y1], half)
-
-
 def project_kernel(idx, mixed, tok, *refs):
-    parts, (cot, cot_up, cot_far, gu_c, resid_ref, normed_ref, pack_ref, corner_ref) = refs[:4], refs[4:]
+    parts, (cot_up, cot_far, cot_diag, gu_c, resid_ref, normed_ref, pack_ref) = refs[:4], refs[4:]
     total = tok[...].astype(F32)
     for k, w in enumerate(parts):
         total = total + dot_nn(mixed[:, at(idx[FS + k], w.shape[0])], w[...])
@@ -550,16 +539,15 @@
     normed = (total * fold(total)).astype(BF)
     normed_ref[...] = normed
     rows = normed.shape[0]
-    corner_ref[0:rows, :] = normed
-    corner_ref[rows:, :] = cot[...]
     pack_ref[0:rows, :] = normed
-    pack_ref[rows : 2 * rows, :] = cot_up[...]
-    pack_ref[2 * rows : 3 * rows, :] = cot_far[...]
-    pack_ref[3 * rows :, 0 : gu_c.shape[1]] = gu_c[...]
-    pack_ref[3 * rows :, gu_c.shape[1] :] = jnp.zeros((rows, pack_ref.shape[1] - gu_c.shape[1]), BF)
-
-
-def columns_kernel(idx, gate_ref, up_ref, gain_ref, own_ref, near_ref, far_ref, other_ref, all_ref):
+    for i, ref in enumerate((cot_up, cot_far, cot_diag)):
+        pack_ref[(i + 1) * rows : (i + 2) * rows, :] = ref[...]
+    n = gu_c.shape[0] // 2
+    pack_ref[4 * rows :, 0 : gu_c.shape[1]] = gu_c[n:, :]
+    pack_ref[4 * rows :, gu_c.shape[1] :] = jnp.zeros((n, pack_ref.shape[1] - gu_c.shape[1]), BF)
+
+
+def columns_kernel(idx, gate_ref, up_ref, gain_ref, own_ref, near_ref, pair_ref, all_ref):
     gain = gain_ref[...].astype(F32)
     n, rows, two = all_ref.shape
     cols = gate_ref.shape[1] // n
@@ -568,20 +556,18 @@
         for part, ref in enumerate((gate_ref, up_ref)):
             block = (ref[:, j * cols : (j + 1) * cols].astype(F32) * gain).astype(BF)
             all_ref[j, :, part * (two // 2) : (part + 1) * (two // 2)] = jnp.concatenate([block, gap], axis=1)
-    band = at(idx[Y0], rows // 2)
-    own_ref[...] = all_ref[2 * idx[FS] + idx[ZL]]
-    near_ref[...] = all_ref[2 * idx[FS + 1] + idx[ZL]]
-    far_ref[...] = all_ref[2 * idx[FS + 2] + idx[ZL], band, :]
-    other_ref[...] = all_ref[2 * idx[FS + 3] + idx[ZL], band, :]
-
-
-def assemble_kernel(idx, *refs):
-    parts, (down, gu_ref, dn_ref) = refs[:6], refs[6:]
-    n = gu_ref.shape[1]
-    for i, (w, where) in enumerate(quarters(idx, parts)):
-        gu_ref[where, :] = w[-parts[2].shape[0] :, :n] if i == 3 else w[...]
-    n = down.shape[0] // 2
-    dn_ref[0:n, :] = down[at(idx[ZL], n), :]
+    own_ref[...] = all_ref[idx[BLOCK]]
+    near_ref[...] = all_ref[idx[BLOCK] ^ 4]
+    pair_ref[0:rows, :] = own_ref[...]
+    pair_ref[rows:, :] = near_ref[...]
+
+
+def assemble_kernel(idx, own, near, far, pack, down, gu_ref, dn_ref):
+    part, n = own.shape
+    for k, w in enumerate((own[...], near[...], far[0:part, :], pack[-part:, 0:n])):
+        gu_ref[at(idx[FS + k], part), :] = w
+    n = down.shape[0]
+    dn_ref[0:n, :] = down[...]
     dn_ref[n:, :] = jnp.zeros((dn_ref.shape[0] - n, dn_ref.shape[1]), BF)
 
 
@@ -589,7 +575,7 @@
     return ref[where : where + rows, :]
 
 
-def unit_kernel(places, n0, n1, c0, c1, w_gu, w_dn, hid_ref, both_ref, dkeep, dsend, okeep, osend):
+def unit_kernel(places, n0, n1, c0, c1, w_gu, w_dn, hid_ref, both_ref, dkeep, okeep, send):
     rows = dkeep.shape[0]
     wide = w_dn.shape[0]
     n0, n1, c0, c1 = (rows_of(ref, p, rows) for ref, p in zip((n0, n1, c0, c1), places))
@@ -604,14 +590,14 @@
     both_ref[:, wide:] = (dhid * act).astype(BF)
     dn = contract_cols(both_ref[...], w_gu[...])
     dkeep[...] = dn[:rows]
-    dsend[...] = dn[rows:].astype(BF)
+    send[0:rows, :] = dn[rows:].astype(BF)
     out = dot_nn(hid, w_dn[...])
     okeep[...] = out[:rows]
-    osend[...] = out[rows:].astype(BF)
+    send[rows:, :] = out[rows:].astype(BF)
 
 
 def relative_columns(idx, shard):
-    return [at(2 * idx[yy] + idx[zz], shard) for yy in (Y1, Y0) for zz in (ZH1, ZH0)]
+    return [at(2 * idx[xx] + idx[zz], shard) for xx in (X1, X0) for zz in (ZH1, ZH0)]
 
 
 def grow_kernel(places, idx, hid, both, n0, n1, c0, c1, *refs):
@@ -645,10 +631,10 @@
         two[:, there] = gu[wide : wide + ff8].astype(BF)
 
 
-def middle_kernel(idx, dkeep, near, far, up, diag, resid_ref, cot, *refs):
+def middle_kernel(idx, e_own, far, up, diag, resid_ref, cot, *refs):
     parts, (dresid_ref, dattn_ref, dmixed_ref, sum_ref) = refs[:4], refs[4:]
-    e = dkeep[...]
-    for v in (near, far, up, diag):
+    e = e_own[...]
+    for v in (far, up, diag):
         e = e + v[...].astype(F32)
     resid = resid_ref[...]
     rms = fold(resid)
@@ -744,21 +730,19 @@
                     out[i, 4 * j + kz, HD + n_lat :, :] = sums_ref[:, cols]
 
 
-def outer_query_kernel(idx, na, p0, p1, p2, p3, send, keep, total_ref):
+def outer_query_kernel(idx, na, p0, p1, p2, p3, own, near, far, diag, total_ref):
     rows = p0.shape[0]
     wide = 2 * HD
     total = None
     for k, piece in enumerate((p0, p1, p2, p3)):
-        first = piece.shape[1] - 2 * wide
+        first = p0.shape[1] - 2 * wide
         for j, yy in enumerate((Y0, Y1)):
             right = piece[:, first + j * wide : first + (j + 1) * wide]
             term = contract_rows(na[at(2 * idx[ZS + k] + idx[yy], rows), :], right)
             total = term if total is None else total + term
     total_ref[...] = total.astype(BF)
-    shard = send.shape[1]
-    for out, ks in ((send, (1, 3)), (keep, (0, 2))):
-        for i, k in enumerate(ks):
-            out[i, :, :] = total_ref[at(idx[FS + k], shard), :]
+    for k, out in enumerate((own, near, far, diag)):
+        out[...] = total_ref[at(idx[FS + k], out.shape[0]), :]
 
 
 def tokens_kernel(p0, p1, p2, p3, e_ref, wlt, tok, dresid, out_ref):
@@ -776,23 +760,35 @@
 
 
 def pass_kernel(*refs):
-    n = len(refs) // 2
-    for src, dst in zip(refs[:n], refs[n:]):
-        dst[...] = src[...]
+    pass
+
+
+def half_kernel(both, second):
+    second[...] = both[second.shape[0] :, :]
 
 
 def through(values, deps):
-    return call(pass_kernel, 0, [(v.shape, v.dtype) for v in values])(*values, deps=deps)
-
-
-def pairs_kernel(*refs):
-    n = len(refs) // 3
-    for i in range(n):
-        refs[2 * n + i][...] = wide_sum(refs[2 * i][...], refs[2 * i + 1][...]).astype(BF)
-
-
-def add_pairs(pairs, deps=()):
-    return call(pairs_kernel, 0, [(a.shape, BF) for a, _ in pairs])(*[v for pair in pairs for v in pair], deps=deps)
+    n = len(values)
+    return pl.pallas_call(
+        pass_kernel,
+        in_specs=[pl.BlockSpec(memory_space=pl.ANY)] * (n + len(deps)),
+        out_specs=[pl.BlockSpec(memory_space=pl.ANY)] * n,
+        out_shape=[jax.ShapeDtypeStruct(v.shape, v.dtype) for v in values],
+        input_output_aliases={i: i for i in range(n)},
+        compiler_params=pltpu.CompilerParams(vmem_limit_bytes=MIB),
+    )(*values, *deps)
+
+
+def rows_kernel(*refs):
+    keeps, theres, (e0, e1, e2, e3, o0, o_up, o_x) = refs[0:8], refs[8:12], refs[12:19]
+    rows = e0.shape[0]
+    for i, e in enumerate((e0, e1, e2, e3)):
+        e[...] = wide_sum(keeps[i][...], theres[i][0:rows, :]).astype(e.dtype)
+    sums = [wide_sum(keeps[4 + i][...], theres[i][rows:, :]) for i in range(4)]
+    o0[...] = sums[0]
+    o_up[...] = sums[1]
+    o_x[0:rows, :] = sums[2].astype(BF)
+    o_x[rows:, :] = sums[3].astype(BF)
 
 
 def halves_kernel(*refs):
@@ -810,58 +806,39 @@
     far[...] = wide_sum(keep[1], there[1]).astype(BF)
 
 
-def eleventh_kernel(up_keep, up_there, go_keep, go_there, up_a, go_own, cross):
-    n, shard = up_a.shape
-    total = wide_sum(up_keep[...], up_there[...]).astype(BF)
-    up_a[...] = total[:, shard:]
-    cross[0:n, :] = total[:, :shard]
+def eleventh_kernel(up_keep, up_there, go_keep, go_there, up_b, up_a, go_own, go_far):
+    halves_kernel(up_keep, up_there, up_b, up_a)
     go_own[...] = wide_sum(go_keep[0], go_there[0]).astype(BF)
-    cross[n:, :] = wide_sum(go_keep[1], go_there[1]).astype(BF)
-
-
-def exchange_kernel(keep, there, go_own, cross, b_keep, b_there, p0, p1, p2, p3, go_all, b_own, b_far, up_b):
-    two_kernel(b_keep, b_there, b_own, b_far)
+    go_far[...] = wide_sum(go_keep[1], go_there[1]).astype(BF)
+
+
+def exchange_kernel(keep, there, go_own, go_far, b_keep, b_there, o_up, o_x, p0, p1, p2, p3, b_x, b_xy, y_send, y_keep):
     rows, wide = p0.shape
     n = wide - 4 * HD
     for k, out in enumerate((p0, p1, p2, p3)):
         band = slice(k * rows, (k + 1) * rows)
         out[:, 0:n] = wide_sum(keep[band, 0:n], there[band, 0:n]).astype(BF)
         out[:, n : n + 2 * HD] = keep[band, n:]
-        out[:, n + 2 * HD :] = there[band, n:]
-    n = up_b.shape[0]
-    up_b[...] = cross[0:n, :]
-    go_all[...] = wide_sum(go_own[...], cross[n:, :]).astype(BF)
-
-
-def later_kernel(b_own, b_far, go_all, send, keep):
-    half, tall = b_own.shape[0] // 2, b_own.shape[1]
-    n = go_all.shape[0] // 2
-    for out, h in ((send, 0), (keep, 1)):
-        for i in range(half):
-            out[i * tall : (i + 1) * tall, :] = wide_sum(b_own[h * half + i], b_far[h * half + i]).astype(BF)
-        out[half * tall :, :] = go_all[h * n : (h + 1) * n, :]
-
-
-def quarters_kernel(rows, keep, there, q_keep, q_there, *outs):
-    two_kernel(q_keep, q_there, outs[4], outs[5])
-    tall = outs[0].shape[0] - rows
-    for k in range(4):
-        for lo, n, into in ((k * tall, tall, 0), (4 * tall + k * rows, rows, tall)):
-            outs[k][into : into + n, :] = wide_sum(keep[lo : lo + n, :], there[lo : lo + n, :]).astype(BF)
-
-
-def stack_kernel(*refs):
-    out = refs[-1]
-    rows = refs[0].shape[0]
-    for i, ref in enumerate(refs[:-1]):
-        out[i * rows : (i + 1) * rows, :] = ref[...]
-
-
-def outputs_kernel(k0, k1, k2, k3, there, own, *outs):
-    rows = own.shape[0]
-    own[...] = wide_sum(k0[...], there[0:rows, :])
-    for i, (keep, out) in enumerate(zip((k1, k2, k3), outs)):
-        out[...] = wide_sum(keep[...], there[(i + 1) * rows : (i + 2) * rows, :]).astype(BF)
+        out[:, n + 2 * HD : wide] = there[band, n:]
+    p1[:, wide:] = wide_sum(o_up[...], o_x[rows:, :]).astype(BF)
+    tall = b_keep.shape[2]
+    for j in range(8):
+        band = slice(j % 4 * tall, (j % 4 + 1) * tall)
+        (y_send, y_keep)[j // 4][band, :] = wide_sum(b_keep[0, j], b_there[0, j]).astype(BF)
+        (b_xy, b_x)[j // 4][band, :] = wide_sum(b_keep[1, j], b_there[1, j]).astype(BF)
+    half = go_own.shape[0] // 2
+    for i, out in enumerate((y_send, y_keep)):
+        band = slice(i * half, (i + 1) * half)
+        out[4 * tall :, :] = wide_sum(go_own[band, :], go_far[band, :]).astype(BF)
+
+
+def quarters_kernel(rows, keep, y_there, x_there, xy_there, z0, z1, z2, z3):
+    tall = z0.shape[0] - rows
+    for k, out in enumerate((z0, z1, z2, z3)):
+        band = slice(k * tall, (k + 1) * tall)
+        out[0:tall, :] = (wide_sum(keep[band, :], y_there[band, :]) + wide_sum(x_there[band, :], xy_there[band, :])).astype(BF)
+        band = slice(4 * tall + k * rows, 4 * tall + (k + 1) * rows)
+        out[tall:, :] = wide_sum(keep[band, :], y_there[band, :]).astype(BF)
 
 
 def swap(value, axis):
@@ -873,7 +850,7 @@
 
 
 def corner(value):
-    return lax.ppermute(value, ("x", "z"), [(i, i ^ 5) for i in range(8)])
+    return lax.ppermute(value, ("z", "y"), [(i, i ^ 3) for i in range(8)])
 
 
 def plus(left, right):
@@ -906,7 +883,7 @@
         return (weight.astype(F32) * gain).astype(BF)
 
     owners = [s, owner(place - 1), owner(place + 1), owner(place - 2), owner(place + 2), owner(place - 3), owner(place + 3), owner(place - 4)]
-    idx = jnp.stack(owners + [f, f ^ 1, f ^ 2, f ^ 3, z, z ^ 1, z ^ 2, z ^ 3, y, y ^ 1, zh, zh ^ 1, zl, s * rows]).astype(jnp.int32)
+    idx = jnp.stack(owners + [f, f ^ 1, f ^ 2, f ^ 3, z, z ^ 1, z ^ 2, z ^ 3, y, y ^ 1, zh, zh ^ 1, zl, s * rows, 4 * c + 2 * zl + y, x, x ^ 1]).astype(jnp.int32)
     gain_a = attn_gain.astype(F32)[:, None]
     gain_m = mlp_gain.astype(F32)[:, None]
 
@@ -920,80 +897,84 @@
     wb_own = jnp.concatenate([fold_into(gain_a, w_query), w_key_up, w_value_up], axis=1)
     wb_own, wb_a, wb_b = through((wb_own, wb_own[:, :cut], wb_own[:, cut:]), (a1,))
     wb_near, wb_far = swap(wb_own, "c"), [swap(wb_a, "x")]
-    gu_shapes = [((shard, 2 * wide), BF)] * 2 + [((half, 2 * wide), BF)] * 2
-    gu_own, gu_near, gu_far, gu_other = call(columns_kernel, 1, gu_shapes, [((8, shard, 2 * wide), BF)], limit=16)(
+    gu_own, gu_near, gu_far = call(columns_kernel, 1, [((shard, 2 * wide), BF)] * 2 + [((2 * shard, 2 * wide), BF)], [((8, shard, 2 * wide), BF)], limit=16)(
         idx, w_gate, w_up, mlp_gain[:, None], deps=(a1,)
     )
     gu_near = swap(gu_near, "c")
     a2, b2 = through((a2, b2), (wb_far[0], gu_own))
     a3, b3 = ring(a2, cw), ring(b2, ccw)
-    wb_far.append(swap(through((wb_b,), (a2,))[0], "x"))
-    a3, wo_own = through((a3, w_out), (b3, wb_far[1]))
+    wo_own = through((w_out,), (a2,))[0]
+    wo_far, wo_near = swap(wo_own, "x"), swap(wo_own, "c")
+    a3, wb_b = through((a3, wb_b), (b3, wo_far, gu_near))
     a4 = ring(a3, cw)
-    wo_far, wo_near = swap(wo_own, "x"), swap(wo_own, "c")
-    wb_diag = [swap(v, "c") for v in wb_far]
-
-    a4, gu_far, gu_other, cot = through((a4, gu_far, gu_other, cotangent), (wo_far,))
-    wo_diag = swap(wo_far, "c")
-    gu_far, gu_other = swap(gu_far, "x"), swap(gu_other, "x")
-    cot_far, cot_up, cot_near = swap(cot, "x"), hop(cot, 1), swap(cot, "c")
+    wb_far.append(swap(wb_b, "x"))
+    wb_diag, wo_diag = [swap(v, "c") for v in wb_far], swap(wo_far, "c")
+
+    a4, gu_far, cot, down_rows = through((a4, gu_far, cotangent, lax.dynamic_slice_in_dim(w_down, y * ff8, ff8, 0)), (wb_far[1], wo_diag))
+    gu_far = swap(gu_far, "x")
+    pairs = []
+    for i in range(16):
+        xx, cc, zz = i // 8, i // 4 % 2, i % 4
+        pairs.append(((2 * cc + zz % 2) * 4 + zz - zz % 2 + xx, i))
+    down_rows = lax.ppermute(down_rows, ("x", "c", "z"), pairs)
+    cot_far, cot_up, cot_near, cot_diag = swap(cot, "y"), hop(cot, 1), swap(cot, "c"), corner(cot)
     mixed, probs, outs, qs, queries, na_all, lat_all, w_q, w_key, w_value, w_lat_t = attend(
         idx, lengths, (tokens, a1, b1, a2, b2, a3, b3, a4), (wl_own, wl_near, wl_far, wl_diag), (wb_own, wb_near, *wb_far, *wb_diag)
     )
     w_os = (w_out, wo_near, wo_far, wo_diag)
-    resid, normed, pack, corner_rows = call(
-        project_kernel, 1, [((rows, d), F32), ((rows, d), BF), ((4 * rows, d), BF), ((2 * rows, d), BF)]
-    )(idx, mixed, tokens, *w_os, cot, cot_up, cot_far, gu_other, deps=(gu_far,))
+    resid, normed, pack = call(project_kernel, 1, [((rows, d), F32), ((rows, d), BF), ((4 * rows + shard, d), BF)])(
+        idx, mixed, tokens, *w_os, cot_up, cot_far, cot_diag, gu_far, deps=(down_rows,)
+    )
 
     pack = swap(pack, "c")
-    nm_far, nm_up, diag_rows = swap(normed, "x"), hop(normed, 1), corner(corner_rows)
-    gu_y, gu_yc = through((gu_far, gu_other), (normed,))
-    gu_y = swap(gu_y, "y")
-    gu_yc = lax.ppermute(gu_yc, ("c", "y"), [(i, i ^ 3) for i in range(4)])
-    nm_up2, nm_far2, diag_rows2 = swap(nm_up, "c"), swap(nm_far, "c"), swap(diag_rows, "c")
+    nm_far, nm_up, nm_diag = swap(normed, "y"), hop(normed, 1), corner(normed)
+    nm_up2, nm_far2, nm_diag2 = swap(nm_up, "c"), swap(nm_far, "c"), swap(nm_diag, "c")
     w_gu, w_dn = call(assemble_kernel, 1, [((d, 2 * wide), BF), ((wide, d), BF)])(
-        idx, gu_own, gu_near, gu_far, pack, gu_y, gu_yc, w_down, deps=(nm_far, nm_up, diag_rows)
+        idx, gu_own, gu_near, gu_far, pack, down_rows, deps=(nm_far, nm_up, nm_diag)
     )
 
     def unit(places, *args, deps=()):
-        shapes = [((2 * rows, wide), BF), ((2 * rows, 2 * wide), BF), ((rows, d), F32), ((rows, d), BF), ((rows, d), F32), ((rows, d), BF)]
+        shapes = [((2 * rows, wide), BF), ((2 * rows, 2 * wide), BF), ((rows, d), F32), ((rows, d), F32), ((2 * rows, d), BF)]
         return call(functools.partial(unit_kernel, places), 0, shapes)(*args, w_gu, w_dn, deps=deps)
 
     def grow(places, *args, deps=()):
         return call(functools.partial(grow_kernel, places), 1, [((wide, d), F32), ((2 * wide, d), F32)], limit=12)(idx, *args, deps=deps)
 
-    at_own, at_up, at_far, at_diag = (0, 0, 0, 0), (0, 0, 0, rows), (0, 0, 0, 2 * rows), (0, 0, rows, rows)
+    at_own, at_up, at_far, at_diag = (0, 0, 0, 0), (0, 0, 0, rows), (0, 0, 0, 2 * rows), (0, 0, 0, 3 * rows)
     own_rows, up_rows, far_rows = (normed, pack, cot, cot_near), (nm_up, nm_up2, cot_up, pack), (nm_far, nm_far2, cot_far, pack)
-    diag_rows = (diag_rows, diag_rows2, diag_rows, diag_rows2)
+    diag_rows = (nm_diag, nm_diag2, cot_diag, pack)
     own = unit(at_own, *own_rows)
     sums = grow(at_own, *own[:2], *own_rows)
     up = unit(at_up, *up_rows, deps=(sums[0],))
     far = unit(at_far, *far_rows, deps=(up[0],))
     diag = unit(at_diag, *diag_rows, deps=(far[0],))
-    d_near2, d_up2, d_far2, d_diag2 = (swap(v[3], "c") for v in (own, up, far, diag))
-    early = add_pairs([(up[2], d_up2), (far[2], d_far2), (diag[2], d_diag2)], deps=(d_near2,))
-    d_up, d_far, d_diag = hop(early[0], 1), swap(early[1], "x"), corner(early[2])
+    near2, up2, far2, diag2 = (swap(v[4], "c") for v in (own, up, far, diag))
+    units = (own, up, far, diag)
+    shapes = [((rows, d), F32)] + [((rows, d), BF)] * 3 + [((rows, d), F32)] * 2 + [((2 * rows, d), BF)]
+    e_own, *early, o_own, o_up, o_x = call(rows_kernel, 0, shapes)(*[v[2] for v in units], *[v[3] for v in units], near2, up2, far2, diag2)
+    d_up, d_far, d_diag = hop(early[0], 1), swap(early[1], "y"), corner(early[2])
     sums = grow(at_up, *up[:2], *up_rows, *sums, deps=early)
     sums = grow(at_far, *far[:2], *far_rows, *sums)
     shapes = [((2 * ff8, 2 * shard), BF)] * 2 + [((ff8, 2 * shard), BF)] * 2
     y1_send, y1_keep, y2_send, y2_keep = call(functools.partial(last_kernel, ff8, at_diag), 1, shapes)(idx, *diag[:2], *diag_rows, *sums)
-    y1_there = swap(y1_send, "y")
+    y1_there = swap(y1_send, "x")
     dresid, dattn, dmixed, v_m = call(middle_kernel, 1, [((rows, d), F32), ((rows, d), BF), ((rows, QW), BF), ((8, d), F32)])(
-        idx, own[2], d_near2, d_far, d_up, d_diag, resid, cotangent, *w_os, deps=(y1_there,)
-    )
-
-    def home(value, flip, m):
+        idx, e_own, d_far, d_up, d_diag, resid, cotangent, *w_os, deps=(y1_there,)
+    )
+
+    def home(value, m):
         pairs = []
-        for i in range(32):
-            xx, cc, zz, yy = i // 16, i // 8 % 2, i // 2 % 4, i % 2
-            pairs.append((i, ((yy * 2 + (zz // 2 ^ m)) * 4 + 2 * (xx ^ flip) + cc) * 2 + zz % 2))
-        return lax.ppermute(value, ("x", "c", "z", "y"), pairs)
+        for i in range(8):
+            cc, hh, ll = i // 4, i // 2 % 2, i % 2
+            pairs.append((i, (hh ^ m) * 4 + 2 * cc + ll))
+        return lax.ppermute(value, ("c", "z"), pairs)
 
     go_send, go_keep = call(outer_out_kernel, 1, [((2, QW, shard), BF)] * 2)(idx, mixed, dattn)
     go_there = swap(go_send, "c")
     f1_b, f1_a = call(halves_kernel, 0, [((2 * ff8, shard), BF)] * 2)(y1_keep, y1_there, deps=(go_send,))
-    f1_a, f1_b = home(f1_a, 0, 0), swap(f1_b, "x")
-    y2_there = swap(through((y2_send,), (go_send,))[0], "y")
+    f1_a, f1_b = home(f1_a, 0), home(f1_b, 1)
+    o_x = swap(through((o_x,), (go_send,))[0], "y")
+    y2_there = swap(through((y2_send,), (go_send,))[0], "x")
     dlat, p_send, p_keep, dq, ups = call(
         attend_back_kernel,
         1,
@@ -1011,42 +992,37 @@
         limit=24,
         far_in=(1, 2, 4),
     )(idx, dlat, na_all, w_lat_t, dq, w_q, ups, v_m)
-    f2_a, go_own, cross = call(eleventh_kernel, 0, [((ff8, shard), BF), ((QW, shard), BF), ((ff8 + QW, shard), BF)])(
-        y2_keep, y2_there, go_keep, go_there, deps=(b_send, f1_a)
-    )
-    f1_b, b_send, p_send = through((f1_b, b_send, p_send), (cross,))
+    f2_b, f2_a, go_own, go_far = call(eleventh_kernel, 0, [((ff8, shard), BF)] * 2 + [((QW, shard), BF)] * 2)(
+        y2_keep, y2_there, go_keep, go_there, deps=(b_send, f1_a, f1_b, o_x)
+    )
+    b_send, p_send = through((b_send, p_send), (go_far,))
     p_there = swap(p_send, "y")
-    f2_a, f1_b2 = home(f2_a, 0, 0), home(f1_b, 1, 1)
-    cross, b_there = swap(cross, "x"), swap(b_send, "c")
-    shapes = [((rows, n_lat + 4 * HD), BF)] * 4 + [((QW, shard), BF)] + [((8, tall, shard), BF)] * 2 + [((ff8, shard), BF)]
-    p0, p1, p2, p3, go_all, b_own, b_sum, f2_b = call(exchange_kernel, 0, shapes)(
-        p_keep, p_there, go_own, cross, b_keep, b_there, deps=(f2_a, f1_b2)
+    f2_a, f2_b = home(f2_a, 0), home(f2_b, 1)
+    go_far, b_there = swap(go_far, "x"), swap(b_send, "c")
+    flat = ((4 * tall, shard), BF)
+    tower = ((4 * tall + QW // 2, shard), BF)
+    n_p = n_lat + 4 * HD
+    shapes = [((rows, n), BF) for n in (n_p, n_p + d, n_p, n_p)] + [flat, flat, tower, tower]
+    p0, p1, p2, p3, b_x, b_xy, y_send, y_keep = call(exchange_kernel, 0, shapes)(
+        p_keep, p_there, go_own, go_far, b_keep, b_there, o_up, o_x, deps=(f2_a, f2_b)
     )
     pieces = (p0, hop(p1, 1), hop(p2, 2), hop(p3, 3))
-    b_far = swap(b_sum, "x")
-    o_there = swap(call(stack_kernel, 0, [((4 * rows, d), BF)])(*[v[5] for v in (own, up, far, diag)], deps=(b_sum,))[0], "c")
-    flat = ((4 * (tall + rows), shard), BF)
-    yz_send, yz_keep = call(later_kernel, 0, [flat] * 2)(b_own, b_far, go_all, deps=pieces[1:])
-    gq_send, gq_keep = call(outer_query_kernel, 1, [((2, shard, 2 * HD), BF)] * 2, [((d, 2 * HD), BF)], far_in=(0,))(idx, na_all, *pieces, deps=(yz_send,))
-    o_own, o_up, o_far, o_diag = call(outputs_kernel, 0, [((rows, d), F32)] + [((rows, d), BF)] * 3)(
-        *[v[4] for v in (own, up, far, diag)], o_there, deps=(yz_send,)
-    )
-    f2_b2 = home(through((f2_b,), (yz_send,))[0], 1, 1)
-    yz_there, gq_there = swap(yz_send, "y"), swap(gq_send, "c")
-    o_up, o_far, o_diag = hop(o_up, 1), swap(o_far, "x"), corner(o_diag)
-    tokens_grad = call(tokens_kernel, 0, [((rows, d), BF)])(*pieces, e_q, w_lat_t, tokens, dresid, deps=(o_own,))[0]
-    shapes = [((tall + rows, shard), BF)] * 4 + [((shard, 2 * HD), BF)] * 2
-    z0, z1, z2, z3, gq_own, gq_sum = call(functools.partial(quarters_kernel, rows), 0, shapes)(
-        yz_keep, yz_there, gq_keep, gq_there, deps=(tokens_grad, o_up, o_far, o_diag)
+    b_x, y_there = swap(b_x, "x"), swap(y_send, "y")
+    b_xy = lax.ppermute(b_xy, ("x", "y"), [(i, i ^ 3) for i in range(4)])
+    z0, z1, z2, z3 = call(functools.partial(quarters_kernel, rows), 0, [((tall + rows, shard), BF)] * 4)(
+        y_keep, y_there, b_x, b_xy, deps=pieces[1:]
     )
     last = z0.astype(F32) + hop(z1, 1) + hop(z2, 2) + hop(z3, 3)
-    gq_far = swap(gq_sum, "x")
-
-    grad_query = plus(gq_own, gq_far) * gain_a
-    output = (resid + o_own + o_up + o_far + o_diag).astype(BF)
-    grad_down = plus(f1_a[:ff8], f1_b2[:ff8])
-    grad_gate = plus(f1_a[ff8:], f1_b2[ff8:]).T * gain_m
-    grad_up = plus(f2_a, f2_b2).T * gain_m
+    gq, gq_near, gq_far, gq_diag = call(outer_query_kernel, 1, [((shard, 2 * HD), BF)] * 4, [((d, 2 * HD), BF)], far_in=(0,))(
+        idx, na_all, *pieces, deps=(z0,)
+    )
+    gq_near, gq_far, gq_diag = swap(gq_near, "c"), swap(gq_far, "x"), lax.ppermute(gq_diag, ("x", "c"), [(i, i ^ 3) for i in range(4)])
+    tokens_grad = call(tokens_kernel, 0, [((rows, d), BF)])(*pieces, e_q, w_lat_t, tokens, dresid, deps=(gq,))[0]
+    grad_query = (plus(gq, gq_near) + plus(gq_far, gq_diag)) * gain_a
+    output = (resid + o_own + o_x[:rows] + pieces[1][:, n_p:]).astype(BF)
+    grad_down = plus(f1_a[:ff8], f1_b[:ff8])
+    grad_gate = plus(f1_a[ff8:], f1_b[ff8:]).T * gain_m
+    grad_up = plus(f2_a, f2_b).T * gain_m
     grad_out = last[tall:]
     eighth = HD // 2
     n_small = n_lat // 8

time: 267 us -> 236 us (0.88)
  starting transfers between devices: 81.1 us -> 59 us
  waiting for transfers between devices: 97.9 us -> 87.7 us
    ppermute x40 -> x36, starting transfers between devices: 40.4 us -> 20.7 us  [swap(): return lax.ppermute(value, axis, [(0, 1), (1, 0)])]
    ppermute x8 -> x10, waiting for transfers between devices: 39.3 us -> 21.4 us  [the longest x4 15 us: home(): return lax.ppermute(value, ('c', 'z'), pairs)]
    ppermute x40 -> x36, waiting for transfers between devices: 23.4 us -> 33 us  [swap(): return lax.ppermute(value, axis, [(0, 1), (1, 0)])]
    ppermute x7, waiting for transfers between devices: 13 us -> 7.19 us  [ring(): return lax.ppermute(value, ('z', 'y'), pairs)]
    ppermute x10 -> x9, waiting for transfers between devices: 22.3 us -> 26.1 us  [hop(): return lax.ppermute(value, 'z', [(i, i ^ k) for i in range(4)])]
    pallas_call x36 -> x23, Pallas kernels: 59.7 us -> 57.7 us  [run(): pl.pallas_call(body, in_specs=[pl.BlockSpec(memory_space=pltpu.SMEM)] * n...]
    ppermute x8 -> x10, starting transfers between devices: 17.2 us -> 15.6 us  [the longest x4 7.1 us: home(): return lax.ppermute(value, ('c', 'z'), pairs)]
    unnamed x172 -> x128, local copies, waits for them, and re-layouts: 12.8 us -> 11.8 us
  transfers between devices with their start and end apart: 65 -> 62, of which waited for: 24 -> 22; matrix products, arithmetic and copies ran while one was open for 3% -> 5% of each run, Pallas kernels for 18% -> 18%
where the time goes in v2:
time: 236 us; the launch traced here: 232 us
  waiting for transfers between devices  87.7 us (37%)
  starting transfers between devices  59 us (25%)
  Pallas kernels  57.7 us (24%)
  local copies, waits for them, and re-layouts  16.5 us (7%)
  other arithmetic  8.88 us (4%)
    pallas_call x23, Pallas kernels, run(): pl.pallas_call(body, in_specs=[pl.BlockSpec(memory_space=pltpu.SMEM)] * n...  57.7 us
    ppermute x36, waiting for transfers between devices, swap(): return lax.ppermute(value, axis, [(0, 1), (1, 0)])  33 us
    ppermute x9, waiting for transfers between devices, hop(): return lax.ppermute(value, 'z', [(i, i ^ k) for i in range(4)])  26.1 us
    ppermute x36, starting transfers between devices, swap(): return lax.ppermute(value, axis, [(0, 1), (1, 0)])  20.7 us
    ppermute x4, waiting for transfers between devices, home(): return lax.ppermute(value, ('c', 'z'), pairs)  15 us
    ppermute x9, starting transfers between devices, hop(): return lax.ppermute(value, 'z', [(i, i ^ k) for i in range(4)])  13.9 us
    unnamed x128, local copies, waits for them, and re-layouts  11.8 us
    ppermute x7, starting transfers between devices, ring(): return lax.ppermute(value, ('z', 'y'), pairs)  8.77 us
  transfers between devices with their start and end apart: 62, of which 22 were waited for; matrix products, arithmetic and copies ran while one was open for 5% of the time, Pallas kernels for 18%

profile of v2, /device:TPU:0, one launch (start us, length us, event | category | flops | bytes accessed | tf_op | source)
XLA Modules:
  0.0 231.7 jit_solution(7212676497909278440)
XLA Ops:
  0.7 3.1 %collective-permute-start = (bf16[128,1024]{1,0:T(8,128)(2,1)}, bf16[128,1024]{1,0:T(8,128)(2,1)S(1)}, u32[]{:S(2)}, u32[]{:S(2)}) collective-permute-start(bf16[128,1024]{1,0:T(8,128)(2,1)} %refs_6_.3), channel_id=1, source_target_pairs={{0,2},{2,4},{4,6},{6,7},{7,5},{5,3},{3,1},{1,0},{8,10},{10,12},{12... | collective-permute-start | bytes 786440 | tf_op jit(solution)/shard_map/ppermute | solution.py:880
  11.8 2.4 %collective-permute-done.2.refs_2_.refs_12_ = bf16[256,512]{1,0:T(8,128)(2,1)} collective-permute-done((bf16[256,512]{1,0:T(8,128)(2,1)}, bf16[256,512]{1,0:T(8,128)(2,1)}, u32[]{:S(2)}, u32[]{:S(2)}) %collective-permute-start.2) | collective-permute-done | bytes 262176 | tf_op jit(solution)/shard_map/ppermute | solution.py:845
  23.2 2.7 %shard_map.222 = (bf16[256,768]{1,0:T(8,128)(2,1)S(1)}, bf16[256,768]{1,0:T(8,128)(2,1)S(1)}, bf16[512,768]{1,0:T(8,128)(2,1)}) custom-call(s32[25]{0:T(128)S(1)} %stack.103.refs_0_, bf16[256,2816]{1,0:T(8,128)(2,1)S(1)} %copy-done.24, bf16[256,2816]{1,0:T(8,128)(2,1)S(1)} %copy-done.25, bf16[256,1]{1,0:T(8,128)(2,1)S(1)} %copy-done.54, ...), custom_call_target="tpu_custom_call" | custom-call | flops 1 | tf_op jit(solution)/shard_map/pallas_call | solution.py:442
  29.2 8.9 %collective-permute-done.8.refs_3_.refs_5_.refs_9_ = bf16[256,1024]{1,0:T(8,128)(2,1)S(1)} collective-permute-done((bf16[256,1024]{1,0:T(8,128)(2,1)S(1)}, bf16[256,1024]{1,0:T(8,128)(2,1)S(1)}, u32[]{:S(2)}, u32[]{:S(2)}) %collective-permute-start.8) | collective-permute-done | bytes 524320 | tf_op jit(solution)/shard_map/ppermute | solution.py:845
  40.7 6.3 %collective-permute-done.10.refs_0_ = bf16[128,1024]{1,0:T(8,128)(2,1)S(1)} collective-permute-done((bf16[128,1024]{1,0:T(8,128)(2,1)S(1)}, bf16[128,1024]{1,0:T(8,128)(2,1)S(1)}, u32[]{:S(2)}, u32[]{:S(2)}) %collective-permute-start.10) | collective-permute-done | bytes 262176 | tf_op jit(solution)/shard_map/ppermute | solution.py:880
  48.6 2.7 %collective-permute-done.11.refs_4_.refs_17_ = bf16[256,768]{1,0:T(8,128)(2,1)} collective-permute-done((bf16[256,768]{1,0:T(8,128)(2,1)}, bf16[256,768]{1,0:T(8,128)(2,1)}, u32[]{:S(2)}, u32[]{:S(2)}) %collective-permute-start.11) | collective-permute-done | bytes 393248 | tf_op jit(solution)/shard_map/ppermute | solution.py:845
  62.8 14.4 %shard_map.227 = (bf16[128,1024]{1,0:T(8,128)(2,1)}, bf16[2048,1024]{1,0:T(8,128)(2,1)}, bf16[2048,256]{1,0:T(8,128)(2,1)}, bf16[2048,256]{1,0:T(8,128)(2,1)}, b...) custom-call(s32[25]{0:T(128)} %copy-done.55, ...), custom_call_target="tpu_custom_call" | custom-call | flops 1 | tf_op jit(solution)/shard_map/pallas_call | solution.py:442
  87.1 5.6 %collective-permute-done.27.refs_7_.refs_0_.refs_3_ = bf16[128,1024]{1,0:T(8,128)(2,1)S(1)} collective-permute-done((bf16[128,1024]{1,0:T(8,128)(2,1)S(1)}, bf16[128,1024]{1,0:T(8,128)(2,1)S(1)}, u32[]{:S(2)}, u32[]{:S(2)}) %collective-permute-start.27) | collective-permute-done | bytes 262176 | tf_op jit(solution)/shard_map/ppermute | solution.py:849
  92.7 6.7 %collective-permute-done.26.refs_6_.refs_0_.refs_3_ = bf16[128,1024]{1,0:T(8,128)(2,1)S(1)} collective-permute-done((bf16[128,1024]{1,0:T(8,128)(2,1)S(1)}, bf16[128,1024]{1,0:T(8,128)(2,1)S(1)}, u32[]{:S(2)}, u32[]{:S(2)}) %collective-permute-start.26) | collective-permute-done | bytes 262176 | tf_op jit(solution)/shard_map/ppermute | solution.py:845
  122.6 4.8 %collective-permute-done.36.refs_2_ = bf16[128,1024]{1,0:T(8,128)(2,1)S(1)} collective-permute-done((bf16[128,1024]{1,0:T(8,128)(2,1)S(1)}, bf16[128,1024]{1,0:T(8,128)(2,1)S(1)}, u32[]{:S(2)}, u32[]{:S(2)}) %collective-permute-start.36) | collective-permute-done | bytes 262176 | tf_op jit(solution)/shard_map/ppermute | solution.py:845
  128.7 5.5 %collective-permute-done.38.refs_4_ = bf16[128,1024]{1,0:T(8,128)(2,1)S(1)} collective-permute-done((bf16[128,1024]{1,0:T(8,128)(2,1)S(1)}, bf16[128,1024]{1,0:T(8,128)(2,1)S(1)}, u32[]{:S(2)}, u32[]{:S(2)}) %collective-permute-start.38) | collective-permute-done | bytes 262176 | tf_op jit(solution)/shard_map/ppermute | solution.py:853
  134.2 2.7 %collective-permute-done.39.refs_11_.refs_9_.refs_1_ = bf16[704,512]{1,0:T(8,128)(2,1)S(1)} collective-permute-done((bf16[704,512]{1,0:T(8,128)(2,1)S(1)}, bf16[704,512]{1,0:T(8,128)(2,1)S(1)}, u32[]{:S(2)}, u32[]{:S(2)}) %collective-permute-start.39) | collective-permute-done | bytes 720928 | tf_op jit(solution)/shard_map/ppermute | solution.py:845
  137.0 2.3 shard_map.239
  144.4 3.2 %collective-permute-start.44 = (bf16[704,256]{1,0:T(8,128)(2,1)S(1)}, bf16[704,256]{1,0:T(8,128)(2,1)S(1)}, u32[]{:S(2)}, u32[]{:S(2)}) collective-permute-start(bf16[704,256]{1,0:T(8,128)(2,1)S(1)} %get-tuple-element.199), channel_id=1, source_target_pairs={{0,8},{2,10},{4,0},{6,2},{8,12},{10,14},{12,4},{14,6},{1,9},{3,11}... | collective-permute-start | bytes 1081352 | tf_op jit(solution)/shard_map/ppermute | solution.py:970
  147.7 8.9 %shard_map.242 = (bf16[1024,512]{1,0:T(8,128)(2,1)S(1)}, bf16[512,640]{1,0:T(8,128)(2,1)S(1)}, bf16[512,640]{1,0:T(8,128)(2,1)S(1)}, bf16[128,1024]{1,0:T(8,128)(2,1)S(1)}, bf16[4,8,64,256]{3,2,1,0:T(8,128)(2,1)S(1)}) custom-call(s32[25]{0:T(128)S(1)} %copy-done.56, bf16[128,1024]{1,0:T(8,128)(2,1)S(1)} %get-tuple-element.176.refs_1_, ...), custom_call_target="tpu_custom_call" | custom-call | flops 1 | tf_op jit(solution)/shard_map/pallas_call | solution.py:442
  156.6 3.6 %shard_map.243 = (f32[128,1024]{1,0:T(8,128)S(1)}, bf16[2,8,144,256]{3,2,1,0:T(8,128)(2,1)S(1)}, bf16[2,8,144,256]{3,2,1,0:T(8,128)(2,1)S(1)}) custom-call(s32[25]{0:T(128)S(1)} %copy-done.56, bf16[1024,512]{1,0:T(8,128)(2,1)S(1)} %get-tuple-element.185.refs_1_, bf16[1024,1024]{1,0:T(8,128)(2,1)S(1)} %copy-done.3, bf16[512,1024]{1,0:T(8,128)(2,1)S(1)} %copy-done.6, ...), custom_call_target="tpu_custom_call" | custom-call | flops 1 | tf_op jit(solution)/shard_map/pallas_call | solution.py:442
  160.3 4.1 %collective-permute-done.44.refs_6_ = bf16[704,256]{1,0:T(8,128)(2,1)S(1)} collective-permute-done((bf16[704,256]{1,0:T(8,128)(2,1)S(1)}, bf16[704,256]{1,0:T(8,128)(2,1)S(1)}, u32[]{:S(2)}, u32[]{:S(2)}) %collective-permute-start.44) | collective-permute-done | bytes 360480 | tf_op jit(solution)/shard_map/ppermute | solution.py:970
  170.9 10.9 %collective-permute-done.49.refs_9_ = bf16[352,256]{1,0:T(8,128)(2,1)S(1)} collective-permute-done((bf16[352,256]{1,0:T(8,128)(2,1)S(1)}, bf16[352,256]{1,0:T(8,128)(2,1)S(1)}, u32[]{:S(2)}, u32[]{:S(2)}) %collective-permute-start.49) | collective-permute-done | bytes 180256 | tf_op jit(solution)/shard_map/ppermute | solution.py:970
  192.5 5.5 %collective-permute-done.51.refs_5_.refs_4_.refs_2_ = bf16[128,768]{1,0:T(8,128)(2,1)S(1)} collective-permute-done((bf16[128,768]{1,0:T(8,128)(2,1)}, bf16[128,768]{1,0:T(8,128)(2,1)S(1)}, u32[]{:S(2)}, u32[]{:S(2)}) %collective-permute-start.51) | collective-permute-done | bytes 196640 | tf_op jit(solution)/shard_map/ppermute | solution.py:849
  198.0 2.5 %collective-permute-start.52 = (bf16[128,768]{1,0:T(8,128)(2,1)}, bf16[128,768]{1,0:T(8,128)(2,1)S(1)}, u32[]{:S(2)}, u32[]{:S(2)}) collective-permute-start(bf16[128,768]{1,0:T(8,128)(2,1)} %copy-done.57), channel_id=1, source_target_pairs={{0,6},{2,4},{4,2},{6,0},{1,7},{3,5},{5,3},{7,1},{8,14},{10,12},{12... | collective-permute-start | bytes 589832 | tf_op jit(solution)/shard_map/ppermute | solution.py:849
  200.5 2.3 %convert_add_fusion = (f32[352,256]{1,0:T(8,128)}, f32[256,352]{0,1:T(8,128)}, f32[256,352]{0,1:T(8,128)}) fusion(bf16[704,256]{1,0:T(8,128)(2,1)} %copy-done.27, bf16[704,256]{1,0:T(8,128)(2,1)} %copy-done.26, f32[256]{0:T(256)S(1)} %convert_element_type.85, bf16[352,256]{1,0:T(8,128)(2,1)} %copy-done.42, bf16[352,256]{1,0:T(8,128)(2,1)} %copy-done.41), kind=kLoop, calls=%fused_computation.4 | loop fusion | flops 991232 | bytes 2163712 | tf_op jit(solution)/shard_map/add | solution.py:857
  202.8 5.0 %collective-permute-done.52.refs_6_.refs_5_.refs_3_ = bf16[128,768]{1,0:T(8,128)(2,1)S(1)} collective-permute-done((bf16[128,768]{1,0:T(8,128)(2,1)}, bf16[128,768]{1,0:T(8,128)(2,1)S(1)}, u32[]{:S(2)}, u32[]{:S(2)}) %collective-permute-start.52) | collective-permute-done | bytes 196640 | tf_op jit(solution)/shard_map/ppermute | solution.py:849
  213.9 2.3 %collective-permute-start.58 = (bf16[272,256]{1,0:T(8,128)(2,1)S(1)}, bf16[272,256]{1,0:T(8,128)(2,1)S(1)}, u32[]{:S(2)}, u32[]{:S(2)}) collective-permute-start(bf16[272,256]{1,0:T(8,128)(2,1)S(1)} %get-tuple-element.222), channel_id=1, source_target_pairs={{0,6},{2,4},{4,2},{6,0},{1,7},{3,5},{5,3},{7,1},{8,14},{10,12},{12... | collective-permute-start | bytes 417800 | tf_op jit(solution)/shard_map/ppermute | solution.py:849
  222.4 6.4 %collective-permute-done.57 = bf16[272,256]{1,0:T(8,128)(2,1)S(1)} collective-permute-done((bf16[272,256]{1,0:T(8,128)(2,1)S(1)}, bf16[272,256]{1,0:T(8,128)(2,1)S(1)}, u32[]{:S(2)}, u32[]{:S(2)}) %collective-permute-start.57) | collective-permute-done | bytes 139296 | tf_op jit(solution)/shard_map/ppermute | solution.py:849
  (279 shorter events, 106.8 us)
Async XLA Ops:
  29.2 27.7 %collective-permute-start.15 = (bf16[256,1536]{1,0:T(8,128)(2,1)S(1)}, bf16[256,1536]{1,0:T(8,128)(2,1)}, u32[]{:S(2)}, u32[]{:S(2)}) collective-permute-start(bf16[256,1536]{1,0:T(8,128)(2,1)S(1)} %get-tuple-element.131.refs_14_), channel_id=1, source_target_pairs={{0,8},{8,0},{1,9},{9,1},{2,10},{10,2},{3,11},{11,3},{4,12},{12,4},... | collective-permute-start | bytes 2359304 | tf_op jit(solution)/shard_map/ppermute | solution.py:845
  52.1 26.0 %collective-permute-start.22 = (bf16[512,768]{1,0:T(8,128)(2,1)}, bf16[512,768]{1,0:T(8,128)(2,1)S(1)}, u32[]{:S(2)}, u32[]{:S(2)}) collective-permute-start(bf16[512,768]{1,0:T(8,128)(2,1)} %get-tuple-element.134), channel_id=1, source_target_pairs={{0,16},{16,0},{1,17},{17,1},{2,18},{18,2},{3,19},{19,3},{4,20},{20... | collective-permute-start | bytes 2359304 | tf_op jit(solution)/shard_map/ppermute | solution.py:845
  52.6 25.5 %collective-permute-start.23 = (bf16[352,1024]{1,0:T(8,128)(2,1)}, bf16[352,1024]{1,0:T(8,128)(2,1)S(1)}, u32[]{:S(2)}, u32[]{:S(2)}) collective-permute-start(bf16[352,1024]{1,0:T(8,128)(2,1)} %get-tuple-element.135), channel_id=1, source_target_pairs={{0,0},{8,2},{4,4},{12,6},{16,8},{24,10},{20,12},{28,14},{2,16},{10... | collective-permute-start | bytes 2162696 | tf_op jit(solution)/shard_map/ppermute | solution.py:919
  58.4 18.8 %collective-permute-start.19 = (bf16[128,1024]{1,0:T(8,128)(2,1)S(1)}, bf16[128,1024]{1,0:T(8,128)(2,1)S(1)}, u32[]{:S(2)}, u32[]{:S(2)}) collective-permute-start(bf16[128,1024]{1,0:T(8,128)(2,1)S(1)} %get-tuple-element.133.refs_2_.refs_5_), channel_id=1, source_target_pairs={{0,2},{2,0},{4,6},{6,4},{1,3},{3,1},{5,7},{7,5},{8,10},{10,8},{12,... | collective-permute-start | bytes 786440 | tf_op jit(solution)/shard_map/ppermute | solution.py:849
  60.8 16.4 %collective-permute-start.20 = (bf16[128,1024]{1,0:T(8,128)(2,1)S(1)}, bf16[128,1024]{1,0:T(8,128)(2,1)S(1)}, u32[]{:S(2)}, u32[]{:S(2)}) collective-permute-start(bf16[128,1024]{1,0:T(8,128)(2,1)S(1)} %get-tuple-element.133.refs_2_.refs_5_), channel_id=1, source_target_pairs={{0,1},{1,0},{2,3},{3,2},{4,5},{5,4},{6,7},{7,6},{8,9},{9,8},{10,11... | collective-permute-start | bytes 786440 | tf_op jit(solution)/shard_map/ppermute | solution.py:845
  61.3 16.8 %collective-permute-start.21 = (bf16[128,1024]{1,0:T(8,128)(2,1)S(1)}, bf16[128,1024]{1,0:T(8,128)(2,1)S(1)}, u32[]{:S(2)}, u32[]{:S(2)}) collective-permute-start(bf16[128,1024]{1,0:T(8,128)(2,1)S(1)} %get-tuple-element.133.refs_2_.refs_5_), channel_id=1, source_target_pairs={{0,3},{1,2},{2,1},{3,0},{4,7},{5,6},{6,5},{7,4},{8,11},{9,10},{10,... | collective-permute-start | bytes 786440 | tf_op jit(solution)/shard_map/ppermute | solution.py:853
  81.9 18.1 %collective-permute-start.24 = (bf16[768,1024]{1,0:T(8,128)(2,1)S(1)}, bf16[768,1024]{1,0:T(8,128)(2,1)S(1)}, u32[]{:S(2)}, u32[]{:S(2)}) collective-permute-start(bf16[768,1024]{1,0:T(8,128)(2,1)S(1)} %get-tuple-element.138), channel_id=1, source_target_pairs={{0,8},{8,0},{1,9},{9,1},{2,10},{10,2},{3,11},{11,3},{4,12},{12,4},... | collective-permute-start | bytes 4718600 | tf_op jit(solution)/shard_map/ppermute | solution.py:845
  85.4 14.0 %collective-permute-start.26 = (bf16[128,1024]{1,0:T(8,128)(2,1)S(1)}, bf16[128,1024]{1,0:T(8,128)(2,1)S(1)}, u32[]{:S(2)}, u32[]{:S(2)}) collective-permute-start(bf16[128,1024]{1,0:T(8,128)(2,1)S(1)} %get-tuple-element.137.refs_0_.refs_3_), channel_id=1, source_target_pairs={{0,1},{1,0},{2,3},{3,2},{4,5},{5,4},{6,7},{7,6},{8,9},{9,8},{10,11... | collective-permute-start | bytes 786440 | tf_op jit(solution)/shard_map/ppermute | solution.py:845
  85.8 13.6 %collective-permute-start.28 = (bf16[128,1024]{1,0:T(8,128)(2,1)S(1)}, bf16[128,1024]{1,0:T(8,128)(2,1)S(1)}, u32[]{:S(2)}, u32[]{:S(2)}) collective-permute-start(bf16[128,1024]{1,0:T(8,128)(2,1)S(1)} %get-tuple-element.137.refs_0_.refs_3_), channel_id=1, source_target_pairs={{0,3},{1,2},{2,1},{3,0},{4,7},{5,6},{6,5},{7,4},{8,11},{9,10},{10,... | collective-permute-start | bytes 786440 | tf_op jit(solution)/shard_map/ppermute | solution.py:853
  87.1 13.6 %collective-permute-start.25 = (bf16[128,1024]{1,0:T(8,128)(2,1)S(1)}, bf16[128,1024]{1,0:T(8,128)(2,1)S(1)}, u32[]{:S(2)}, u32[]{:S(2)}) collective-permute-start(bf16[128,1024]{1,0:T(8,128)(2,1)S(1)} %get-tuple-element.133.refs_2_.refs_5_), channel_id=1, source_target_pairs={{0,8},{8,0},{1,9},{9,1},{2,10},{10,2},{3,11},{11,3},{4,12},{12,4},... | collective-permute-start | bytes 786440 | tf_op jit(solution)/shard_map/ppermute | solution.py:845
  118.4 18.5 %collective-permute-start.39 = (bf16[704,512]{1,0:T(8,128)(2,1)S(1)}, bf16[704,512]{1,0:T(8,128)(2,1)S(1)}, u32[]{:S(2)}, u32[]{:S(2)}) collective-permute-start(bf16[704,512]{1,0:T(8,128)(2,1)S(1)} %get-tuple-element.173), channel_id=1, source_target_pairs={{0,16},{16,0},{1,17},{17,1},{2,18},{18,2},{3,19},{19,3},{4,20},{20... | collective-permute-start | bytes 2162696 | tf_op jit(solution)/shard_map/ppermute | solution.py:845
  120.7 13.5 %collective-permute-start.38 = (bf16[128,1024]{1,0:T(8,128)(2,1)S(1)}, bf16[128,1024]{1,0:T(8,128)(2,1)S(1)}, u32[]{:S(2)}, u32[]{:S(2)}) collective-permute-start(bf16[128,1024]{1,0:T(8,128)(2,1)S(1)} %get-tuple-element.163.refs_11_), channel_id=1, source_target_pairs={{0,3},{1,2},{2,1},{3,0},{4,7},{5,6},{6,5},{7,4},{8,11},{9,10},{10,... | collective-permute-start | bytes 786440 | tf_op jit(solution)/shard_map/ppermute | solution.py:853
  140.6 23.8 %collective-permute-start.42 = (bf16[2,1024,256]{2,1,0:T(8,128)(2,1)S(1)}, bf16[2,1024,256]{2,1,0:T(8,128)(2,1)}, u32[]{:S(2)}, u32[]{:S(2)}) collective-permute-start(bf16[2,1024,256]{2,1,0:T(8,128)(2,1)S(1)} %get-tuple-element.175.refs_1_.refs_10_.refs_2_), channel_id=1, source_target_pairs={{0,8},{8,0},{1,9},{9,1},{2,10},{10,2},{3,11},{11,3},{4,12},{12,4},... | collective-permute-start | bytes 3145736 | tf_op jit(solution)/shard_map/ppermute | solution.py:845
  140.7 23.7 %collective-permute-start.40 = (bf16[256,1024]{1,0:T(8,128)(2,1)}, bf16[256,1024]{1,0:T(8,128)(2,1)S(1)}, u32[]{:S(2)}, u32[]{:S(2)}) collective-permute-start(bf16[256,1024]{1,0:T(8,128)(2,1)} %shard_map.241), channel_id=1, source_target_pairs={{0,1},{1,0},{2,3},{3,2},{4,5},{5,4},{6,7},{7,6},{8,9},{9,8},{10,11... | collective-permute-start | bytes 1572872 | tf_op jit(solution)/shard_map/ppermute | solution.py:845
  141.2 19.1 %collective-permute-start.41 = (bf16[352,512]{1,0:T(8,128)(2,1)S(1)}, bf16[352,512]{1,0:T(8,128)(2,1)S(1)}, u32[]{:S(2)}, u32[]{:S(2)}) collective-permute-start(bf16[352,512]{1,0:T(8,128)(2,1)S(1)} %shard_map.244), channel_id=1, source_target_pairs={{0,16},{16,0},{1,17},{17,1},{2,18},{18,2},{3,19},{19,3},{4,20},{20... | collective-permute-start | bytes 1081352 | tf_op jit(solution)/shard_map/ppermute | solution.py:845
  142.6 17.7 %collective-permute-start.43 = (bf16[704,256]{1,0:T(8,128)(2,1)}, bf16[704,256]{1,0:T(8,128)(2,1)S(1)}, u32[]{:S(2)}, u32[]{:S(2)}) collective-permute-start(bf16[704,256]{1,0:T(8,128)(2,1)} %get-tuple-element.198), channel_id=1, source_target_pairs={{0,0},{2,2},{4,8},{6,10},{8,4},{10,6},{12,12},{14,14},{1,1},{3,3},... | collective-permute-start | bytes 1081352 | tf_op jit(solution)/shard_map/ppermute | solution.py:970
  144.4 20.0 %collective-permute-start.44 = (bf16[704,256]{1,0:T(8,128)(2,1)S(1)}, bf16[704,256]{1,0:T(8,128)(2,1)S(1)}, u32[]{:S(2)}, u32[]{:S(2)}) collective-permute-start(bf16[704,256]{1,0:T(8,128)(2,1)S(1)} %get-tuple-element.199), channel_id=1, source_target_pairs={{0,8},{2,10},{4,0},{6,2},{8,12},{10,14},{12,4},{14,6},{1,9},{3,11}... | collective-permute-start | bytes 1081352 | tf_op jit(solution)/shard_map/ppermute | solution.py:970
  166.1 17.2 %collective-permute-start.47 = (bf16[2,8,144,256]{3,2,1,0:T(8,128)(2,1)S(1)}, bf16[2,8,144,256]{3,2,1,0:T(8,128)(2,1)S(1)}, u32[]{:S(2)}, u32[]{:S(2)}) collective-permute-start(bf16[2,8,144,256]{3,2,1,0:T(8,128)(2,1)S(1)} %get-tuple-element.204), channel_id=1, source_target_pairs={{0,8},{8,0},{1,9},{9,1},{2,10},{10,2},{3,11},{11,3},{4,12},{12,4},... | collective-permute-start | bytes 3538952 | tf_op jit(solution)/shard_map/ppermute | solution.py:845
  166.2 17.1 %collective-permute-start.45 = (bf16[512,640]{1,0:T(8,128)(2,1)S(1)}, bf16[512,640]{1,0:T(8,128)(2,1)S(1)}, u32[]{:S(2)}, u32[]{:S(2)}) collective-permute-start(bf16[512,640]{1,0:T(8,128)(2,1)S(1)} %get-tuple-element.201), channel_id=1, source_target_pairs={{0,1},{1,0},{2,3},{3,2},{4,5},{5,4},{6,7},{7,6},{8,9},{9,8},{10,11... | collective-permute-start | bytes 1966088 | tf_op jit(solution)/shard_map/ppermute | solution.py:845
  167.7 14.1 %collective-permute-start.46 = (bf16[1024,256]{1,0:T(8,128)(2,1)S(1)}, bf16[1024,256]{1,0:T(8,128)(2,1)S(1)}, u32[]{:S(2)}, u32[]{:S(2)}) collective-permute-start(bf16[1024,256]{1,0:T(8,128)(2,1)S(1)} %get-tuple-element.200.refs_2_), channel_id=1, source_target_pairs={{0,16},{16,0},{1,17},{17,1},{2,18},{18,2},{3,19},{19,3},{4,20},{20... | collective-permute-start | bytes 1572872 | tf_op jit(solution)/shard_map/ppermute | solution.py:845
  186.3 21.8 %collective-permute-start.53 = (bf16[1088,256]{1,0:T(8,128)(2,1)}, bf16[1088,256]{1,0:T(8,128)(2,1)}, u32[]{:S(2)}, u32[]{:S(2)}) collective-permute-start(bf16[1088,256]{1,0:T(8,128)(2,1)} %get-tuple-element.215), channel_id=1, source_target_pairs={{0,1},{1,0},{2,3},{3,2},{4,5},{5,4},{6,7},{7,6},{8,9},{9,8},{10,11... | collective-permute-start | bytes 1671176 | tf_op jit(solution)/shard_map/ppermute | solution.py:845
  187.7 20.4 %collective-permute-start.50 = (bf16[128,1792]{1,0:T(8,128)(2,1)}, bf16[128,1792]{1,0:T(8,128)(2,1)S(1)}, u32[]{:S(2)}, u32[]{:S(2)}) collective-permute-start(bf16[128,1792]{1,0:T(8,128)(2,1)} %get-tuple-element.208), channel_id=1, source_target_pairs={{0,2},{2,0},{4,6},{6,4},{1,3},{3,1},{5,7},{7,5},{8,10},{10,8},{12,... | collective-permute-start | bytes 1376264 | tf_op jit(solution)/shard_map/ppermute | solution.py:849
  190.0 17.9 %collective-permute-start.54 = (bf16[576,256]{1,0:T(8,128)(2,1)}, bf16[576,256]{1,0:T(8,128)(2,1)}, u32[]{:S(2)}, u32[]{:S(2)}) collective-permute-start(bf16[576,256]{1,0:T(8,128)(2,1)} %get-tuple-element.216), channel_id=1, source_target_pairs={{0,16},{16,0},{1,17},{17,1},{2,18},{18,2},{3,19},{19,3},{4,20},{20... | collective-permute-start | bytes 884744 | tf_op jit(solution)/shard_map/ppermute | solution.py:845
  190.9 17.0 %collective-permute-start.55 = (bf16[576,256]{1,0:T(8,128)(2,1)}, bf16[576,256]{1,0:T(8,128)(2,1)}, u32[]{:S(2)}, u32[]{:S(2)}) collective-permute-start(bf16[576,256]{1,0:T(8,128)(2,1)} %get-tuple-element.217), channel_id=1, source_target_pairs={{0,17},{1,16},{16,1},{17,0},{2,19},{3,18},{18,3},{19,2},{4,21},{5,... | collective-permute-start | bytes 884744 | tf_op jit(solution)/shard_map/ppermute | solution.py:1011
  (101 other events, 935.0 us)

commit v3 on v2

--- a/solution.py
+++ b/solution.py
@@ -364,7 +364,7 @@
 RING = (0, 2, 4, 6, 7, 5, 3, 1)
 MIB = 2**20
 
-FS, ZS, Y0, Y1, ZH0, ZH1, ZL, ROW0, BLOCK, X0, X1 = 8, 12, 16, 17, 18, 19, 20, 21, 22, 23, 24
+FS, ZS, Y0, Y1, ZH0, ZH1, ZL, ROW0, BLOCK, X0, X1, DOWN = 8, 12, 16, 17, 18, 19, 20, 21, 22, 23, 24, 25
 
 
 def dot_nn(left, right):
@@ -391,8 +391,8 @@
 
 
 class Late:
-    def __init__(self, ref, out, sem):
-        self.ref, self.out, self.sem, self.shape, self.copy = ref, out, sem, ref.shape, None
+    def __init__(self, ref, out, sems, parts):
+        self.ref, self.out, self.sems, self.parts, self.shape, self.copies = ref, out, sems, parts, ref.shape, []
 
     def __getitem__(self, index):
         return self.ref[index]
@@ -401,13 +401,16 @@
         self.ref[index] = value
 
     def flush(self):
-        self.copy = pltpu.make_async_copy(self.ref, self.out, self.sem)
-        self.copy.start()
-
-
-def call(kernel, n_smem, outs, scratch=(), limit=16, flops=1, far_in=(), far_out=()):
+        n = self.shape[0] // self.parts
+        band = pl.ds(len(self.copies) * n, n)
+        copy = pltpu.make_async_copy(self.ref.at[band], self.out.at[band], self.sems[len(self.copies)])
+        copy.start()
+        self.copies.append(copy)
+
+
+def call(kernel, n_smem, outs, scratch=(), limit=16, flops=1, far_in=(), far_out=(), parts=1, split=()):
     far_in, far_out = tuple(far_in), tuple(far_out)
-    n_out, n_far = len(outs), len(far_in) + len(far_out)
+    n_out, n_far, n_sems = len(outs), len(far_in) + len(far_out), len(far_in) + parts * len(far_out)
 
     def run(*args, deps=()):
         n_in = len(args) - n_smem
@@ -423,17 +426,19 @@
                 ins[i] = Lazy(far[k], copy)
             late = []
             for k, i in enumerate(far_out):
-                results[i] = Late(far[len(far_in) + k], results[i], sems.at[len(far_in) + k])
+                own_sems = [sems.at[len(far_in) + parts * k + p] for p in range(parts)]
+                results[i] = Late(far[len(far_in) + k], results[i], own_sems, parts if i in split else 1)
                 late.append(results[i])
             kernel(*smem, *ins, *results, *own)
             for i in far_in:
                 if ins[i].copy is not None:
                     ins[i].copy.wait()
             for v in late:
-                if v.copy is None:
+                while len(v.copies) < v.parts:
                     v.flush()
             for v in late:
-                v.copy.wait()
+                for copy in v.copies:
+                    copy.wait()
 
         spec = lambda i, far: pl.BlockSpec(memory_space=pl.ANY if i in far else pltpu.VMEM)
         shapes = [pltpu.VMEM(shape, dtype) for shape, dtype in scratch]
@@ -444,7 +449,7 @@
             in_specs=[pl.BlockSpec(memory_space=pltpu.SMEM)] * n_smem + [spec(i, far_in) for i in range(n_in)] + [pl.BlockSpec(memory_space=pl.ANY)] * len(deps),
             out_specs=[spec(i, far_out) for i in range(n_out)],
             out_shape=[jax.ShapeDtypeStruct(shape, dtype) for shape, dtype in outs],
-            scratch_shapes=shapes + [pltpu.SemaphoreType.DMA((max(1, n_far),))],
+            scratch_shapes=shapes + [pltpu.SemaphoreType.DMA((max(1, n_sems),))],
             compiler_params=pltpu.CompilerParams(vmem_limit_bytes=limit * MIB),
             cost_estimate=pl.CostEstimate(flops=flops, bytes_accessed=0, transcendentals=0),
         )(*args, *deps)
@@ -459,9 +464,17 @@
     keys = 8 * rows
     part = wl[0].shape[0]
     width = GQ * rows
+    for i in range(8):
+        values = tok[i][...].astype(F32)
+        na_ref[at(idx[i], rows), :] = (values * fold(values)).astype(BF)
+    na_ref.flush()
+    for k in range(4):
+        wlt_ref[:, at(idx[FS + k], part)] = wl[k][...].T
+    wlt_ref.flush()
+    lat_ref[...] = contract_cols(na_ref[...], wlt_ref[...]).astype(BF)
+    lat_ref.flush()
     for k in range(4):
         here = at(idx[FS + k], part)
-        wlt_ref[:, here] = wl[k][...].T
         if k < 2:
             wq_ref[here, :] = wb[k][:, 0:QW]
             wk_ref[:, here] = wb[k][:, QW : QW + LAT_HEAD]
@@ -473,14 +486,8 @@
             wq_ref[here, cut:QW] = second[:, 0 : QW - cut]
             wk_ref[:, here] = second[:, QW - cut : QW - cut + LAT_HEAD]
             wv_ref[:, here] = second[:, QW - cut + LAT_HEAD : QW - cut + 2 * LAT_HEAD]
-    for i in range(8):
-        values = tok[i][...].astype(F32)
-        normed = (values * fold(values)).astype(BF)
-        na_ref[at(idx[i], rows), :] = normed
-        if i == 0:
-            q_ref[...] = dot_nn(normed, wq_ref[...]).astype(BF)
-    lat_ref[...] = contract_cols(na_ref[...], wlt_ref[...]).astype(BF)
-    for ref in (wq_ref, wk_ref, wv_ref, wlt_ref, q_ref, na_ref, lat_ref):
+    q_ref[...] = dot_nn(na_ref[at(idx[0], rows), :], wq_ref[...]).astype(BF)
+    for ref in (wq_ref, wk_ref, wv_ref, q_ref):
         ref.flush()
     place = lax.broadcasted_iota(jnp.int32, (rows, keys), 1)
     own = idx[ROW0] + lax.broadcasted_iota(jnp.int32, (rows, keys), 0)
@@ -508,8 +515,8 @@
             probs_ref[band, :] = (mass * (1.0 / jnp.sum(mass, axis=-1, keepdims=True))).astype(BF)
         band = slice(g * width, (g + 1) * width)
         out_ref[band, :] = dot_nn(probs_ref[band, :], lat).astype(BF)
-    for ref in (probs_ref, qs_ref, out_ref):
-        ref.flush()
+        for ref in (probs_ref, qs_ref, out_ref):
+            ref.flush()
     for p in range(HEADS // 2):
         cols = slice(p * 2 * HD, (p + 1) * 2 * HD)
         a, b = (dot_nn(out_ref[(2 * p + j) * rows : (2 * p + j + 1) * rows, :], wv_ref[:, cols]) for j in range(2))
@@ -524,14 +531,14 @@
     macs = 2 * HEADS * rows * keys * LAT_HEAD + keys * d * n_lat
     return call(
         attend_kernel, 2, [(v, BF) for v in outs], [((2 * rows, keys), F32)], limit=60,
-        far_in=range(18), far_out=range(1, 11),
+        far_in=range(18), far_out=range(1, 11), parts=GROUPS, split=(1, 2, 3),
     )(
         idx, lens, *blocks, *w_lats, *w_bigs, deps=deps
     )
 
 
 def project_kernel(idx, mixed, tok, *refs):
-    parts, (cot_up, cot_far, cot_diag, gu_c, resid_ref, normed_ref, pack_ref) = refs[:4], refs[4:]
+    parts, (cot_up, cot_far, cot_diag, cot, gu_c, down, resid_ref, normed_ref, pack_ref) = refs[:4], refs[4:]
     total = tok[...].astype(F32)
     for k, w in enumerate(parts):
         total = total + dot_nn(mixed[:, at(idx[FS + k], w.shape[0])], w[...])
@@ -540,11 +547,13 @@
     normed_ref[...] = normed
     rows = normed.shape[0]
     pack_ref[0:rows, :] = normed
-    for i, ref in enumerate((cot_up, cot_far, cot_diag)):
+    for i, ref in enumerate((cot_up, cot_far, cot_diag, cot)):
         pack_ref[(i + 1) * rows : (i + 2) * rows, :] = ref[...]
     n = gu_c.shape[0] // 2
-    pack_ref[4 * rows :, 0 : gu_c.shape[1]] = gu_c[n:, :]
-    pack_ref[4 * rows :, gu_c.shape[1] :] = jnp.zeros((n, pack_ref.shape[1] - gu_c.shape[1]), BF)
+    first = 5 * rows
+    pack_ref[first : first + n, 0 : gu_c.shape[1]] = gu_c[n:, :]
+    pack_ref[first : first + n, gu_c.shape[1] :] = jnp.zeros((n, pack_ref.shape[1] - gu_c.shape[1]), BF)
+    pack_ref[first + n :, :] = down[...]
 
 
 def columns_kernel(idx, gate_ref, up_ref, gain_ref, own_ref, near_ref, pair_ref, all_ref):
@@ -562,12 +571,19 @@
     pair_ref[rows:, :] = near_ref[...]
 
 
-def assemble_kernel(idx, own, near, far, pack, down, gu_ref, dn_ref):
+def assemble_kernel(idx, own, near, far, pack, down_x, down, gu_ref, dn_ref, near_ref):
+    near_ref[...] = pack[0 : near_ref.shape[0], :]
     part, n = own.shape
-    for k, w in enumerate((own[...], near[...], far[0:part, :], pack[-part:, 0:n])):
+    first = pack.shape[0] - down.shape[0]
+    for k, w in enumerate((own[...], near[...], far[0:part, :], pack[first - part : first, 0:n])):
         gu_ref[at(idx[FS + k], part), :] = w
     n = down.shape[0]
-    dn_ref[0:n, :] = down[...]
+    for i, ref in enumerate((down_x, pack, down)):
+
+        @pl.when(idx[DOWN] == i)
+        def _(ref=ref):
+            dn_ref[0:n, :] = ref[-n:, :]
+
     dn_ref[n:, :] = jnp.zeros((dn_ref.shape[0] - n, dn_ref.shape[1]), BF)
 
 
@@ -600,31 +616,20 @@
     return [at(2 * idx[xx] + idx[zz], shard) for xx in (X1, X0) for zz in (ZH1, ZH0)]
 
 
-def grow_kernel(places, idx, hid, both, n0, n1, c0, c1, *refs):
-    down_ref, gu_ref = refs[-2:]
-    shard = n0.shape[1] // 4
-    rows = hid.shape[0] // 2
+def outer_kernel(ff8, places, idx, *refs):
+    hids, boths, blocks, (send1, keep1, send2, keep2) = refs[0:4], refs[4:8], refs[8:24], refs[24:28]
+    rows = hids[0].shape[0] // 2
+    shard = send1.shape[1] // 2
+    wide = (ff8 + 127) // 128 * 128
+    hid = jnp.concatenate([ref[...] for ref in hids], 0)
+    both = jnp.concatenate([ref[...] for ref in boths], 0)
     for j, cols in enumerate(relative_columns(idx, shard)):
-        here = slice(j * shard, (j + 1) * shard)
-        v0, v1, t0, t1 = (ref[p : p + rows, cols] for ref, p in zip((n0, n1, c0, c1), places))
-        down = contract_rows(hid[...], jnp.concatenate([t0, t1], 0))
-        gu = contract_rows(both[...], jnp.concatenate([v0, v1], 0))
-        if len(refs) == 4:
-            down, gu = down + refs[0][:, here], gu + refs[1][:, here]
-        down_ref[:, here] = down
-        gu_ref[:, here] = gu
-
-
-def last_kernel(ff8, places, idx, hid, both, n0, n1, c0, c1, down_ref, gu_ref, send1, keep1, send2, keep2):
-    shard = n0.shape[1] // 4
-    rows = hid.shape[0] // 2
-    wide = (ff8 + 127) // 128 * 128
-    for j, cols in enumerate(relative_columns(idx, shard)):
-        here = slice(j * shard, (j + 1) * shard)
         there = slice(j % 2 * shard, (j % 2 + 1) * shard)
-        v0, v1, t0, t1 = (ref[p : p + rows, cols] for ref, p in zip((n0, n1, c0, c1), places))
-        down = down_ref[:, here] + contract_rows(hid[...], jnp.concatenate([t0, t1], 0))
-        gu = gu_ref[:, here] + contract_rows(both[...], jnp.concatenate([v0, v1], 0))
+        values = [ref[p : p + rows, cols] for ref, p in zip(blocks, places)]
+        normed = jnp.concatenate([v for i in range(4) for v in values[4 * i : 4 * i + 2]], 0)
+        cot = jnp.concatenate([v for i in range(4) for v in values[4 * i + 2 : 4 * i + 4]], 0)
+        down = contract_rows(hid, cot)
+        gu = contract_rows(both, normed)
         one, two = (send1, send2) if j < 2 else (keep1, keep2)
         one[0:ff8, there] = down[0:ff8].astype(BF)
         one[ff8:, there] = gu[0:ff8].astype(BF)
@@ -730,7 +735,7 @@
                     out[i, 4 * j + kz, HD + n_lat :, :] = sums_ref[:, cols]
 
 
-def outer_query_kernel(idx, na, p0, p1, p2, p3, own, near, far, diag, total_ref):
+def outer_query_kernel(idx, na, p0, p1, p2, p3, f1, f2, own, near, far, diag, total_ref):
     rows = p0.shape[0]
     wide = 2 * HD
     total = None
@@ -741,8 +746,15 @@
             term = contract_rows(na[at(2 * idx[ZS + k] + idx[yy], rows), :], right)
             total = term if total is None else total + term
     total_ref[...] = total.astype(BF)
-    for k, out in enumerate((own, near, far, diag)):
-        out[...] = total_ref[at(idx[FS + k], out.shape[0]), :]
+    n = own.shape[0]
+    for k, out in ((0, own), (2, far), (3, diag)):
+        out[...] = total_ref[at(idx[FS + k], n), :]
+    first = 0
+    for ref in (f1, f2):
+        near[first : first + ref.shape[0], :] = ref[:, 0 : near.shape[1]]
+        first += ref.shape[0]
+    for i in range(n // rows):
+        near[first:, i * wide : (i + 1) * wide] = total_ref[at(idx[FS + 1] * (n // rows) + i, rows), :]
 
 
 def tokens_kernel(p0, p1, p2, p3, e_ref, wlt, tok, dresid, out_ref):
@@ -791,28 +803,18 @@
     o_x[rows:, :] = sums[3].astype(BF)
 
 
-def halves_kernel(*refs):
-    n = len(refs) // 4
-    for i in range(n):
-        total = wide_sum(refs[2 * i][...], refs[2 * i + 1][...]).astype(BF)
-        first, second = refs[2 * n + 2 * i : 2 * n + 2 * i + 2]
-        cut = first.shape[1]
-        first[...] = total[:, :cut]
-        second[...] = total[:, cut:]
-
-
-def two_kernel(keep, there, own, far):
-    own[...] = wide_sum(keep[0], there[0]).astype(BF)
-    far[...] = wide_sum(keep[1], there[1]).astype(BF)
-
-
-def eleventh_kernel(up_keep, up_there, go_keep, go_there, up_b, up_a, go_own, go_far):
-    halves_kernel(up_keep, up_there, up_b, up_a)
+def sum_kernel(left, right, out):
+    out[...] = wide_sum(left[...], right[...]).astype(BF)
+
+
+def eleventh_kernel(up_keep, up_there, go_keep, go_there, o_up, o_x, up, go_own, go_far, o_send):
+    o_send[...] = wide_sum(o_up[...], o_x[o_up.shape[0] :, :]).astype(BF)
+    sum_kernel(up_keep, up_there, up)
     go_own[...] = wide_sum(go_keep[0], go_there[0]).astype(BF)
     go_far[...] = wide_sum(go_keep[1], go_there[1]).astype(BF)
 
 
-def exchange_kernel(keep, there, go_own, go_far, b_keep, b_there, o_up, o_x, p0, p1, p2, p3, b_x, b_xy, y_send, y_keep):
+def exchange_kernel(keep, there, go_own, go_far, b_keep, b_there, p0, p1, p2, p3, b_x, b_xy, y_send, y_keep):
     rows, wide = p0.shape
     n = wide - 4 * HD
     for k, out in enumerate((p0, p1, p2, p3)):
@@ -820,7 +822,6 @@
         out[:, 0:n] = wide_sum(keep[band, 0:n], there[band, 0:n]).astype(BF)
         out[:, n : n + 2 * HD] = keep[band, n:]
         out[:, n + 2 * HD : wide] = there[band, n:]
-    p1[:, wide:] = wide_sum(o_up[...], o_x[rows:, :]).astype(BF)
     tall = b_keep.shape[2]
     for j in range(8):
         band = slice(j % 4 * tall, (j % 4 + 1) * tall)
@@ -883,7 +884,7 @@
         return (weight.astype(F32) * gain).astype(BF)
 
     owners = [s, owner(place - 1), owner(place + 1), owner(place - 2), owner(place + 2), owner(place - 3), owner(place + 3), owner(place - 4)]
-    idx = jnp.stack(owners + [f, f ^ 1, f ^ 2, f ^ 3, z, z ^ 1, z ^ 2, z ^ 3, y, y ^ 1, zh, zh ^ 1, zl, s * rows, 4 * c + 2 * zl + y, x, x ^ 1]).astype(jnp.int32)
+    idx = jnp.stack(owners + [f, f ^ 1, f ^ 2, f ^ 3, z, z ^ 1, z ^ 2, z ^ 3, y, y ^ 1, zh, zh ^ 1, zl, s * rows, 4 * c + 2 * zl + y, x, x ^ 1, jnp.where(x != c, 0, jnp.where(zl != c, 1, 2))]).astype(jnp.int32)
     gain_a = attn_gain.astype(F32)[:, None]
     gain_m = mlp_gain.astype(F32)[:, None]
 
@@ -906,73 +907,78 @@
     wo_own = through((w_out,), (a2,))[0]
     wo_far, wo_near = swap(wo_own, "x"), swap(wo_own, "c")
     a3, wb_b = through((a3, wb_b), (b3, wo_far, gu_near))
+    down = lax.dynamic_slice_in_dim(w_down, y * ff8, ff8, 0)
     a4 = ring(a3, cw)
     wb_far.append(swap(wb_b, "x"))
     wb_diag, wo_diag = [swap(v, "c") for v in wb_far], swap(wo_far, "c")
 
-    a4, gu_far, cot, down_rows = through((a4, gu_far, cotangent, lax.dynamic_slice_in_dim(w_down, y * ff8, ff8, 0)), (wb_far[1], wo_diag))
+    a4, gu_far, cot = through((a4, gu_far, cotangent), (wb_far[1], wo_diag))
     gu_far = swap(gu_far, "x")
-    pairs = []
-    for i in range(16):
-        xx, cc, zz = i // 8, i // 4 % 2, i % 4
-        pairs.append(((2 * cc + zz % 2) * 4 + zz - zz % 2 + xx, i))
-    down_rows = lax.ppermute(down_rows, ("x", "c", "z"), pairs)
-    cot_far, cot_up, cot_near, cot_diag = swap(cot, "y"), hop(cot, 1), swap(cot, "c"), corner(cot)
+    cot_far, cot_up, cot_diag = swap(cot, "y"), hop(cot, 1), corner(cot)
     mixed, probs, outs, qs, queries, na_all, lat_all, w_q, w_key, w_value, w_lat_t = attend(
         idx, lengths, (tokens, a1, b1, a2, b2, a3, b3, a4), (wl_own, wl_near, wl_far, wl_diag), (wb_own, wb_near, *wb_far, *wb_diag)
     )
     w_os = (w_out, wo_near, wo_far, wo_diag)
-    resid, normed, pack = call(project_kernel, 1, [((rows, d), F32), ((rows, d), BF), ((4 * rows + shard, d), BF)])(
-        idx, mixed, tokens, *w_os, cot_up, cot_far, cot_diag, gu_far, deps=(down_rows,)
+    resid, normed, pack = call(project_kernel, 1, [((rows, d), F32), ((rows, d), BF), ((5 * rows + shard + ff8, d), BF)])(
+        idx, mixed, tokens, *w_os, cot_up, cot_far, cot_diag, cot, gu_far, down
     )
 
     pack = swap(pack, "c")
     nm_far, nm_up, nm_diag = swap(normed, "y"), hop(normed, 1), corner(normed)
-    nm_up2, nm_far2, nm_diag2 = swap(nm_up, "c"), swap(nm_far, "c"), swap(nm_diag, "c")
-    w_gu, w_dn = call(assemble_kernel, 1, [((d, 2 * wide), BF), ((wide, d), BF)])(
-        idx, gu_own, gu_near, gu_far, pack, down_rows, deps=(nm_far, nm_up, nm_diag)
+    down_x = through((down,), (normed,))[0]
+    pairs = []
+    for xx in range(2):
+        for zz in range(4):
+            pairs.append((((1 - xx) * 2 + zz % 2) * 4 + zz, (xx * 2 + 1 - xx) * 4 + zz))
+    down_x = lax.ppermute(down_x, ("x", "c", "z"), pairs)
+    w_gu, w_dn, near = call(assemble_kernel, 1, [((d, 2 * wide), BF), ((wide, d), BF), ((5 * rows, d), BF)])(
+        idx, gu_own, gu_near, gu_far, pack, down_x, down
     )
 
     def unit(places, *args, deps=()):
         shapes = [((2 * rows, wide), BF), ((2 * rows, 2 * wide), BF), ((rows, d), F32), ((rows, d), F32), ((2 * rows, d), BF)]
         return call(functools.partial(unit_kernel, places), 0, shapes)(*args, w_gu, w_dn, deps=deps)
 
-    def grow(places, *args, deps=()):
-        return call(functools.partial(grow_kernel, places), 1, [((wide, d), F32), ((2 * wide, d), F32)], limit=12)(idx, *args, deps=deps)
-
-    at_own, at_up, at_far, at_diag = (0, 0, 0, 0), (0, 0, 0, rows), (0, 0, 0, 2 * rows), (0, 0, 0, 3 * rows)
-    own_rows, up_rows, far_rows = (normed, pack, cot, cot_near), (nm_up, nm_up2, cot_up, pack), (nm_far, nm_far2, cot_far, pack)
-    diag_rows = (nm_diag, nm_diag2, cot_diag, pack)
+    at_own, at_up, at_far, at_diag = (0, 0, 0, 4 * rows), (0, 0, 0, rows), (0, 0, 0, 2 * rows), (0, 0, 0, 3 * rows)
+    own_rows = (normed, near, cot, near)
     own = unit(at_own, *own_rows)
-    sums = grow(at_own, *own[:2], *own_rows)
-    up = unit(at_up, *up_rows, deps=(sums[0],))
-    far = unit(at_far, *far_rows, deps=(up[0],))
-    diag = unit(at_diag, *diag_rows, deps=(far[0],))
+    nm_far = through((nm_far,), (w_dn,))[0]
+    nm_far2 = swap(nm_far, "c")
+    far_rows = (nm_far, nm_far2, cot_far, near)
+    far = unit(at_far, *far_rows, deps=(own[0],))
+    nm_up = through((nm_up,), (own[0],))[0]
+    nm_up2 = swap(nm_up, "c")
+    up_rows = (nm_up, nm_up2, cot_up, near)
+    up = unit(at_up, *up_rows, deps=(far[0],))
+    nm_diag = through((nm_diag,), (own[0],))[0]
+    nm_diag2 = swap(nm_diag, "c")
+    diag_rows = (nm_diag, nm_diag2, cot_diag, near)
+    diag = unit(at_diag, *diag_rows, deps=(up[0],))
     near2, up2, far2, diag2 = (swap(v[4], "c") for v in (own, up, far, diag))
     units = (own, up, far, diag)
     shapes = [((rows, d), F32)] + [((rows, d), BF)] * 3 + [((rows, d), F32)] * 2 + [((2 * rows, d), BF)]
     e_own, *early, o_own, o_up, o_x = call(rows_kernel, 0, shapes)(*[v[2] for v in units], *[v[3] for v in units], near2, up2, far2, diag2)
     d_up, d_far, d_diag = hop(early[0], 1), swap(early[1], "y"), corner(early[2])
-    sums = grow(at_up, *up[:2], *up_rows, *sums, deps=early)
-    sums = grow(at_far, *far[:2], *far_rows, *sums)
     shapes = [((2 * ff8, 2 * shard), BF)] * 2 + [((ff8, 2 * shard), BF)] * 2
-    y1_send, y1_keep, y2_send, y2_keep = call(functools.partial(last_kernel, ff8, at_diag), 1, shapes)(idx, *diag[:2], *diag_rows, *sums)
+    at_all, all_rows = at_own + at_up + at_far + at_diag, own_rows + up_rows + far_rows + diag_rows
+    y1_send, y1_keep, y2_send, y2_keep = call(functools.partial(outer_kernel, ff8, at_all), 1, shapes, limit=24)(
+        idx, *[v[0] for v in units], *[v[1] for v in units], *all_rows
+    )
     y1_there = swap(y1_send, "x")
     dresid, dattn, dmixed, v_m = call(middle_kernel, 1, [((rows, d), F32), ((rows, d), BF), ((rows, QW), BF), ((8, d), F32)])(
         idx, e_own, d_far, d_up, d_diag, resid, cotangent, *w_os, deps=(y1_there,)
     )
 
-    def home(value, m):
+    def home(value):
         pairs = []
         for i in range(8):
             cc, hh, ll = i // 4, i // 2 % 2, i % 2
-            pairs.append((i, (hh ^ m) * 4 + 2 * cc + ll))
+            pairs.append((i, hh * 4 + 2 * cc + ll))
         return lax.ppermute(value, ("c", "z"), pairs)
 
     go_send, go_keep = call(outer_out_kernel, 1, [((2, QW, shard), BF)] * 2)(idx, mixed, dattn)
     go_there = swap(go_send, "c")
-    f1_b, f1_a = call(halves_kernel, 0, [((2 * ff8, shard), BF)] * 2)(y1_keep, y1_there, deps=(go_send,))
-    f1_a, f1_b = home(f1_a, 0), home(f1_b, 1)
+    f1 = home(call(sum_kernel, 0, [((2 * ff8, 2 * shard), BF)])(y1_keep, y1_there, deps=(go_send,))[0])
     o_x = swap(through((o_x,), (go_send,))[0], "y")
     y2_there = swap(through((y2_send,), (go_send,))[0], "x")
     dlat, p_send, p_keep, dq, ups = call(
@@ -992,19 +998,19 @@
         limit=24,
         far_in=(1, 2, 4),
     )(idx, dlat, na_all, w_lat_t, dq, w_q, ups, v_m)
-    f2_b, f2_a, go_own, go_far = call(eleventh_kernel, 0, [((ff8, shard), BF)] * 2 + [((QW, shard), BF)] * 2)(
-        y2_keep, y2_there, go_keep, go_there, deps=(b_send, f1_a, f1_b, o_x)
+    f2, go_own, go_far, o_send = call(eleventh_kernel, 0, [((ff8, 2 * shard), BF)] + [((QW, shard), BF)] * 2 + [((rows, d), BF)])(
+        y2_keep, y2_there, go_keep, go_there, o_up, o_x, deps=(b_send, f1)
     )
     b_send, p_send = through((b_send, p_send), (go_far,))
     p_there = swap(p_send, "y")
-    f2_a, f2_b = home(f2_a, 0), home(f2_b, 1)
+    f2, o_there = home(f2), hop(o_send, 1)
     go_far, b_there = swap(go_far, "x"), swap(b_send, "c")
     flat = ((4 * tall, shard), BF)
     tower = ((4 * tall + QW // 2, shard), BF)
     n_p = n_lat + 4 * HD
-    shapes = [((rows, n), BF) for n in (n_p, n_p + d, n_p, n_p)] + [flat, flat, tower, tower]
+    shapes = [((rows, n_p), BF)] * 4 + [flat, flat, tower, tower]
     p0, p1, p2, p3, b_x, b_xy, y_send, y_keep = call(exchange_kernel, 0, shapes)(
-        p_keep, p_there, go_own, go_far, b_keep, b_there, o_up, o_x, deps=(f2_a, f2_b)
+        p_keep, p_there, go_own, go_far, b_keep, b_there, deps=(f2, o_there)
     )
     pieces = (p0, hop(p1, 1), hop(p2, 2), hop(p3, 3))
     b_x, y_there = swap(b_x, "x"), swap(y_send, "y")
@@ -1013,16 +1019,18 @@
         y_keep, y_there, b_x, b_xy, deps=pieces[1:]
     )
     last = z0.astype(F32) + hop(z1, 1) + hop(z2, 2) + hop(z3, 3)
-    gq, gq_near, gq_far, gq_diag = call(outer_query_kernel, 1, [((shard, 2 * HD), BF)] * 4, [((d, 2 * HD), BF)], far_in=(0,))(
-        idx, na_all, *pieces, deps=(z0,)
-    )
-    gq_near, gq_far, gq_diag = swap(gq_near, "c"), swap(gq_far, "x"), lax.ppermute(gq_diag, ("x", "c"), [(i, i ^ 3) for i in range(4)])
+    quarter = ((shard, 2 * HD), BF)
+    gq, near, gq_far, gq_diag = call(
+        outer_query_kernel, 1, [quarter, ((3 * ff8 + rows, shard), BF), quarter, quarter], [((d, 2 * HD), BF)], far_in=(0,)
+    )(idx, na_all, *pieces, f1, f2, deps=(z0,))
+    near, gq_far, gq_diag = swap(near, "c"), swap(gq_far, "x"), lax.ppermute(gq_diag, ("x", "c"), [(i, i ^ 3) for i in range(4)])
     tokens_grad = call(tokens_kernel, 0, [((rows, d), BF)])(*pieces, e_q, w_lat_t, tokens, dresid, deps=(gq,))[0]
+    gq_near = jnp.concatenate([near[3 * ff8 :, i * 2 * HD : (i + 1) * 2 * HD] for i in range(shard // rows)], 0)
     grad_query = (plus(gq, gq_near) + plus(gq_far, gq_diag)) * gain_a
-    output = (resid + o_own + o_x[:rows] + pieces[1][:, n_p:]).astype(BF)
-    grad_down = plus(f1_a[:ff8], f1_b[:ff8])
-    grad_gate = plus(f1_a[ff8:], f1_b[ff8:]).T * gain_m
-    grad_up = plus(f2_a, f2_b).T * gain_m
+    output = (resid + o_own + o_x[:rows] + o_there).astype(BF)
+    grad_down = plus(f1[:ff8, shard:], near[:ff8])
+    grad_gate = plus(f1[ff8:, shard:], near[ff8 : 2 * ff8]).T * gain_m
+    grad_up = plus(f2[:, shard:], near[2 * ff8 : 3 * ff8]).T * gain_m
     grad_out = last[tall:]
     eighth = HD // 2
     n_small = n_lat // 8

time: 236 us -> 214 us (0.907)
  waiting for transfers between devices: 87.7 us -> 64.6 us
  starting transfers between devices: 59 us -> 67.7 us
  local copies, waits for them, and re-layouts: 16.5 us -> 12.9 us
    ppermute x4 -> x2, waiting for transfers between devices: 15 us -> 0.01 us  [home(): return lax.ppermute(value, ('c', 'z'), pairs)]
    ppermute x36 -> x35, starting transfers between devices: 20.7 us -> 30.6 us  [swap(): return lax.ppermute(value, axis, [(0, 1), (1, 0)])]
    ppermute x3, waiting for transfers between devices: 6.38 us -> 0.63 us  [corner(): return lax.ppermute(value, ('z', 'y'), [(i, i ^ 3) for i in range(8)])]
    ppermute x36 -> x35, waiting for transfers between devices: 33 us -> 27.7 us  [swap(): return lax.ppermute(value, axis, [(0, 1), (1, 0)])]
    ppermute x1, waiting for transfers between devices: 0.01 us -> 5.19 us  [fast_body(): down_x = lax.ppermute(down_x, ('x', 'c', 'z'), pairs)]
    ppermute x4 -> x2, starting transfers between devices: 7.1 us -> 1.97 us  [home(): return lax.ppermute(value, ('c', 'z'), pairs)]
    ppermute x9 -> x10, waiting for transfers between devices: 26.1 us -> 22 us  [hop(): return lax.ppermute(value, 'z', [(i, i ^ k) for i in range(4)])]
    ppermute x9 -> x10, starting transfers between devices: 13.9 us -> 17 us  [hop(): return lax.ppermute(value, 'z', [(i, i ^ k) for i in range(4)])]
  transfers between devices with their start and end apart: 62 -> 60, of which waited for: 22 -> 14; matrix products, arithmetic and copies ran while one was open for 5% -> 4% of each run, Pallas kernels for 18% -> 22%
where the time goes in v3:
time: 214 us; the launch traced here: 211 us
  starting transfers between devices  67.7 us (32%)
  waiting for transfers between devices  64.6 us (30%)
  Pallas kernels  56.8 us (27%)
  local copies, waits for them, and re-layouts  12.9 us (6%)
  other arithmetic  6.89 us (3%)
  between operations  2.23 us (1%)
    pallas_call x20, Pallas kernels, run(): pl.pallas_call(body, in_specs=[pl.BlockSpec(memory_space=pltpu.SMEM)] * n...  56.8 us
    ppermute x35, starting transfers between devices, swap(): return lax.ppermute(value, axis, [(0, 1), (1, 0)])  30.6 us
    ppermute x35, waiting for transfers between devices, swap(): return lax.ppermute(value, axis, [(0, 1), (1, 0)])  27.7 us
    ppermute x10, waiting for transfers between devices, hop(): return lax.ppermute(value, 'z', [(i, i ^ k) for i in range(4)])  22 us
    ppermute x10, starting transfers between devices, hop(): return lax.ppermute(value, 'z', [(i, i ^ k) for i in range(4)])  17 us
    unnamed x155, local copies, waits for them, and re-layouts  10.5 us
    ppermute x7, starting transfers between devices, ring(): return lax.ppermute(value, ('z', 'y'), pairs)  9.22 us
    ppermute x7, waiting for transfers between devices, ring(): return lax.ppermute(value, ('z', 'y'), pairs)  9.11 us
  transfers between devices with their start and end apart: 60, of which 14 were waited for; matrix products, arithmetic and copies ran while one was open for 4% of the time, Pallas kernels for 22%

profile of v3, /device:TPU:0, one launch (start us, length us, event | category | flops | bytes accessed | tf_op | source)
XLA Modules:
  0.0 211.1 jit_solution(316829508289345042)
XLA Ops:
  0.7 3.1 %collective-permute-start = (bf16[128,1024]{1,0:T(8,128)(2,1)}, bf16[128,1024]{1,0:T(8,128)(2,1)S(1)}, u32[]{:S(2)}, u32[]{:S(2)}) collective-permute-start(bf16[128,1024]{1,0:T(8,128)(2,1)} %refs_6_.3), channel_id=1, source_target_pairs={{0,2},{2,4},{4,6},{6,7},{7,5},{5,3},{3,1},{1,0},{8,10},{10,12},{12... | collective-permute-start | bytes 786440 | tf_op jit(solution)/shard_map/ppermute | solution.py:881
  21.6 2.7 %shard_map.222 = (bf16[256,768]{1,0:T(8,128)(2,1)S(1)}, bf16[256,768]{1,0:T(8,128)(2,1)S(1)}, bf16[512,768]{1,0:T(8,128)(2,1)}) custom-call(s32[26]{0:T(128)S(1)} %stack.107.refs_0_, bf16[256,2816]{1,0:T(8,128)(2,1)S(1)} %copy-done.29, bf16[256,2816]{1,0:T(8,128)(2,1)S(1)} %copy-done.30, bf16[256,1]{1,0:T(8,128)(2,1)S(1)} %broadcast_in_dim.6.refs_3_, ...), custom_call_target="tpu_custom_call" | custom-call | flops 1 | tf_op jit(solution)/shard_map/pallas_call | solution.py:447
  27.8 8.4 %collective-permute-done.8.refs_3_.refs_5_.refs_9_ = bf16[256,1024]{1,0:T(8,128)(2,1)S(1)} collective-permute-done((bf16[256,1024]{1,0:T(8,128)(2,1)}, bf16[256,1024]{1,0:T(8,128)(2,1)S(1)}, u32[]{:S(2)}, u32[]{:S(2)}) %collective-permute-start.8) | collective-permute-done | bytes 524320 | tf_op jit(solution)/shard_map/ppermute | solution.py:846
  38.3 2.1 collective-permute-start.10
  40.5 6.9 %collective-permute-done.10.refs_0_ = bf16[128,1024]{1,0:T(8,128)(2,1)S(1)} collective-permute-done((bf16[128,1024]{1,0:T(8,128)(2,1)S(1)}, bf16[128,1024]{1,0:T(8,128)(2,1)S(1)}, u32[]{:S(2)}, u32[]{:S(2)}) %collective-permute-start.10) | collective-permute-done | bytes 262176 | tf_op jit(solution)/shard_map/ppermute | solution.py:881
  56.5 12.7 %shard_map.227 = (bf16[128,1024]{1,0:T(8,128)(2,1)}, bf16[2048,1024]{1,0:T(8,128)(2,1)}, bf16[2048,256]{1,0:T(8,128)(2,1)}, bf16[2048,256]{1,0:T(8,128)(2,1)}, b...) custom-call(s32[26]{0:T(128)} %copy-done.64, ...), custom_call_target="tpu_custom_call" | custom-call | flops 1 | tf_op jit(solution)/shard_map/pallas_call | solution.py:447
  72.6 3.1 %collective-permute-start.24 = (bf16[352,1024]{1,0:T(8,128)(2,1)S(1)}, bf16[352,1024]{1,0:T(8,128)(2,1)S(1)}, u32[]{:S(2)}, u32[]{:S(2)}) collective-permute-start(bf16[352,1024]{1,0:T(8,128)(2,1)S(1)} %shard_map.229), channel_id=1, source_target_pairs={{16,8},{26,10},{20,12},{30,14},{0,16},{10,18},{4,20},{14,22},{17,9... | collective-permute-start | bytes 2162696 | tf_op jit(solution)/shard_map/ppermute | solution.py:933
  76.8 2.4 %collective-permute-start.29 = (bf16[128,1024]{1,0:T(8,128)(2,1)S(1)}, bf16[128,1024]{1,0:T(8,128)(2,1)S(1)}, u32[]{:S(2)}, u32[]{:S(2)}) collective-permute-start(bf16[128,1024]{1,0:T(8,128)(2,1)S(1)} %get-tuple-element.128.refs_1_.refs_0_.refs_9_), channel_id=1, source_target_pairs={{0,3},{1,2},{2,1},{3,0},{4,7},{5,6},{6,5},{7,4},{8,11},{9,10},{10,... | collective-permute-start | bytes 786440 | tf_op jit(solution)/shard_map/ppermute | solution.py:854
  79.2 5.2 %collective-permute-done.24.refs_5_ = bf16[352,1024]{1,0:T(8,128)(2,1)S(1)} collective-permute-done((bf16[352,1024]{1,0:T(8,128)(2,1)S(1)}, bf16[352,1024]{1,0:T(8,128)(2,1)S(1)}, u32[]{:S(2)}, u32[]{:S(2)}) %collective-permute-start.24) | collective-permute-done | bytes 720928 | tf_op jit(solution)/shard_map/ppermute | solution.py:933
  94.9 2.7 %shard_map.237 = (bf16[256,384]{1,0:T(8,128)(2,1)S(1)}, bf16[256,768]{1,0:T(8,128)(2,1)S(1)}, f32[128,1024]{1,0:T(8,128)S(1)}, f32[128,1024]{1,0:T(8,128)S(1)}, bf16[256,1024]{1,0:T(8,128)(2,1)S(1)}) custom-call(bf16[128,1024]{1,0:T(8,128)(2,1)S(1)} %shard_map.236.refs_0_.refs_21_, bf16[128,1024]{1,0:T(8,128)(2,1)S(1)} %collective-permute-done.30.refs_1_.refs_22_, ...), custom_call_target="tpu_custom_call" | custom-call | flops 1 | tf_op jit(solution)/shard_map/pallas_call | solution.py:447
  97.7 3.9 %shard_map.239 = (bf16[704,512]{1,0:T(8,128)(2,1)S(1)}, bf16[704,512]{1,0:T(8,128)(2,1)S(1)}, bf16[352,512]{1,0:T(8,128)(2,1)}, bf16[352,512]{1,0:T(8,128)(2,1)S(1)}) custom-call(s32[26]{0:T(128)S(1)} %copy-done.65, bf16[256,384]{1,0:T(8,128)(2,1)S(1)} %get-tuple-element.134.refs_1_.refs_6_, bf16[256,384]{1,0:T(8,128)(2,1)S(1)} %get-tuple-element.138.refs_6_.refs_2_, ...), custom_call_target="tpu_custom_call" | custom-call | flops 1 | tf_op jit(solution)/shard_map/pallas_call | solution.py:447
  106.8 13.4 %collective-permute-done.38.refs_11_.refs_9_.refs_1_ = bf16[704,512]{1,0:T(8,128)(2,1)S(1)} collective-permute-done((bf16[704,512]{1,0:T(8,128)(2,1)S(1)}, bf16[704,512]{1,0:T(8,128)(2,1)S(1)}, u32[]{:S(2)}, u32[]{:S(2)}) %collective-permute-start.38) | collective-permute-done | bytes 720928 | tf_op jit(solution)/shard_map/ppermute | solution.py:846
  120.3 2.3 %shard_map.240 = (f32[128,1024]{1,0:T(8,128)S(1)}, bf16[128,1024]{1,0:T(8,128)(2,1)S(1)}, bf16[128,1024]{1,0:T(8,128)(2,1)S(1)}, f32[8,1024]{1,0:T(8,128)S(1)}) custom-call(s32[26]{0:T(128)S(1)} %copy-done.65, f32[128,1024]{1,0:T(8,128)S(1)} %get-tuple-element.150.refs_1_, bf16[128,1024]{1,0:T(8,128)(2,1)S(1)} %collective-permute-done.35.refs_2_, ...), custom_call_target="tpu_custom_call" | custom-call | flops 1 | tf_op jit(solution)/shard_map/pallas_call | solution.py:447
  127.7 8.9 %shard_map.244 = (bf16[1024,512]{1,0:T(8,128)(2,1)S(1)}, bf16[512,640]{1,0:T(8,128)(2,1)S(1)}, bf16[512,640]{1,0:T(8,128)(2,1)S(1)}, bf16[128,1024]{1,0:T(8,128)(2,1)S(1)}, bf16[4,8,64,256]{3,2,1,0:T(8,128)(2,1)S(1)}) custom-call(s32[26]{0:T(128)S(1)} %copy-done.65, bf16[128,1024]{1,0:T(8,128)(2,1)S(1)} %get-tuple-element.166.refs_1_, ...), custom_call_target="tpu_custom_call" | custom-call | flops 1 | tf_op jit(solution)/shard_map/pallas_call | solution.py:447
  136.7 3.6 %shard_map.245 = (f32[128,1024]{1,0:T(8,128)S(1)}, bf16[2,8,144,256]{3,2,1,0:T(8,128)(2,1)S(1)}, bf16[2,8,144,256]{3,2,1,0:T(8,128)(2,1)S(1)}) custom-call(s32[26]{0:T(128)S(1)} %copy-done.65, bf16[1024,512]{1,0:T(8,128)(2,1)S(1)} %get-tuple-element.174.refs_1_, bf16[1024,1024]{1,0:T(8,128)(2,1)S(1)} %copy-done.3, bf16[512,1024]{1,0:T(8,128)(2,1)S(1)} %copy-done.11, ...), custom_call_target="tpu_custom_call" | custom-call | flops 1 | tf_op jit(solution)/shard_map/pallas_call | solution.py:447
  142.5 5.5 %collective-permute-start.46 = (bf16[2,8,144,256]{3,2,1,0:T(8,128)(2,1)S(1)}, bf16[2,8,144,256]{3,2,1,0:T(8,128)(2,1)S(1)}, u32[]{:S(2)}, u32[]{:S(2)}) collective-permute-start(bf16[2,8,144,256]{3,2,1,0:T(8,128)(2,1)S(1)} %get-tuple-element.190), channel_id=1, source_target_pairs={{0,8},{8,0},{1,9},{9,1},{2,10},{10,2},{3,11},{11,3},{4,12},{12,4},... | collective-permute-start | bytes 3538952 | tf_op jit(solution)/shard_map/ppermute | solution.py:846
  151.6 10.0 %collective-permute-done.43.refs_7_ = bf16[128,1024]{1,0:T(8,128)(2,1)S(1)} collective-permute-done((bf16[128,1024]{1,0:T(8,128)(2,1)S(1)}, bf16[128,1024]{1,0:T(8,128)(2,1)S(1)}, u32[]{:S(2)}, u32[]{:S(2)}) %collective-permute-start.43) | collective-permute-done | bytes 262176 | tf_op jit(solution)/shard_map/ppermute | solution.py:850
  171.2 3.7 %collective-permute-start.49 = (bf16[128,768]{1,0:T(8,128)(2,1)}, bf16[128,768]{1,0:T(8,128)(2,1)}, u32[]{:S(2)}, u32[]{:S(2)}) collective-permute-start(bf16[128,768]{1,0:T(8,128)(2,1)} %get-tuple-element.194), channel_id=1, source_target_pairs={{0,4},{2,6},{4,0},{6,2},{1,5},{3,7},{5,1},{7,3},{8,12},{10,14},{12... | collective-permute-start | bytes 589832 | tf_op jit(solution)/shard_map/ppermute | solution.py:850
  174.9 4.8 %collective-permute-start.50 = (bf16[128,768]{1,0:T(8,128)(2,1)}, bf16[128,768]{1,0:T(8,128)(2,1)}, u32[]{:S(2)}, u32[]{:S(2)}) collective-permute-start(bf16[128,768]{1,0:T(8,128)(2,1)} %get-tuple-element.195), channel_id=1, source_target_pairs={{0,6},{2,4},{4,2},{6,0},{1,7},{3,5},{5,3},{7,1},{8,14},{10,12},{12... | collective-permute-start | bytes 589832 | tf_op jit(solution)/shard_map/ppermute | solution.py:850
  179.6 9.1 %collective-permute-done.49.refs_5_.refs_4_.refs_2_ = bf16[128,768]{1,0:T(8,128)(2,1)} collective-permute-done((bf16[128,768]{1,0:T(8,128)(2,1)}, bf16[128,768]{1,0:T(8,128)(2,1)}, u32[]{:S(2)}, u32[]{:S(2)}) %collective-permute-start.49) | collective-permute-done | bytes 196640 | tf_op jit(solution)/shard_map/ppermute | solution.py:850
  191.4 2.9 %collective-permute-start.56 = (bf16[272,256]{1,0:T(8,128)(2,1)S(1)}, bf16[272,256]{1,0:T(8,128)(2,1)S(1)}, u32[]{:S(2)}, u32[]{:S(2)}) collective-permute-start(bf16[272,256]{1,0:T(8,128)(2,1)S(1)} %get-tuple-element.206), channel_id=1, source_target_pairs={{0,6},{2,4},{4,2},{6,0},{1,7},{3,5},{5,3},{7,1},{8,14},{10,12},{12... | collective-permute-start | bytes 417800 | tf_op jit(solution)/shard_map/ppermute | solution.py:850
  197.0 2.1 %shard_map.251 = (bf16[256,128]{1,0:T(8,128)(2,1)S(1)}, bf16[1184,256]{1,0:T(8,128)(2,1)S(1)}, bf16[256,128]{1,0:T(8,128)(2,1)S(1)}, bf16[256,128]{1,0:T(8,128)(2,1)S(1)}) custom-call(s32[26]{0:T(128)S(1)} %copy-done.65, bf16[1024,1024]{1,0:T(8,128)(2,1)S(1)} %copy-done.3, bf16[128,768]{1,0:T(8,128)(2,1)S(1)} %copy-done.48, ...), custom_call_target="tpu_custom_call" | custom-call | flops 1 | tf_op jit(solution)/shard_map/pallas_call | solution.py:447
  200.2 2.2 %shard_map.252 = bf16[128,1024]{1,0:T(8,128)(2,1)} custom-call(bf16[128,768]{1,0:T(8,128)(2,1)S(1)} %copy-done.48, bf16[128,768]{1,0:T(8,128)(2,1)S(1)} %collective-permute-done.48.refs_4_.refs_3_.refs_1_, bf16[128,768]{1,0:T(8,128)(2,1)} %collective-permute-done.49.refs_5_.refs_4_.refs_2_, bf16[128,768]{1,0:T(8,128)(2,1)} %collective-permute-done.50.refs_6_.refs_5_.refs_3_, ...), custom_call_target="tpu_custom_call" | custom-call | flops 1 | tf_op jit(solution)/shard_map/pallas_call | solution.py:447
  203.4 2.9 %collective-permute-done.55 = bf16[272,256]{1,0:T(8,128)(2,1)S(1)} collective-permute-done((bf16[272,256]{1,0:T(8,128)(2,1)S(1)}, bf16[272,256]{1,0:T(8,128)(2,1)S(1)}, u32[]{:S(2)}, u32[]{:S(2)}) %collective-permute-start.55) | collective-permute-done | bytes 139296 | tf_op jit(solution)/shard_map/ppermute | solution.py:850
  (304 shorter events, 84.4 us)
Async XLA Ops:
  38.1 12.9 %collective-permute-start.15 = (bf16[256,1536]{1,0:T(8,128)(2,1)S(1)}, bf16[256,1536]{1,0:T(8,128)(2,1)S(1)}, u32[]{:S(2)}, u32[]{:S(2)}) collective-permute-start(bf16[256,1536]{1,0:T(8,128)(2,1)S(1)} %get-tuple-element.123.refs_14_), channel_id=1, source_target_pairs={{0,8},{8,0},{1,9},{9,1},{2,10},{10,2},{3,11},{11,3},{4,12},{12,4},... | collective-permute-start | bytes 2359304 | tf_op jit(solution)/shard_map/ppermute | solution.py:846
  49.3 20.0 %collective-permute-start.22 = (bf16[512,768]{1,0:T(8,128)(2,1)}, bf16[512,768]{1,0:T(8,128)(2,1)}, u32[]{:S(2)}, u32[]{:S(2)}) collective-permute-start(bf16[512,768]{1,0:T(8,128)(2,1)} %get-tuple-element.126), channel_id=1, source_target_pairs={{0,16},{16,0},{1,17},{17,1},{2,18},{18,2},{3,19},{19,3},{4,20},{20... | collective-permute-start | bytes 2359304 | tf_op jit(solution)/shard_map/ppermute | solution.py:846
  50.9 18.3 %collective-permute-start.18 = (bf16[256,1024]{1,0:T(8,128)(2,1)}, bf16[256,1024]{1,0:T(8,128)(2,1)}, u32[]{:S(2)}, u32[]{:S(2)}) collective-permute-start(bf16[256,1024]{1,0:T(8,128)(2,1)} %shard_map.224), channel_id=1, source_target_pairs={{0,8},{8,0},{1,9},{9,1},{2,10},{10,2},{3,11},{11,3},{4,12},{12,4},... | collective-permute-start | bytes 1572872 | tf_op jit(solution)/shard_map/ppermute | solution.py:846
  51.0 18.2 %collective-permute-start.19 = (bf16[128,1024]{1,0:T(8,128)(2,1)S(1)}, bf16[128,1024]{1,0:T(8,128)(2,1)S(1)}, u32[]{:S(2)}, u32[]{:S(2)}) collective-permute-start(bf16[128,1024]{1,0:T(8,128)(2,1)S(1)} %get-tuple-element.125.refs_10_.refs_2_.refs_11_), channel_id=1, source_target_pairs={{0,2},{2,0},{4,6},{6,4},{1,3},{3,1},{5,7},{7,5},{8,10},{10,8},{12,... | collective-permute-start | bytes 786440 | tf_op jit(solution)/shard_map/ppermute | solution.py:850
  52.6 16.6 %collective-permute-start.20 = (bf16[128,1024]{1,0:T(8,128)(2,1)S(1)}, bf16[128,1024]{1,0:T(8,128)(2,1)S(1)}, u32[]{:S(2)}, u32[]{:S(2)}) collective-permute-start(bf16[128,1024]{1,0:T(8,128)(2,1)S(1)} %get-tuple-element.125.refs_10_.refs_2_.refs_11_), channel_id=1, source_target_pairs={{0,1},{1,0},{2,3},{3,2},{4,5},{5,4},{6,7},{7,6},{8,9},{9,8},{10,11... | collective-permute-start | bytes 786440 | tf_op jit(solution)/shard_map/ppermute | solution.py:846
  54.7 14.5 %collective-permute-start.21 = (bf16[128,1024]{1,0:T(8,128)(2,1)S(1)}, bf16[128,1024]{1,0:T(8,128)(2,1)}, u32[]{:S(2)}, u32[]{:S(2)}) collective-permute-start(bf16[128,1024]{1,0:T(8,128)(2,1)S(1)} %get-tuple-element.125.refs_10_.refs_2_.refs_11_), channel_id=1, source_target_pairs={{0,3},{1,2},{2,1},{3,0},{4,7},{5,6},{6,5},{7,4},{8,11},{9,10},{10,... | collective-permute-start | bytes 786440 | tf_op jit(solution)/shard_map/ppermute | solution.py:854
  76.8 12.6 %collective-permute-start.25 = (bf16[128,1024]{1,0:T(8,128)(2,1)S(1)}, bf16[128,1024]{1,0:T(8,128)(2,1)S(1)}, u32[]{:S(2)}, u32[]{:S(2)}) collective-permute-start(bf16[128,1024]{1,0:T(8,128)(2,1)S(1)} %get-tuple-element.128.refs_1_.refs_0_.refs_9_), channel_id=1, source_target_pairs={{0,2},{2,0},{4,6},{6,4},{1,3},{3,1},{5,7},{7,5},{8,10},{10,8},{12,... | collective-permute-start | bytes 786440 | tf_op jit(solution)/shard_map/ppermute | solution.py:850
  76.8 13.3 %collective-permute-start.29 = (bf16[128,1024]{1,0:T(8,128)(2,1)S(1)}, bf16[128,1024]{1,0:T(8,128)(2,1)S(1)}, u32[]{:S(2)}, u32[]{:S(2)}) collective-permute-start(bf16[128,1024]{1,0:T(8,128)(2,1)S(1)} %get-tuple-element.128.refs_1_.refs_0_.refs_9_), channel_id=1, source_target_pairs={{0,3},{1,2},{2,1},{3,0},{4,7},{5,6},{6,5},{7,4},{8,11},{9,10},{10,... | collective-permute-start | bytes 786440 | tf_op jit(solution)/shard_map/ppermute | solution.py:854
  101.6 18.5 %collective-permute-start.38 = (bf16[704,512]{1,0:T(8,128)(2,1)S(1)}, bf16[704,512]{1,0:T(8,128)(2,1)S(1)}, u32[]{:S(2)}, u32[]{:S(2)}) collective-permute-start(bf16[704,512]{1,0:T(8,128)(2,1)S(1)} %get-tuple-element.159), channel_id=1, source_target_pairs={{0,16},{16,0},{1,17},{17,1},{2,18},{18,2},{3,19},{19,3},{4,20},{20... | collective-permute-start | bytes 2162696 | tf_op jit(solution)/shard_map/ppermute | solution.py:846
  103.2 17.0 %collective-permute-start.35 = (bf16[128,1024]{1,0:T(8,128)(2,1)S(1)}, bf16[128,1024]{1,0:T(8,128)(2,1)S(1)}, u32[]{:S(2)}, u32[]{:S(2)}) collective-permute-start(bf16[128,1024]{1,0:T(8,128)(2,1)S(1)} %get-tuple-element.151), channel_id=1, source_target_pairs={{0,1},{1,0},{2,3},{3,2},{4,5},{5,4},{6,7},{7,6},{8,9},{9,8},{10,11... | collective-permute-start | bytes 786440 | tf_op jit(solution)/shard_map/ppermute | solution.py:846
  104.6 15.6 %collective-permute-start.36 = (bf16[128,1024]{1,0:T(8,128)(2,1)S(1)}, bf16[128,1024]{1,0:T(8,128)(2,1)S(1)}, u32[]{:S(2)}, u32[]{:S(2)}) collective-permute-start(bf16[128,1024]{1,0:T(8,128)(2,1)S(1)} %get-tuple-element.152), channel_id=1, source_target_pairs={{0,2},{2,0},{4,6},{6,4},{1,3},{3,1},{5,7},{7,5},{8,10},{10,8},{12,... | collective-permute-start | bytes 786440 | tf_op jit(solution)/shard_map/ppermute | solution.py:850
  106.1 14.1 %collective-permute-start.37 = (bf16[128,1024]{1,0:T(8,128)(2,1)S(1)}, bf16[128,1024]{1,0:T(8,128)(2,1)S(1)}, u32[]{:S(2)}, u32[]{:S(2)}) collective-permute-start(bf16[128,1024]{1,0:T(8,128)(2,1)S(1)} %get-tuple-element.153), channel_id=1, source_target_pairs={{0,3},{1,2},{2,1},{3,0},{4,7},{5,6},{6,5},{7,4},{8,11},{9,10},{10,... | collective-permute-start | bytes 786440 | tf_op jit(solution)/shard_map/ppermute | solution.py:854
  123.9 16.5 %collective-permute-start.41 = (bf16[2,1024,256]{2,1,0:T(8,128)(2,1)S(1)}, bf16[2,1024,256]{2,1,0:T(8,128)(2,1)}, u32[]{:S(2)}, u32[]{:S(2)}) collective-permute-start(bf16[2,1024,256]{2,1,0:T(8,128)(2,1)S(1)} %get-tuple-element.161.refs_1_.refs_10_.refs_2_), channel_id=1, source_target_pairs={{0,8},{8,0},{1,9},{9,1},{2,10},{10,2},{3,11},{11,3},{4,12},{12,4},... | collective-permute-start | bytes 3145736 | tf_op jit(solution)/shard_map/ppermute | solution.py:846
  124.2 16.2 %collective-permute-start.42 = (bf16[704,512]{1,0:T(8,128)(2,1)S(1)}, bf16[704,512]{1,0:T(8,128)(2,1)S(1)}, u32[]{:S(2)}, u32[]{:S(2)}) collective-permute-start(bf16[704,512]{1,0:T(8,128)(2,1)S(1)} %shard_map.246), channel_id=1, source_target_pairs={{0,0},{2,2},{4,8},{6,10},{8,4},{10,6},{12,12},{14,14},{1,1},{3,3},... | collective-permute-start | bytes 2162696 | tf_op jit(solution)/shard_map/ppermute | solution.py:977
  125.3 15.1 %collective-permute-start.39 = (bf16[256,1024]{1,0:T(8,128)(2,1)S(1)}, bf16[256,1024]{1,0:T(8,128)(2,1)S(1)}, u32[]{:S(2)}, u32[]{:S(2)}) collective-permute-start(bf16[256,1024]{1,0:T(8,128)(2,1)S(1)} %shard_map.242), channel_id=1, source_target_pairs={{0,1},{1,0},{2,3},{3,2},{4,5},{5,4},{6,7},{7,6},{8,9},{9,8},{10,11... | collective-permute-start | bytes 1572872 | tf_op jit(solution)/shard_map/ppermute | solution.py:846
  126.7 13.7 %collective-permute-start.40 = (bf16[352,512]{1,0:T(8,128)(2,1)}, bf16[352,512]{1,0:T(8,128)(2,1)}, u32[]{:S(2)}, u32[]{:S(2)}) collective-permute-start(bf16[352,512]{1,0:T(8,128)(2,1)} %shard_map.243), channel_id=1, source_target_pairs={{0,16},{16,0},{1,17},{17,1},{2,18},{18,2},{3,19},{19,3},{4,20},{20... | collective-permute-start | bytes 1081352 | tf_op jit(solution)/shard_map/ppermute | solution.py:846
  142.5 22.2 %collective-permute-start.46 = (bf16[2,8,144,256]{3,2,1,0:T(8,128)(2,1)S(1)}, bf16[2,8,144,256]{3,2,1,0:T(8,128)(2,1)S(1)}, u32[]{:S(2)}, u32[]{:S(2)}) collective-permute-start(bf16[2,8,144,256]{3,2,1,0:T(8,128)(2,1)S(1)} %get-tuple-element.190), channel_id=1, source_target_pairs={{0,8},{8,0},{1,9},{9,1},{2,10},{10,2},{3,11},{11,3},{4,12},{12,4},... | collective-permute-start | bytes 3538952 | tf_op jit(solution)/shard_map/ppermute | solution.py:846
  148.0 16.7 %collective-permute-start.44 = (bf16[512,640]{1,0:T(8,128)(2,1)S(1)}, bf16[512,640]{1,0:T(8,128)(2,1)S(1)}, u32[]{:S(2)}, u32[]{:S(2)}) collective-permute-start(bf16[512,640]{1,0:T(8,128)(2,1)S(1)} %get-tuple-element.187), channel_id=1, source_target_pairs={{0,1},{1,0},{2,3},{3,2},{4,5},{5,4},{6,7},{7,6},{8,9},{9,8},{10,11... | collective-permute-start | bytes 1966088 | tf_op jit(solution)/shard_map/ppermute | solution.py:846
  149.3 13.6 %collective-permute-start.45 = (bf16[1024,256]{1,0:T(8,128)(2,1)S(1)}, bf16[1024,256]{1,0:T(8,128)(2,1)S(1)}, u32[]{:S(2)}, u32[]{:S(2)}) collective-permute-start(bf16[1024,256]{1,0:T(8,128)(2,1)S(1)} %get-tuple-element.186.refs_2_), channel_id=1, source_target_pairs={{0,16},{16,0},{1,17},{17,1},{2,18},{18,2},{3,19},{19,3},{4,20},{20... | collective-permute-start | bytes 1572872 | tf_op jit(solution)/shard_map/ppermute | solution.py:846
  167.4 21.3 %collective-permute-start.51 = (bf16[1088,256]{1,0:T(8,128)(2,1)}, bf16[1088,256]{1,0:T(8,128)(2,1)}, u32[]{:S(2)}, u32[]{:S(2)}) collective-permute-start(bf16[1088,256]{1,0:T(8,128)(2,1)} %get-tuple-element.199), channel_id=1, source_target_pairs={{0,1},{1,0},{2,3},{3,2},{4,5},{5,4},{6,7},{7,6},{8,9},{9,8},{10,11... | collective-permute-start | bytes 1671176 | tf_op jit(solution)/shard_map/ppermute | solution.py:846
  169.1 19.7 %collective-permute-start.52 = (bf16[576,256]{1,0:T(8,128)(2,1)}, bf16[576,256]{1,0:T(8,128)(2,1)}, u32[]{:S(2)}, u32[]{:S(2)}) collective-permute-start(bf16[576,256]{1,0:T(8,128)(2,1)} %get-tuple-element.200), channel_id=1, source_target_pairs={{0,16},{16,0},{1,17},{17,1},{2,18},{18,2},{3,19},{19,3},{4,20},{20... | collective-permute-start | bytes 884744 | tf_op jit(solution)/shard_map/ppermute | solution.py:846
  170.0 18.7 %collective-permute-start.53 = (bf16[576,256]{1,0:T(8,128)(2,1)}, bf16[576,256]{1,0:T(8,128)(2,1)}, u32[]{:S(2)}, u32[]{:S(2)}) collective-permute-start(bf16[576,256]{1,0:T(8,128)(2,1)} %get-tuple-element.201), channel_id=1, source_target_pairs={{0,17},{1,16},{16,1},{17,0},{2,19},{3,18},{18,3},{19,2},{4,21},{5,... | collective-permute-start | bytes 884744 | tf_op jit(solution)/shard_map/ppermute | solution.py:1017
  171.2 17.6 %collective-permute-start.49 = (bf16[128,768]{1,0:T(8,128)(2,1)}, bf16[128,768]{1,0:T(8,128)(2,1)}, u32[]{:S(2)}, u32[]{:S(2)}) collective-permute-start(bf16[128,768]{1,0:T(8,128)(2,1)} %get-tuple-element.194), channel_id=1, source_target_pairs={{0,4},{2,6},{4,0},{6,2},{1,5},{3,7},{5,1},{7,3},{8,12},{10,14},{12... | collective-permute-start | bytes 589832 | tf_op jit(solution)/shard_map/ppermute | solution.py:850
  174.9 13.9 %collective-permute-start.50 = (bf16[128,768]{1,0:T(8,128)(2,1)}, bf16[128,768]{1,0:T(8,128)(2,1)}, u32[]{:S(2)}, u32[]{:S(2)}) collective-permute-start(bf16[128,768]{1,0:T(8,128)(2,1)} %get-tuple-element.195), channel_id=1, source_target_pairs={{0,6},{2,4},{4,2},{6,0},{1,7},{3,5},{5,3},{7,1},{8,14},{10,12},{12... | collective-permute-start | bytes 589832 | tf_op jit(solution)/shard_map/ppermute | solution.py:850
  (112 other events, 951.0 us)

commit v4 on v3

--- a/solution.py
+++ b/solution.py
@@ -814,7 +814,7 @@
     go_far[...] = wide_sum(go_keep[1], go_there[1]).astype(BF)
 
 
-def exchange_kernel(keep, there, go_own, go_far, b_keep, b_there, p0, p1, p2, p3, b_x, b_xy, y_send, y_keep):
+def pieces_kernel(keep, there, p0, p1, p2, p3):
     rows, wide = p0.shape
     n = wide - 4 * HD
     for k, out in enumerate((p0, p1, p2, p3)):
@@ -822,6 +822,9 @@
         out[:, 0:n] = wide_sum(keep[band, 0:n], there[band, 0:n]).astype(BF)
         out[:, n : n + 2 * HD] = keep[band, n:]
         out[:, n + 2 * HD : wide] = there[band, n:]
+
+
+def exchange_kernel(go_own, go_far, b_keep, b_there, b_x, b_xy, y_send, y_keep):
     tall = b_keep.shape[2]
     for j in range(8):
         band = slice(j % 4 * tall, (j % 4 + 1) * tall)
@@ -966,7 +969,7 @@
     )
     y1_there = swap(y1_send, "x")
     dresid, dattn, dmixed, v_m = call(middle_kernel, 1, [((rows, d), F32), ((rows, d), BF), ((rows, QW), BF), ((8, d), F32)])(
-        idx, e_own, d_far, d_up, d_diag, resid, cotangent, *w_os, deps=(y1_there,)
+        idx, e_own, d_far, d_up, d_diag, resid, cotangent, *w_os
     )
 
     def home(value):
@@ -988,7 +991,7 @@
         [((HEADS * rows, keys), BF), ((HEADS * rows, LAT_HEAD), BF), ((HEADS * rows, LAT_HEAD), BF)],
         limit=40,
         far_in=range(1, 8),
-    )(idx, dmixed, queries, lat_all, w_key, w_value, probs, outs, qs, deps=(y1_there, go_send))
+    )(idx, dmixed, queries, lat_all, w_key, w_value, probs, outs, qs, deps=(go_send,))
     tall = HD + n_lat // 8 + 16
     e_q, b_send, b_keep = call(
         bundle_kernel,
@@ -1001,22 +1004,22 @@
     f2, go_own, go_far, o_send = call(eleventh_kernel, 0, [((ff8, 2 * shard), BF)] + [((QW, shard), BF)] * 2 + [((rows, d), BF)])(
         y2_keep, y2_there, go_keep, go_there, o_up, o_x, deps=(b_send, f1)
     )
-    b_send, p_send = through((b_send, p_send), (go_far,))
+    b_send = through((b_send,), (go_far,))[0]
     p_there = swap(p_send, "y")
     f2, o_there = home(f2), hop(o_send, 1)
     go_far, b_there = swap(go_far, "x"), swap(b_send, "c")
     flat = ((4 * tall, shard), BF)
     tower = ((4 * tall + QW // 2, shard), BF)
     n_p = n_lat + 4 * HD
-    shapes = [((rows, n_p), BF)] * 4 + [flat, flat, tower, tower]
-    p0, p1, p2, p3, b_x, b_xy, y_send, y_keep = call(exchange_kernel, 0, shapes)(
-        p_keep, p_there, go_own, go_far, b_keep, b_there, deps=(f2, o_there)
+    p0, p1, p2, p3 = call(pieces_kernel, 0, [((rows, n_p), BF)] * 4)(p_keep, p_there, deps=(b_there,))
+    b_x, b_xy, y_send, y_keep = call(exchange_kernel, 0, [flat, flat, tower, tower])(
+        go_own, go_far, b_keep, b_there, deps=(f2, o_there)
     )
     pieces = (p0, hop(p1, 1), hop(p2, 2), hop(p3, 3))
     b_x, y_there = swap(b_x, "x"), swap(y_send, "y")
     b_xy = lax.ppermute(b_xy, ("x", "y"), [(i, i ^ 3) for i in range(4)])
     z0, z1, z2, z3 = call(functools.partial(quarters_kernel, rows), 0, [((tall + rows, shard), BF)] * 4)(
-        y_keep, y_there, b_x, b_xy, deps=pieces[1:]
+        y_keep, y_there, b_x, b_xy
     )
     last = z0.astype(F32) + hop(z1, 1) + hop(z2, 2) + hop(z3, 3)
     quarter = ((shard, 2 * HD), BF)

time: 214 us -> 210 us (0.981)
  waiting for transfers between devices: 64.6 us -> 60.7 us
  starting transfers between devices: 67.7 us -> 64.1 us
    ppermute x10, waiting for transfers between devices: 22 us -> 15.3 us  [hop(): return lax.ppermute(value, 'z', [(i, i ^ k) for i in range(4)])]
    ppermute x35, waiting for transfers between devices: 27.7 us -> 22 us  [swap(): return lax.ppermute(value, axis, [(0, 1), (1, 0)])]
    ppermute x3, waiting for transfers between devices: 0.63 us -> 5.18 us  [corner(): return lax.ppermute(value, ('z', 'y'), [(i, i ^ 3) for i in range(8)])]
    ppermute x1, waiting for transfers between devices: 0.01 us -> 3.95 us  [fast_body(): b_xy = lax.ppermute(b_xy, ('x', 'y'), [(i, i ^ 3) for i in range(4)])]
    ppermute x10, starting transfers between devices: 17 us -> 14.6 us  [hop(): return lax.ppermute(value, 'z', [(i, i ^ k) for i in range(4)])]
    unnamed x155 -> x157, local copies, waits for them, and re-layouts: 10.5 us -> 12 us
    pallas_call x20 -> x21, Pallas kernels: 56.8 us -> 56.8 us  [run(): pl.pallas_call(body, in_specs=[pl.BlockSpec(memory_space=pltpu.SMEM)] * n...]
  transfers between devices with their start and end apart: 60 -> 60, of which waited for: 14 -> 16; matrix products, arithmetic and copies ran while one was open for 4% -> 5% of each run, Pallas kernels for 22% -> 26%
where the time goes in v4:
time: 210 us; the launch traced here: 206 us
  starting transfers between devices  64.1 us (31%)
  waiting for transfers between devices  60.7 us (29%)
  Pallas kernels  56.9 us (27%)
  local copies, waits for them, and re-layouts  14.5 us (7%)
  other arithmetic  7.92 us (4%)
  between operations  2.2 us (1%)
    pallas_call x21, Pallas kernels, run(): pl.pallas_call(body, in_specs=[pl.BlockSpec(memory_space=pltpu.SMEM)] * n...  56.8 us
    ppermute x35, starting transfers between devices, swap(): return lax.ppermute(value, axis, [(0, 1), (1, 0)])  28.7 us
    ppermute x35, waiting for transfers between devices, swap(): return lax.ppermute(value, axis, [(0, 1), (1, 0)])  22 us
    ppermute x10, waiting for transfers between devices, hop(): return lax.ppermute(value, 'z', [(i, i ^ k) for i in range(4)])  15.3 us
    ppermute x10, starting transfers between devices, hop(): return lax.ppermute(value, 'z', [(i, i ^ k) for i in range(4)])  14.6 us
    unnamed x157, local copies, waits for them, and re-layouts  12 us
    ppermute x7, starting transfers between devices, ring(): return lax.ppermute(value, ('z', 'y'), pairs)  9.22 us
    ppermute x7, waiting for transfers between devices, ring(): return lax.ppermute(value, ('z', 'y'), pairs)  9.11 us
  transfers between devices with their start and end apart: 60, of which 16 were waited for; matrix products, arithmetic and copies ran while one was open for 5% of the time, Pallas kernels for 26%

profile of v4, /device:TPU:0, one launch (start us, length us, event | category | flops | bytes accessed | tf_op | source)
XLA Modules:
  0.0 206.3 jit_solution(15508808346627182849)
XLA Ops:
  0.7 3.1 %collective-permute-start = (bf16[128,1024]{1,0:T(8,128)(2,1)}, bf16[128,1024]{1,0:T(8,128)(2,1)S(1)}, u32[]{:S(2)}, u32[]{:S(2)}) collective-permute-start(bf16[128,1024]{1,0:T(8,128)(2,1)} %refs_6_.3), channel_id=1, source_target_pairs={{0,2},{2,4},{4,6},{6,7},{7,5},{5,3},{3,1},{1,0},{8,10},{10,12},{12... | collective-permute-start | bytes 786440 | tf_op jit(solution)/shard_map/ppermute | solution.py:884
  21.7 2.7 %shard_map.222 = (bf16[256,768]{1,0:T(8,128)(2,1)S(1)}, bf16[256,768]{1,0:T(8,128)(2,1)S(1)}, bf16[512,768]{1,0:T(8,128)(2,1)}) custom-call(s32[26]{0:T(128)S(1)} %stack.107.refs_0_, bf16[256,2816]{1,0:T(8,128)(2,1)S(1)} %copy-done.29, bf16[256,2816]{1,0:T(8,128)(2,1)S(1)} %copy-done.30, bf16[256,1]{1,0:T(8,128)(2,1)S(1)} %broadcast_in_dim.6.refs_3_, ...), custom_call_target="tpu_custom_call" | custom-call | flops 1 | tf_op jit(solution)/shard_map/pallas_call | solution.py:447
  27.8 8.4 %collective-permute-done.8.refs_3_.refs_5_.refs_9_ = bf16[256,1024]{1,0:T(8,128)(2,1)S(1)} collective-permute-done((bf16[256,1024]{1,0:T(8,128)(2,1)}, bf16[256,1024]{1,0:T(8,128)(2,1)S(1)}, u32[]{:S(2)}, u32[]{:S(2)}) %collective-permute-start.8) | collective-permute-done | bytes 524320 | tf_op jit(solution)/shard_map/ppermute | solution.py:849
  40.5 6.9 %collective-permute-done.10.refs_0_ = bf16[128,1024]{1,0:T(8,128)(2,1)S(1)} collective-permute-done((bf16[128,1024]{1,0:T(8,128)(2,1)S(1)}, bf16[128,1024]{1,0:T(8,128)(2,1)S(1)}, u32[]{:S(2)}, u32[]{:S(2)}) %collective-permute-start.10) | collective-permute-done | bytes 262176 | tf_op jit(solution)/shard_map/ppermute | solution.py:884
  56.5 12.7 %shard_map.227 = (bf16[128,1024]{1,0:T(8,128)(2,1)}, bf16[2048,1024]{1,0:T(8,128)(2,1)}, bf16[2048,256]{1,0:T(8,128)(2,1)}, bf16[2048,256]{1,0:T(8,128)(2,1)}, b...) custom-call(s32[26]{0:T(128)} %copy-done.61, ...), custom_call_target="tpu_custom_call" | custom-call | flops 1 | tf_op jit(solution)/shard_map/pallas_call | solution.py:447
  72.6 3.0 %collective-permute-start.24 = (bf16[352,1024]{1,0:T(8,128)(2,1)S(1)}, bf16[352,1024]{1,0:T(8,128)(2,1)S(1)}, u32[]{:S(2)}, u32[]{:S(2)}) collective-permute-start(bf16[352,1024]{1,0:T(8,128)(2,1)S(1)} %shard_map.229), channel_id=1, source_target_pairs={{16,8},{26,10},{20,12},{30,14},{0,16},{10,18},{4,20},{14,22},{17,9... | collective-permute-start | bytes 2162696 | tf_op jit(solution)/shard_map/ppermute | solution.py:936
  76.9 2.3 %collective-permute-start.29 = (bf16[128,1024]{1,0:T(8,128)(2,1)S(1)}, bf16[128,1024]{1,0:T(8,128)(2,1)S(1)}, u32[]{:S(2)}, u32[]{:S(2)}) collective-permute-start(bf16[128,1024]{1,0:T(8,128)(2,1)S(1)} %get-tuple-element.126.refs_1_.refs_0_.refs_9_), channel_id=1, source_target_pairs={{0,3},{1,2},{2,1},{3,0},{4,7},{5,6},{6,5},{7,4},{8,11},{9,10},{10,... | collective-permute-start | bytes 786440 | tf_op jit(solution)/shard_map/ppermute | solution.py:857
  79.2 5.2 %collective-permute-done.24.refs_5_ = bf16[352,1024]{1,0:T(8,128)(2,1)S(1)} collective-permute-done((bf16[352,1024]{1,0:T(8,128)(2,1)S(1)}, bf16[352,1024]{1,0:T(8,128)(2,1)S(1)}, u32[]{:S(2)}, u32[]{:S(2)}) %collective-permute-start.24) | collective-permute-done | bytes 720928 | tf_op jit(solution)/shard_map/ppermute | solution.py:936
  94.8 2.7 %shard_map.237 = (bf16[256,384]{1,0:T(8,128)(2,1)S(1)}, bf16[256,768]{1,0:T(8,128)(2,1)S(1)}, f32[128,1024]{1,0:T(8,128)S(1)}, f32[128,1024]{1,0:T(8,128)S(1)}, bf16[256,1024]{1,0:T(8,128)(2,1)S(1)}) custom-call(bf16[128,1024]{1,0:T(8,128)(2,1)S(1)} %shard_map.236.refs_0_.refs_21_, bf16[128,1024]{1,0:T(8,128)(2,1)S(1)} %collective-permute-done.30.refs_1_.refs_22_, ...), custom_call_target="tpu_custom_call" | custom-call | flops 1 | tf_op jit(solution)/shard_map/pallas_call | solution.py:447
  97.7 3.9 %shard_map.242 = (bf16[704,512]{1,0:T(8,128)(2,1)S(1)}, bf16[704,512]{1,0:T(8,128)(2,1)S(1)}, bf16[352,512]{1,0:T(8,128)(2,1)}, bf16[352,512]{1,0:T(8,128)(2,1)S(1)}) custom-call(s32[26]{0:T(128)S(1)} %copy-done.62, bf16[256,384]{1,0:T(8,128)(2,1)S(1)} %get-tuple-element.132.refs_1_.refs_6_, bf16[256,384]{1,0:T(8,128)(2,1)S(1)} %get-tuple-element.136.refs_6_.refs_2_, ...), custom_call_target="tpu_custom_call" | custom-call | flops 1 | tf_op jit(solution)/shard_map/pallas_call | solution.py:447
  106.7 4.8 %collective-permute-done.35.refs_2_ = bf16[128,1024]{1,0:T(8,128)(2,1)S(1)} collective-permute-done((bf16[128,1024]{1,0:T(8,128)(2,1)S(1)}, bf16[128,1024]{1,0:T(8,128)(2,1)S(1)}, u32[]{:S(2)}, u32[]{:S(2)}) %collective-permute-start.35) | collective-permute-done | bytes 262176 | tf_op jit(solution)/shard_map/ppermute | solution.py:849
  111.5 2.2 %collective-permute-done.36.refs_3_ = bf16[128,1024]{1,0:T(8,128)(2,1)S(1)} collective-permute-done((bf16[128,1024]{1,0:T(8,128)(2,1)S(1)}, bf16[128,1024]{1,0:T(8,128)(2,1)S(1)}, u32[]{:S(2)}, u32[]{:S(2)}) %collective-permute-start.36) | collective-permute-done | bytes 262176 | tf_op jit(solution)/shard_map/ppermute | solution.py:853
  113.7 4.6 %collective-permute-done.37.refs_4_ = bf16[128,1024]{1,0:T(8,128)(2,1)S(1)} collective-permute-done((bf16[128,1024]{1,0:T(8,128)(2,1)S(1)}, bf16[128,1024]{1,0:T(8,128)(2,1)S(1)}, u32[]{:S(2)}, u32[]{:S(2)}) %collective-permute-start.37) | collective-permute-done | bytes 262176 | tf_op jit(solution)/shard_map/ppermute | solution.py:857
  118.3 2.3 %shard_map.239 = (f32[128,1024]{1,0:T(8,128)S(1)}, bf16[128,1024]{1,0:T(8,128)(2,1)S(1)}, bf16[128,1024]{1,0:T(8,128)(2,1)S(1)}, f32[8,1024]{1,0:T(8,128)S(1)}) custom-call(s32[26]{0:T(128)S(1)} %copy-done.62, f32[128,1024]{1,0:T(8,128)S(1)} %get-tuple-element.148.refs_1_, bf16[128,1024]{1,0:T(8,128)(2,1)S(1)} %collective-permute-done.35.refs_2_, ...), custom_call_target="tpu_custom_call" | custom-call | flops 1 | tf_op jit(solution)/shard_map/pallas_call | solution.py:447
  125.9 8.9 %shard_map.244 = (bf16[1024,512]{1,0:T(8,128)(2,1)S(1)}, bf16[512,640]{1,0:T(8,128)(2,1)S(1)}, bf16[512,640]{1,0:T(8,128)(2,1)S(1)}, bf16[128,1024]{1,0:T(8,128)(2,1)S(1)}, bf16[4,8,64,256]{3,2,1,0:T(8,128)(2,1)S(1)}) custom-call(s32[26]{0:T(128)S(1)} %copy-done.62, bf16[128,1024]{1,0:T(8,128)(2,1)S(1)} %get-tuple-element.163.refs_1_, ...), custom_call_target="tpu_custom_call" | custom-call | flops 1 | tf_op jit(solution)/shard_map/pallas_call | solution.py:447
  135.7 3.6 %shard_map.245 = (f32[128,1024]{1,0:T(8,128)S(1)}, bf16[2,8,144,256]{3,2,1,0:T(8,128)(2,1)S(1)}, bf16[2,8,144,256]{3,2,1,0:T(8,128)(2,1)S(1)}) custom-call(s32[26]{0:T(128)S(1)} %copy-done.62, bf16[1024,512]{1,0:T(8,128)(2,1)S(1)} %get-tuple-element.171.refs_1_, bf16[1024,1024]{1,0:T(8,128)(2,1)S(1)} %copy-done.3, bf16[512,1024]{1,0:T(8,128)(2,1)S(1)} %copy-done.11, ...), custom_call_target="tpu_custom_call" | custom-call | flops 1 | tf_op jit(solution)/shard_map/pallas_call | solution.py:447
  141.7 4.0 %collective-permute-start.45 = (bf16[2,8,144,256]{3,2,1,0:T(8,128)(2,1)S(1)}, bf16[2,8,144,256]{3,2,1,0:T(8,128)(2,1)S(1)}, u32[]{:S(2)}, u32[]{:S(2)}) collective-permute-start(bf16[2,8,144,256]{3,2,1,0:T(8,128)(2,1)S(1)} %shard_map.248), channel_id=1, source_target_pairs={{0,8},{8,0},{1,9},{9,1},{2,10},{10,2},{3,11},{11,3},{4,12},{12,4},... | collective-permute-start | bytes 3538952 | tf_op jit(solution)/shard_map/ppermute | solution.py:849
  149.9 11.3 %collective-permute-done.43.refs_5_ = bf16[128,1024]{1,0:T(8,128)(2,1)S(1)} collective-permute-done((bf16[128,1024]{1,0:T(8,128)(2,1)S(1)}, bf16[128,1024]{1,0:T(8,128)(2,1)S(1)}, u32[]{:S(2)}, u32[]{:S(2)}) %collective-permute-start.43) | collective-permute-done | bytes 262176 | tf_op jit(solution)/shard_map/ppermute | solution.py:853
  168.3 3.5 %collective-permute-start.47 = (bf16[128,768]{1,0:T(8,128)(2,1)}, bf16[128,768]{1,0:T(8,128)(2,1)S(1)}, u32[]{:S(2)}, u32[]{:S(2)}) collective-permute-start(bf16[128,768]{1,0:T(8,128)(2,1)} %copy-done.66), channel_id=1, source_target_pairs={{0,4},{2,6},{4,0},{6,2},{1,5},{3,7},{5,1},{7,3},{8,12},{10,14},{12... | collective-permute-start | bytes 589832 | tf_op jit(solution)/shard_map/ppermute | solution.py:853
  173.6 2.8 %collective-permute-start.48 = (bf16[128,768]{1,0:T(8,128)(2,1)}, bf16[128,768]{1,0:T(8,128)(2,1)S(1)}, u32[]{:S(2)}, u32[]{:S(2)}) collective-permute-start(bf16[128,768]{1,0:T(8,128)(2,1)} %copy-done.65), channel_id=1, source_target_pairs={{0,6},{2,4},{4,2},{6,0},{1,7},{3,5},{5,3},{7,1},{8,14},{10,12},{12... | collective-permute-start | bytes 589832 | tf_op jit(solution)/shard_map/ppermute | solution.py:853
  176.4 3.9 %collective-permute-done.53.refs_3_ = bf16[576,256]{1,0:T(8,128)(2,1)} collective-permute-done((bf16[576,256]{1,0:T(8,128)(2,1)}, bf16[576,256]{1,0:T(8,128)(2,1)}, u32[]{:S(2)}, u32[]{:S(2)}) %collective-permute-start.53) | collective-permute-done | bytes 294944 | tf_op jit(solution)/shard_map/ppermute | solution.py:1020
  180.3 4.3 %collective-permute-done.51.refs_1_ = bf16[1088,256]{1,0:T(8,128)(2,1)} collective-permute-done((bf16[1088,256]{1,0:T(8,128)(2,1)}, bf16[1088,256]{1,0:T(8,128)(2,1)}, u32[]{:S(2)}, u32[]{:S(2)}) %collective-permute-start.51) | collective-permute-done | bytes 557088 | tf_op jit(solution)/shard_map/ppermute | solution.py:849
  188.6 3.1 %collective-permute-start.54 = (bf16[272,256]{1,0:T(8,128)(2,1)S(1)}, bf16[272,256]{1,0:T(8,128)(2,1)S(1)}, u32[]{:S(2)}, u32[]{:S(2)}) collective-permute-start(bf16[272,256]{1,0:T(8,128)(2,1)S(1)} %get-tuple-element.200), channel_id=1, source_target_pairs={{0,2},{2,0},{4,6},{6,4},{1,3},{3,1},{5,7},{7,5},{8,10},{10,8},{12,... | collective-permute-start | bytes 417800 | tf_op jit(solution)/shard_map/ppermute | solution.py:853
  196.7 2.1 %shard_map.253 = bf16[128,1024]{1,0:T(8,128)(2,1)} custom-call(bf16[128,768]{1,0:T(8,128)(2,1)S(1)} %copy-done.46, bf16[128,768]{1,0:T(8,128)(2,1)} %collective-permute-done.46.refs_3_.refs_1_, bf16[128,768]{1,0:T(8,128)(2,1)S(1)} %collective-permute-done.47.refs_4_.refs_2_, bf16[128,768]{1,0:T(8,128)(2,1)S(1)} %collective-permute-done.48.refs_5_.refs_3_, ...), custom_call_target="tpu_custom_call" | custom-call | flops 1 | tf_op jit(solution)/shard_map/pallas_call | solution.py:447
  (307 shorter events, 91.7 us)
Async XLA Ops:
  38.1 12.9 %collective-permute-start.15 = (bf16[256,1536]{1,0:T(8,128)(2,1)S(1)}, bf16[256,1536]{1,0:T(8,128)(2,1)S(1)}, u32[]{:S(2)}, u32[]{:S(2)}) collective-permute-start(bf16[256,1536]{1,0:T(8,128)(2,1)S(1)} %get-tuple-element.121.refs_14_), channel_id=1, source_target_pairs={{0,8},{8,0},{1,9},{9,1},{2,10},{10,2},{3,11},{11,3},{4,12},{12,4},... | collective-permute-start | bytes 2359304 | tf_op jit(solution)/shard_map/ppermute | solution.py:849
  49.3 20.0 %collective-permute-start.22 = (bf16[512,768]{1,0:T(8,128)(2,1)}, bf16[512,768]{1,0:T(8,128)(2,1)}, u32[]{:S(2)}, u32[]{:S(2)}) collective-permute-start(bf16[512,768]{1,0:T(8,128)(2,1)} %get-tuple-element.124), channel_id=1, source_target_pairs={{0,16},{16,0},{1,17},{17,1},{2,18},{18,2},{3,19},{19,3},{4,20},{20... | collective-permute-start | bytes 2359304 | tf_op jit(solution)/shard_map/ppermute | solution.py:849
  50.9 18.3 %collective-permute-start.18 = (bf16[256,1024]{1,0:T(8,128)(2,1)}, bf16[256,1024]{1,0:T(8,128)(2,1)}, u32[]{:S(2)}, u32[]{:S(2)}) collective-permute-start(bf16[256,1024]{1,0:T(8,128)(2,1)} %shard_map.224), channel_id=1, source_target_pairs={{0,8},{8,0},{1,9},{9,1},{2,10},{10,2},{3,11},{11,3},{4,12},{12,4},... | collective-permute-start | bytes 1572872 | tf_op jit(solution)/shard_map/ppermute | solution.py:849
  51.0 18.2 %collective-permute-start.19 = (bf16[128,1024]{1,0:T(8,128)(2,1)S(1)}, bf16[128,1024]{1,0:T(8,128)(2,1)S(1)}, u32[]{:S(2)}, u32[]{:S(2)}) collective-permute-start(bf16[128,1024]{1,0:T(8,128)(2,1)S(1)} %get-tuple-element.123.refs_10_.refs_2_.refs_11_), channel_id=1, source_target_pairs={{0,2},{2,0},{4,6},{6,4},{1,3},{3,1},{5,7},{7,5},{8,10},{10,8},{12,... | collective-permute-start | bytes 786440 | tf_op jit(solution)/shard_map/ppermute | solution.py:853
  52.6 16.6 %collective-permute-start.20 = (bf16[128,1024]{1,0:T(8,128)(2,1)S(1)}, bf16[128,1024]{1,0:T(8,128)(2,1)S(1)}, u32[]{:S(2)}, u32[]{:S(2)}) collective-permute-start(bf16[128,1024]{1,0:T(8,128)(2,1)S(1)} %get-tuple-element.123.refs_10_.refs_2_.refs_11_), channel_id=1, source_target_pairs={{0,1},{1,0},{2,3},{3,2},{4,5},{5,4},{6,7},{7,6},{8,9},{9,8},{10,11... | collective-permute-start | bytes 786440 | tf_op jit(solution)/shard_map/ppermute | solution.py:849
  54.7 14.5 %collective-permute-start.21 = (bf16[128,1024]{1,0:T(8,128)(2,1)S(1)}, bf16[128,1024]{1,0:T(8,128)(2,1)}, u32[]{:S(2)}, u32[]{:S(2)}) collective-permute-start(bf16[128,1024]{1,0:T(8,128)(2,1)S(1)} %get-tuple-element.123.refs_10_.refs_2_.refs_11_), channel_id=1, source_target_pairs={{0,3},{1,2},{2,1},{3,0},{4,7},{5,6},{6,5},{7,4},{8,11},{9,10},{10,... | collective-permute-start | bytes 786440 | tf_op jit(solution)/shard_map/ppermute | solution.py:857
  76.9 12.6 %collective-permute-start.25 = (bf16[128,1024]{1,0:T(8,128)(2,1)S(1)}, bf16[128,1024]{1,0:T(8,128)(2,1)S(1)}, u32[]{:S(2)}, u32[]{:S(2)}) collective-permute-start(bf16[128,1024]{1,0:T(8,128)(2,1)S(1)} %get-tuple-element.126.refs_1_.refs_0_.refs_9_), channel_id=1, source_target_pairs={{0,2},{2,0},{4,6},{6,4},{1,3},{3,1},{5,7},{7,5},{8,10},{10,8},{12,... | collective-permute-start | bytes 786440 | tf_op jit(solution)/shard_map/ppermute | solution.py:853
  76.9 13.3 %collective-permute-start.29 = (bf16[128,1024]{1,0:T(8,128)(2,1)S(1)}, bf16[128,1024]{1,0:T(8,128)(2,1)S(1)}, u32[]{:S(2)}, u32[]{:S(2)}) collective-permute-start(bf16[128,1024]{1,0:T(8,128)(2,1)S(1)} %get-tuple-element.126.refs_1_.refs_0_.refs_9_), channel_id=1, source_target_pairs={{0,3},{1,2},{2,1},{3,0},{4,7},{5,6},{6,5},{7,4},{8,11},{9,10},{10,... | collective-permute-start | bytes 786440 | tf_op jit(solution)/shard_map/ppermute | solution.py:857
  101.6 20.4 %collective-permute-start.41 = (bf16[704,512]{1,0:T(8,128)(2,1)S(1)}, bf16[704,512]{1,0:T(8,128)(2,1)S(1)}, u32[]{:S(2)}, u32[]{:S(2)}) collective-permute-start(bf16[704,512]{1,0:T(8,128)(2,1)S(1)} %get-tuple-element.180), channel_id=1, source_target_pairs={{0,16},{16,0},{1,17},{17,1},{2,18},{18,2},{3,19},{19,3},{4,20},{20... | collective-permute-start | bytes 2162696 | tf_op jit(solution)/shard_map/ppermute | solution.py:849
  121.9 18.2 %collective-permute-start.40 = (bf16[2,1024,256]{2,1,0:T(8,128)(2,1)S(1)}, bf16[2,1024,256]{2,1,0:T(8,128)(2,1)S(1)}, u32[]{:S(2)}, u32[]{:S(2)}) collective-permute-start(bf16[2,1024,256]{2,1,0:T(8,128)(2,1)S(1)} %get-tuple-element.153.refs_1_.refs_9_.refs_2_), channel_id=1, source_target_pairs={{0,8},{8,0},{1,9},{9,1},{2,10},{10,2},{3,11},{11,3},{4,12},{12,4},... | collective-permute-start | bytes 3145736 | tf_op jit(solution)/shard_map/ppermute | solution.py:849
  122.2 17.9 %collective-permute-start.42 = (bf16[704,512]{1,0:T(8,128)(2,1)S(1)}, bf16[704,512]{1,0:T(8,128)(2,1)S(1)}, u32[]{:S(2)}, u32[]{:S(2)}) collective-permute-start(bf16[704,512]{1,0:T(8,128)(2,1)S(1)} %shard_map.246), channel_id=1, source_target_pairs={{0,0},{2,2},{4,8},{6,10},{8,4},{10,6},{12,12},{14,14},{1,1},{3,3},... | collective-permute-start | bytes 2162696 | tf_op jit(solution)/shard_map/ppermute | solution.py:980
  123.4 16.8 %collective-permute-start.38 = (bf16[256,1024]{1,0:T(8,128)(2,1)S(1)}, bf16[256,1024]{1,0:T(8,128)(2,1)S(1)}, u32[]{:S(2)}, u32[]{:S(2)}) collective-permute-start(bf16[256,1024]{1,0:T(8,128)(2,1)S(1)} %shard_map.241), channel_id=1, source_target_pairs={{0,1},{1,0},{2,3},{3,2},{4,5},{5,4},{6,7},{7,6},{8,9},{9,8},{10,11... | collective-permute-start | bytes 1572872 | tf_op jit(solution)/shard_map/ppermute | solution.py:849
  124.8 15.3 %collective-permute-start.39 = (bf16[352,512]{1,0:T(8,128)(2,1)}, bf16[352,512]{1,0:T(8,128)(2,1)}, u32[]{:S(2)}, u32[]{:S(2)}) collective-permute-start(bf16[352,512]{1,0:T(8,128)(2,1)} %shard_map.243), channel_id=1, source_target_pairs={{0,16},{16,0},{1,17},{17,1},{2,18},{18,2},{3,19},{19,3},{4,20},{20... | collective-permute-start | bytes 1081352 | tf_op jit(solution)/shard_map/ppermute | solution.py:849
  141.7 19.5 %collective-permute-start.45 = (bf16[2,8,144,256]{3,2,1,0:T(8,128)(2,1)S(1)}, bf16[2,8,144,256]{3,2,1,0:T(8,128)(2,1)S(1)}, u32[]{:S(2)}, u32[]{:S(2)}) collective-permute-start(bf16[2,8,144,256]{3,2,1,0:T(8,128)(2,1)S(1)} %shard_map.248), channel_id=1, source_target_pairs={{0,8},{8,0},{1,9},{9,1},{2,10},{10,2},{3,11},{11,3},{4,12},{12,4},... | collective-permute-start | bytes 3538952 | tf_op jit(solution)/shard_map/ppermute | solution.py:849
  145.7 15.6 %collective-permute-start.50 = (bf16[1024,256]{1,0:T(8,128)(2,1)S(1)}, bf16[1024,256]{1,0:T(8,128)(2,1)S(1)}, u32[]{:S(2)}, u32[]{:S(2)}) collective-permute-start(bf16[1024,256]{1,0:T(8,128)(2,1)S(1)} %get-tuple-element.184.refs_1_), channel_id=1, source_target_pairs={{0,16},{16,0},{1,17},{17,1},{2,18},{18,2},{3,19},{19,3},{4,20},{20... | collective-permute-start | bytes 1572872 | tf_op jit(solution)/shard_map/ppermute | solution.py:849
  146.8 14.4 %collective-permute-start.49 = (bf16[352,512]{1,0:T(8,128)(2,1)S(1)}, bf16[352,512]{1,0:T(8,128)(2,1)S(1)}, u32[]{:S(2)}, u32[]{:S(2)}) collective-permute-start(bf16[352,512]{1,0:T(8,128)(2,1)S(1)} %get-tuple-element.191), channel_id=1, source_target_pairs={{0,0},{2,2},{4,8},{6,10},{8,4},{10,6},{12,12},{14,14},{1,1},{3,3},... | collective-permute-start | bytes 1081352 | tf_op jit(solution)/shard_map/ppermute | solution.py:980
  147.8 18.3 %collective-permute-start.44 = (bf16[512,640]{1,0:T(8,128)(2,1)S(1)}, bf16[512,640]{1,0:T(8,128)(2,1)S(1)}, u32[]{:S(2)}, u32[]{:S(2)}) collective-permute-start(bf16[512,640]{1,0:T(8,128)(2,1)S(1)} %copy-done.64), channel_id=1, source_target_pairs={{0,1},{1,0},{2,3},{3,2},{4,5},{5,4},{6,7},{7,6},{8,9},{9,8},{10,11... | collective-permute-start | bytes 1966088 | tf_op jit(solution)/shard_map/ppermute | solution.py:849
  162.5 22.1 %collective-permute-start.51 = (bf16[1088,256]{1,0:T(8,128)(2,1)}, bf16[1088,256]{1,0:T(8,128)(2,1)}, u32[]{:S(2)}, u32[]{:S(2)}) collective-permute-start(bf16[1088,256]{1,0:T(8,128)(2,1)} %get-tuple-element.195), channel_id=1, source_target_pairs={{0,1},{1,0},{2,3},{3,2},{4,5},{5,4},{6,7},{7,6},{8,9},{9,8},{10,11... | collective-permute-start | bytes 1671176 | tf_op jit(solution)/shard_map/ppermute | solution.py:849
  164.2 16.1 %collective-permute-start.53 = (bf16[576,256]{1,0:T(8,128)(2,1)}, bf16[576,256]{1,0:T(8,128)(2,1)}, u32[]{:S(2)}, u32[]{:S(2)}) collective-permute-start(bf16[576,256]{1,0:T(8,128)(2,1)} %get-tuple-element.197), channel_id=1, source_target_pairs={{0,17},{1,16},{16,1},{17,0},{2,19},{3,18},{18,3},{19,2},{4,21},{5,... | collective-permute-start | bytes 884744 | tf_op jit(solution)/shard_map/ppermute | solution.py:1020
  168.2 20.3 %collective-permute-start.46 = (bf16[128,768]{1,0:T(8,128)(2,1)}, bf16[128,768]{1,0:T(8,128)(2,1)}, u32[]{:S(2)}, u32[]{:S(2)}) collective-permute-start(bf16[128,768]{1,0:T(8,128)(2,1)} %get-tuple-element.186), channel_id=1, source_target_pairs={{0,2},{2,0},{4,6},{6,4},{1,3},{3,1},{5,7},{7,5},{8,10},{10,8},{12,... | collective-permute-start | bytes 589832 | tf_op jit(solution)/shard_map/ppermute | solution.py:853
  168.3 25.2 %collective-permute-start.47 = (bf16[128,768]{1,0:T(8,128)(2,1)}, bf16[128,768]{1,0:T(8,128)(2,1)S(1)}, u32[]{:S(2)}, u32[]{:S(2)}) collective-permute-start(bf16[128,768]{1,0:T(8,128)(2,1)} %copy-done.66), channel_id=1, source_target_pairs={{0,4},{2,6},{4,0},{6,2},{1,5},{3,7},{5,1},{7,3},{8,12},{10,14},{12... | collective-permute-start | bytes 589832 | tf_op jit(solution)/shard_map/ppermute | solution.py:853
  173.6 20.0 %collective-permute-start.48 = (bf16[128,768]{1,0:T(8,128)(2,1)}, bf16[128,768]{1,0:T(8,128)(2,1)S(1)}, u32[]{:S(2)}, u32[]{:S(2)}) collective-permute-start(bf16[128,768]{1,0:T(8,128)(2,1)} %copy-done.65), channel_id=1, source_target_pairs={{0,6},{2,4},{4,2},{6,0},{1,7},{3,5},{5,3},{7,1},{8,14},{10,12},{12... | collective-permute-start | bytes 589832 | tf_op jit(solution)/shard_map/ppermute | solution.py:853
  188.6 13.0 %collective-permute-start.55 = (bf16[272,256]{1,0:T(8,128)(2,1)S(1)}, bf16[272,256]{1,0:T(8,128)(2,1)S(1)}, u32[]{:S(2)}, u32[]{:S(2)}) collective-permute-start(bf16[272,256]{1,0:T(8,128)(2,1)S(1)} %get-tuple-element.201), channel_id=1, source_target_pairs={{0,4},{2,6},{4,0},{6,2},{1,5},{3,7},{5,1},{7,3},{8,12},{10,14},{12... | collective-permute-start | bytes 417800 | tf_op jit(solution)/shard_map/ppermute | solution.py:853
  188.6 13.0 %collective-permute-start.54 = (bf16[272,256]{1,0:T(8,128)(2,1)S(1)}, bf16[272,256]{1,0:T(8,128)(2,1)S(1)}, u32[]{:S(2)}, u32[]{:S(2)}) collective-permute-start(bf16[272,256]{1,0:T(8,128)(2,1)S(1)} %get-tuple-element.200), channel_id=1, source_target_pairs={{0,2},{2,0},{4,6},{6,4},{1,3},{3,1},{5,7},{7,5},{8,10},{10,8},{12,... | collective-permute-start | bytes 417800 | tf_op jit(solution)/shard_map/ppermute | solution.py:853
  (113 other events, 943.7 us)

commit v5 on v4

--- a/solution.py
+++ b/solution.py
@@ -1018,7 +1018,7 @@
     pieces = (p0, hop(p1, 1), hop(p2, 2), hop(p3, 3))
     b_x, y_there = swap(b_x, "x"), swap(y_send, "y")
     b_xy = lax.ppermute(b_xy, ("x", "y"), [(i, i ^ 3) for i in range(4)])
-    z0, z1, z2, z3 = call(functools.partial(quarters_kernel, rows), 0, [((tall + rows, shard), BF)] * 4)(
+    z0, z1, z2, z3 = call(functools.partial(quarters_kernel, rows), 0, [((tall + rows, shard), BF)] * 4, far_in=(0,))(
         y_keep, y_there, b_x, b_xy
     )
     last = z0.astype(F32) + hop(z1, 1) + hop(z2, 2) + hop(z3, 3)

time: 210 us -> 210 us (level)
  no operation moved by 1% of the time
where the time goes in v5:
time: 210 us; the launch traced here: 206 us
  starting transfers between devices  64.1 us (31%)
  waiting for transfers between devices  60.7 us (29%)
  Pallas kernels  56.9 us (27%)
  local copies, waits for them, and re-layouts  14.5 us (7%)
  other arithmetic  7.92 us (4%)
  between operations  2.2 us (1%)
    pallas_call x21, Pallas kernels, run(): pl.pallas_call(body, in_specs=[pl.BlockSpec(memory_space=pltpu.SMEM)] * n...  56.9 us
    ppermute x35, starting transfers between devices, swap(): return lax.ppermute(value, axis, [(0, 1), (1, 0)])  28.7 us
    ppermute x35, waiting for transfers between devices, swap(): return lax.ppermute(value, axis, [(0, 1), (1, 0)])  22 us
    ppermute x10, waiting for transfers between devices, hop(): return lax.ppermute(value, 'z', [(i, i ^ k) for i in range(4)])  15.2 us
    ppermute x10, starting transfers between devices, hop(): return lax.ppermute(value, 'z', [(i, i ^ k) for i in range(4)])  14.6 us
    unnamed x157, local copies, waits for them, and re-layouts  12 us
    ppermute x7, starting transfers between devices, ring(): return lax.ppermute(value, ('z', 'y'), pairs)  9.22 us
    ppermute x7, waiting for transfers between devices, ring(): return lax.ppermute(value, ('z', 'y'), pairs)  9.11 us
  transfers between devices with their start and end apart: 60, of which 16 were waited for; matrix products, arithmetic and copies ran while one was open for 5% of the time, Pallas kernels for 26%

profile of v5, /device:TPU:0, one launch (start us, length us, event | category | flops | bytes accessed | tf_op | source)
XLA Modules:
  0.0 206.3 jit_solution(6024498651567661949)
XLA Ops:
  0.7 3.1 %collective-permute-start = (bf16[128,1024]{1,0:T(8,128)(2,1)}, bf16[128,1024]{1,0:T(8,128)(2,1)S(1)}, u32[]{:S(2)}, u32[]{:S(2)}) collective-permute-start(bf16[128,1024]{1,0:T(8,128)(2,1)} %refs_6_.3), channel_id=1, source_target_pairs={{0,2},{2,4},{4,6},{6,7},{7,5},{5,3},{3,1},{1,0},{8,10},{10,12},{12... | collective-permute-start | bytes 786440 | tf_op jit(solution)/shard_map/ppermute | solution.py:884
  21.7 2.7 %shard_map.222 = (bf16[256,768]{1,0:T(8,128)(2,1)S(1)}, bf16[256,768]{1,0:T(8,128)(2,1)S(1)}, bf16[512,768]{1,0:T(8,128)(2,1)}) custom-call(s32[26]{0:T(128)S(1)} %stack.107.refs_0_, bf16[256,2816]{1,0:T(8,128)(2,1)S(1)} %copy-done.29, bf16[256,2816]{1,0:T(8,128)(2,1)S(1)} %copy-done.30, bf16[256,1]{1,0:T(8,128)(2,1)S(1)} %broadcast_in_dim.6.refs_3_, ...), custom_call_target="tpu_custom_call" | custom-call | flops 1 | tf_op jit(solution)/shard_map/pallas_call | solution.py:447
  27.8 8.4 %collective-permute-done.8.refs_3_.refs_5_.refs_9_ = bf16[256,1024]{1,0:T(8,128)(2,1)S(1)} collective-permute-done((bf16[256,1024]{1,0:T(8,128)(2,1)}, bf16[256,1024]{1,0:T(8,128)(2,1)S(1)}, u32[]{:S(2)}, u32[]{:S(2)}) %collective-permute-start.8) | collective-permute-done | bytes 524320 | tf_op jit(solution)/shard_map/ppermute | solution.py:849
  40.5 6.9 %collective-permute-done.10.refs_0_ = bf16[128,1024]{1,0:T(8,128)(2,1)S(1)} collective-permute-done((bf16[128,1024]{1,0:T(8,128)(2,1)S(1)}, bf16[128,1024]{1,0:T(8,128)(2,1)S(1)}, u32[]{:S(2)}, u32[]{:S(2)}) %collective-permute-start.10) | collective-permute-done | bytes 262176 | tf_op jit(solution)/shard_map/ppermute | solution.py:884
  56.5 12.7 %shard_map.227 = (bf16[128,1024]{1,0:T(8,128)(2,1)}, bf16[2048,1024]{1,0:T(8,128)(2,1)}, bf16[2048,256]{1,0:T(8,128)(2,1)}, bf16[2048,256]{1,0:T(8,128)(2,1)}, b...) custom-call(s32[26]{0:T(128)} %copy-done.61, ...), custom_call_target="tpu_custom_call" | custom-call | flops 1 | tf_op jit(solution)/shard_map/pallas_call | solution.py:447
  72.6 3.0 %collective-permute-start.24 = (bf16[352,1024]{1,0:T(8,128)(2,1)S(1)}, bf16[352,1024]{1,0:T(8,128)(2,1)S(1)}, u32[]{:S(2)}, u32[]{:S(2)}) collective-permute-start(bf16[352,1024]{1,0:T(8,128)(2,1)S(1)} %shard_map.229), channel_id=1, source_target_pairs={{16,8},{26,10},{20,12},{30,14},{0,16},{10,18},{4,20},{14,22},{17,9... | collective-permute-start | bytes 2162696 | tf_op jit(solution)/shard_map/ppermute | solution.py:936
  76.9 2.3 %collective-permute-start.29 = (bf16[128,1024]{1,0:T(8,128)(2,1)S(1)}, bf16[128,1024]{1,0:T(8,128)(2,1)S(1)}, u32[]{:S(2)}, u32[]{:S(2)}) collective-permute-start(bf16[128,1024]{1,0:T(8,128)(2,1)S(1)} %get-tuple-element.126.refs_1_.refs_0_.refs_9_), channel_id=1, source_target_pairs={{0,3},{1,2},{2,1},{3,0},{4,7},{5,6},{6,5},{7,4},{8,11},{9,10},{10,... | collective-permute-start | bytes 786440 | tf_op jit(solution)/shard_map/ppermute | solution.py:857
  79.2 5.2 %collective-permute-done.24.refs_5_ = bf16[352,1024]{1,0:T(8,128)(2,1)S(1)} collective-permute-done((bf16[352,1024]{1,0:T(8,128)(2,1)S(1)}, bf16[352,1024]{1,0:T(8,128)(2,1)S(1)}, u32[]{:S(2)}, u32[]{:S(2)}) %collective-permute-start.24) | collective-permute-done | bytes 720928 | tf_op jit(solution)/shard_map/ppermute | solution.py:936
  94.8 2.7 %shard_map.237 = (bf16[256,384]{1,0:T(8,128)(2,1)S(1)}, bf16[256,768]{1,0:T(8,128)(2,1)S(1)}, f32[128,1024]{1,0:T(8,128)S(1)}, f32[128,1024]{1,0:T(8,128)S(1)}, bf16[256,1024]{1,0:T(8,128)(2,1)S(1)}) custom-call(bf16[128,1024]{1,0:T(8,128)(2,1)S(1)} %shard_map.236.refs_0_.refs_21_, bf16[128,1024]{1,0:T(8,128)(2,1)S(1)} %collective-permute-done.30.refs_1_.refs_22_, ...), custom_call_target="tpu_custom_call" | custom-call | flops 1 | tf_op jit(solution)/shard_map/pallas_call | solution.py:447
  97.7 3.9 %shard_map.242 = (bf16[704,512]{1,0:T(8,128)(2,1)S(1)}, bf16[704,512]{1,0:T(8,128)(2,1)S(1)}, bf16[352,512]{1,0:T(8,128)(2,1)}, bf16[352,512]{1,0:T(8,128)(2,1)S(1)}) custom-call(s32[26]{0:T(128)S(1)} %copy-done.62, bf16[256,384]{1,0:T(8,128)(2,1)S(1)} %get-tuple-element.132.refs_1_.refs_6_, bf16[256,384]{1,0:T(8,128)(2,1)S(1)} %get-tuple-element.136.refs_6_.refs_2_, ...), custom_call_target="tpu_custom_call" | custom-call | flops 1 | tf_op jit(solution)/shard_map/pallas_call | solution.py:447
  106.7 4.8 %collective-permute-done.35.refs_2_ = bf16[128,1024]{1,0:T(8,128)(2,1)S(1)} collective-permute-done((bf16[128,1024]{1,0:T(8,128)(2,1)S(1)}, bf16[128,1024]{1,0:T(8,128)(2,1)S(1)}, u32[]{:S(2)}, u32[]{:S(2)}) %collective-permute-start.35) | collective-permute-done | bytes 262176 | tf_op jit(solution)/shard_map/ppermute | solution.py:849
  111.5 2.2 %collective-permute-done.36.refs_3_ = bf16[128,1024]{1,0:T(8,128)(2,1)S(1)} collective-permute-done((bf16[128,1024]{1,0:T(8,128)(2,1)S(1)}, bf16[128,1024]{1,0:T(8,128)(2,1)S(1)}, u32[]{:S(2)}, u32[]{:S(2)}) %collective-permute-start.36) | collective-permute-done | bytes 262176 | tf_op jit(solution)/shard_map/ppermute | solution.py:853
  113.7 4.6 %collective-permute-done.37.refs_4_ = bf16[128,1024]{1,0:T(8,128)(2,1)S(1)} collective-permute-done((bf16[128,1024]{1,0:T(8,128)(2,1)S(1)}, bf16[128,1024]{1,0:T(8,128)(2,1)S(1)}, u32[]{:S(2)}, u32[]{:S(2)}) %collective-permute-start.37) | collective-permute-done | bytes 262176 | tf_op jit(solution)/shard_map/ppermute | solution.py:857
  118.3 2.3 %shard_map.239 = (f32[128,1024]{1,0:T(8,128)S(1)}, bf16[128,1024]{1,0:T(8,128)(2,1)S(1)}, bf16[128,1024]{1,0:T(8,128)(2,1)S(1)}, f32[8,1024]{1,0:T(8,128)S(1)}) custom-call(s32[26]{0:T(128)S(1)} %copy-done.62, f32[128,1024]{1,0:T(8,128)S(1)} %get-tuple-element.148.refs_1_, bf16[128,1024]{1,0:T(8,128)(2,1)S(1)} %collective-permute-done.35.refs_2_, ...), custom_call_target="tpu_custom_call" | custom-call | flops 1 | tf_op jit(solution)/shard_map/pallas_call | solution.py:447
  125.9 8.9 %shard_map.244 = (bf16[1024,512]{1,0:T(8,128)(2,1)S(1)}, bf16[512,640]{1,0:T(8,128)(2,1)S(1)}, bf16[512,640]{1,0:T(8,128)(2,1)S(1)}, bf16[128,1024]{1,0:T(8,128)(2,1)S(1)}, bf16[4,8,64,256]{3,2,1,0:T(8,128)(2,1)S(1)}) custom-call(s32[26]{0:T(128)S(1)} %copy-done.62, bf16[128,1024]{1,0:T(8,128)(2,1)S(1)} %get-tuple-element.163.refs_1_, ...), custom_call_target="tpu_custom_call" | custom-call | flops 1 | tf_op jit(solution)/shard_map/pallas_call | solution.py:447
  135.7 3.6 %shard_map.245 = (f32[128,1024]{1,0:T(8,128)S(1)}, bf16[2,8,144,256]{3,2,1,0:T(8,128)(2,1)S(1)}, bf16[2,8,144,256]{3,2,1,0:T(8,128)(2,1)S(1)}) custom-call(s32[26]{0:T(128)S(1)} %copy-done.62, bf16[1024,512]{1,0:T(8,128)(2,1)S(1)} %get-tuple-element.171.refs_1_, bf16[1024,1024]{1,0:T(8,128)(2,1)S(1)} %copy-done.3, bf16[512,1024]{1,0:T(8,128)(2,1)S(1)} %copy-done.11, ...), custom_call_target="tpu_custom_call" | custom-call | flops 1 | tf_op jit(solution)/shard_map/pallas_call | solution.py:447
  141.7 4.0 %collective-permute-start.45 = (bf16[2,8,144,256]{3,2,1,0:T(8,128)(2,1)S(1)}, bf16[2,8,144,256]{3,2,1,0:T(8,128)(2,1)S(1)}, u32[]{:S(2)}, u32[]{:S(2)}) collective-permute-start(bf16[2,8,144,256]{3,2,1,0:T(8,128)(2,1)S(1)} %shard_map.248), channel_id=1, source_target_pairs={{0,8},{8,0},{1,9},{9,1},{2,10},{10,2},{3,11},{11,3},{4,12},{12,4},... | collective-permute-start | bytes 3538952 | tf_op jit(solution)/shard_map/ppermute | solution.py:849
  149.9 11.3 %collective-permute-done.43.refs_5_ = bf16[128,1024]{1,0:T(8,128)(2,1)S(1)} collective-permute-done((bf16[128,1024]{1,0:T(8,128)(2,1)S(1)}, bf16[128,1024]{1,0:T(8,128)(2,1)S(1)}, u32[]{:S(2)}, u32[]{:S(2)}) %collective-permute-start.43) | collective-permute-done | bytes 262176 | tf_op jit(solution)/shard_map/ppermute | solution.py:853
  168.3 3.5 %collective-permute-start.47 = (bf16[128,768]{1,0:T(8,128)(2,1)}, bf16[128,768]{1,0:T(8,128)(2,1)S(1)}, u32[]{:S(2)}, u32[]{:S(2)}) collective-permute-start(bf16[128,768]{1,0:T(8,128)(2,1)} %copy-done.66), channel_id=1, source_target_pairs={{0,4},{2,6},{4,0},{6,2},{1,5},{3,7},{5,1},{7,3},{8,12},{10,14},{12... | collective-permute-start | bytes 589832 | tf_op jit(solution)/shard_map/ppermute | solution.py:853
  173.6 2.8 %collective-permute-start.48 = (bf16[128,768]{1,0:T(8,128)(2,1)}, bf16[128,768]{1,0:T(8,128)(2,1)S(1)}, u32[]{:S(2)}, u32[]{:S(2)}) collective-permute-start(bf16[128,768]{1,0:T(8,128)(2,1)} %copy-done.65), channel_id=1, source_target_pairs={{0,6},{2,4},{4,2},{6,0},{1,7},{3,5},{5,3},{7,1},{8,14},{10,12},{12... | collective-permute-start | bytes 589832 | tf_op jit(solution)/shard_map/ppermute | solution.py:853
  176.4 3.9 %collective-permute-done.53.refs_3_ = bf16[576,256]{1,0:T(8,128)(2,1)} collective-permute-done((bf16[576,256]{1,0:T(8,128)(2,1)}, bf16[576,256]{1,0:T(8,128)(2,1)}, u32[]{:S(2)}, u32[]{:S(2)}) %collective-permute-start.53) | collective-permute-done | bytes 294944 | tf_op jit(solution)/shard_map/ppermute | solution.py:1020
  180.3 4.3 %collective-permute-done.51.refs_1_ = bf16[1088,256]{1,0:T(8,128)(2,1)} collective-permute-done((bf16[1088,256]{1,0:T(8,128)(2,1)}, bf16[1088,256]{1,0:T(8,128)(2,1)}, u32[]{:S(2)}, u32[]{:S(2)}) %collective-permute-start.51) | collective-permute-done | bytes 557088 | tf_op jit(solution)/shard_map/ppermute | solution.py:849
  188.6 3.1 %collective-permute-start.54 = (bf16[272,256]{1,0:T(8,128)(2,1)S(1)}, bf16[272,256]{1,0:T(8,128)(2,1)S(1)}, u32[]{:S(2)}, u32[]{:S(2)}) collective-permute-start(bf16[272,256]{1,0:T(8,128)(2,1)S(1)} %get-tuple-element.200), channel_id=1, source_target_pairs={{0,2},{2,0},{4,6},{6,4},{1,3},{3,1},{5,7},{7,5},{8,10},{10,8},{12,... | collective-permute-start | bytes 417800 | tf_op jit(solution)/shard_map/ppermute | solution.py:853
  196.8 2.1 %shard_map.253 = bf16[128,1024]{1,0:T(8,128)(2,1)} custom-call(bf16[128,768]{1,0:T(8,128)(2,1)S(1)} %copy-done.46, bf16[128,768]{1,0:T(8,128)(2,1)} %collective-permute-done.46.refs_3_.refs_1_, bf16[128,768]{1,0:T(8,128)(2,1)S(1)} %collective-permute-done.47.refs_4_.refs_2_, bf16[128,768]{1,0:T(8,128)(2,1)S(1)} %collective-permute-done.48.refs_5_.refs_3_, ...), custom_call_target="tpu_custom_call" | custom-call | flops 1 | tf_op jit(solution)/shard_map/pallas_call | solution.py:447
  (307 shorter events, 91.7 us)
Async XLA Ops:
  38.1 12.9 %collective-permute-start.15 = (bf16[256,1536]{1,0:T(8,128)(2,1)S(1)}, bf16[256,1536]{1,0:T(8,128)(2,1)S(1)}, u32[]{:S(2)}, u32[]{:S(2)}) collective-permute-start(bf16[256,1536]{1,0:T(8,128)(2,1)S(1)} %get-tuple-element.121.refs_14_), channel_id=1, source_target_pairs={{0,8},{8,0},{1,9},{9,1},{2,10},{10,2},{3,11},{11,3},{4,12},{12,4},... | collective-permute-start | bytes 2359304 | tf_op jit(solution)/shard_map/ppermute | solution.py:849
  49.3 20.0 %collective-permute-start.22 = (bf16[512,768]{1,0:T(8,128)(2,1)}, bf16[512,768]{1,0:T(8,128)(2,1)}, u32[]{:S(2)}, u32[]{:S(2)}) collective-permute-start(bf16[512,768]{1,0:T(8,128)(2,1)} %get-tuple-element.124), channel_id=1, source_target_pairs={{0,16},{16,0},{1,17},{17,1},{2,18},{18,2},{3,19},{19,3},{4,20},{20... | collective-permute-start | bytes 2359304 | tf_op jit(solution)/shard_map/ppermute | solution.py:849
  50.9 18.3 %collective-permute-start.18 = (bf16[256,1024]{1,0:T(8,128)(2,1)}, bf16[256,1024]{1,0:T(8,128)(2,1)}, u32[]{:S(2)}, u32[]{:S(2)}) collective-permute-start(bf16[256,1024]{1,0:T(8,128)(2,1)} %shard_map.224), channel_id=1, source_target_pairs={{0,8},{8,0},{1,9},{9,1},{2,10},{10,2},{3,11},{11,3},{4,12},{12,4},... | collective-permute-start | bytes 1572872 | tf_op jit(solution)/shard_map/ppermute | solution.py:849
  51.0 18.2 %collective-permute-start.19 = (bf16[128,1024]{1,0:T(8,128)(2,1)S(1)}, bf16[128,1024]{1,0:T(8,128)(2,1)S(1)}, u32[]{:S(2)}, u32[]{:S(2)}) collective-permute-start(bf16[128,1024]{1,0:T(8,128)(2,1)S(1)} %get-tuple-element.123.refs_10_.refs_2_.refs_11_), channel_id=1, source_target_pairs={{0,2},{2,0},{4,6},{6,4},{1,3},{3,1},{5,7},{7,5},{8,10},{10,8},{12,... | collective-permute-start | bytes 786440 | tf_op jit(solution)/shard_map/ppermute | solution.py:853
  52.6 16.6 %collective-permute-start.20 = (bf16[128,1024]{1,0:T(8,128)(2,1)S(1)}, bf16[128,1024]{1,0:T(8,128)(2,1)S(1)}, u32[]{:S(2)}, u32[]{:S(2)}) collective-permute-start(bf16[128,1024]{1,0:T(8,128)(2,1)S(1)} %get-tuple-element.123.refs_10_.refs_2_.refs_11_), channel_id=1, source_target_pairs={{0,1},{1,0},{2,3},{3,2},{4,5},{5,4},{6,7},{7,6},{8,9},{9,8},{10,11... | collective-permute-start | bytes 786440 | tf_op jit(solution)/shard_map/ppermute | solution.py:849
  54.7 14.5 %collective-permute-start.21 = (bf16[128,1024]{1,0:T(8,128)(2,1)S(1)}, bf16[128,1024]{1,0:T(8,128)(2,1)}, u32[]{:S(2)}, u32[]{:S(2)}) collective-permute-start(bf16[128,1024]{1,0:T(8,128)(2,1)S(1)} %get-tuple-element.123.refs_10_.refs_2_.refs_11_), channel_id=1, source_target_pairs={{0,3},{1,2},{2,1},{3,0},{4,7},{5,6},{6,5},{7,4},{8,11},{9,10},{10,... | collective-permute-start | bytes 786440 | tf_op jit(solution)/shard_map/ppermute | solution.py:857
  76.9 12.6 %collective-permute-start.25 = (bf16[128,1024]{1,0:T(8,128)(2,1)S(1)}, bf16[128,1024]{1,0:T(8,128)(2,1)S(1)}, u32[]{:S(2)}, u32[]{:S(2)}) collective-permute-start(bf16[128,1024]{1,0:T(8,128)(2,1)S(1)} %get-tuple-element.126.refs_1_.refs_0_.refs_9_), channel_id=1, source_target_pairs={{0,2},{2,0},{4,6},{6,4},{1,3},{3,1},{5,7},{7,5},{8,10},{10,8},{12,... | collective-permute-start | bytes 786440 | tf_op jit(solution)/shard_map/ppermute | solution.py:853
  76.9 13.3 %collective-permute-start.29 = (bf16[128,1024]{1,0:T(8,128)(2,1)S(1)}, bf16[128,1024]{1,0:T(8,128)(2,1)S(1)}, u32[]{:S(2)}, u32[]{:S(2)}) collective-permute-start(bf16[128,1024]{1,0:T(8,128)(2,1)S(1)} %get-tuple-element.126.refs_1_.refs_0_.refs_9_), channel_id=1, source_target_pairs={{0,3},{1,2},{2,1},{3,0},{4,7},{5,6},{6,5},{7,4},{8,11},{9,10},{10,... | collective-permute-start | bytes 786440 | tf_op jit(solution)/shard_map/ppermute | solution.py:857
  101.6 20.4 %collective-permute-start.41 = (bf16[704,512]{1,0:T(8,128)(2,1)S(1)}, bf16[704,512]{1,0:T(8,128)(2,1)S(1)}, u32[]{:S(2)}, u32[]{:S(2)}) collective-permute-start(bf16[704,512]{1,0:T(8,128)(2,1)S(1)} %get-tuple-element.180), channel_id=1, source_target_pairs={{0,16},{16,0},{1,17},{17,1},{2,18},{18,2},{3,19},{19,3},{4,20},{20... | collective-permute-start | bytes 2162696 | tf_op jit(solution)/shard_map/ppermute | solution.py:849
  121.9 18.2 %collective-permute-start.40 = (bf16[2,1024,256]{2,1,0:T(8,128)(2,1)S(1)}, bf16[2,1024,256]{2,1,0:T(8,128)(2,1)S(1)}, u32[]{:S(2)}, u32[]{:S(2)}) collective-permute-start(bf16[2,1024,256]{2,1,0:T(8,128)(2,1)S(1)} %get-tuple-element.153.refs_1_.refs_9_.refs_2_), channel_id=1, source_target_pairs={{0,8},{8,0},{1,9},{9,1},{2,10},{10,2},{3,11},{11,3},{4,12},{12,4},... | collective-permute-start | bytes 3145736 | tf_op jit(solution)/shard_map/ppermute | solution.py:849
  122.2 17.9 %collective-permute-start.42 = (bf16[704,512]{1,0:T(8,128)(2,1)S(1)}, bf16[704,512]{1,0:T(8,128)(2,1)S(1)}, u32[]{:S(2)}, u32[]{:S(2)}) collective-permute-start(bf16[704,512]{1,0:T(8,128)(2,1)S(1)} %shard_map.246), channel_id=1, source_target_pairs={{0,0},{2,2},{4,8},{6,10},{8,4},{10,6},{12,12},{14,14},{1,1},{3,3},... | collective-permute-start | bytes 2162696 | tf_op jit(solution)/shard_map/ppermute | solution.py:980
  123.4 16.8 %collective-permute-start.38 = (bf16[256,1024]{1,0:T(8,128)(2,1)S(1)}, bf16[256,1024]{1,0:T(8,128)(2,1)S(1)}, u32[]{:S(2)}, u32[]{:S(2)}) collective-permute-start(bf16[256,1024]{1,0:T(8,128)(2,1)S(1)} %shard_map.241), channel_id=1, source_target_pairs={{0,1},{1,0},{2,3},{3,2},{4,5},{5,4},{6,7},{7,6},{8,9},{9,8},{10,11... | collective-permute-start | bytes 1572872 | tf_op jit(solution)/shard_map/ppermute | solution.py:849
  124.8 15.3 %collective-permute-start.39 = (bf16[352,512]{1,0:T(8,128)(2,1)}, bf16[352,512]{1,0:T(8,128)(2,1)}, u32[]{:S(2)}, u32[]{:S(2)}) collective-permute-start(bf16[352,512]{1,0:T(8,128)(2,1)} %shard_map.243), channel_id=1, source_target_pairs={{0,16},{16,0},{1,17},{17,1},{2,18},{18,2},{3,19},{19,3},{4,20},{20... | collective-permute-start | bytes 1081352 | tf_op jit(solution)/shard_map/ppermute | solution.py:849
  141.7 19.5 %collective-permute-start.45 = (bf16[2,8,144,256]{3,2,1,0:T(8,128)(2,1)S(1)}, bf16[2,8,144,256]{3,2,1,0:T(8,128)(2,1)S(1)}, u32[]{:S(2)}, u32[]{:S(2)}) collective-permute-start(bf16[2,8,144,256]{3,2,1,0:T(8,128)(2,1)S(1)} %shard_map.248), channel_id=1, source_target_pairs={{0,8},{8,0},{1,9},{9,1},{2,10},{10,2},{3,11},{11,3},{4,12},{12,4},... | collective-permute-start | bytes 3538952 | tf_op jit(solution)/shard_map/ppermute | solution.py:849
  145.7 15.6 %collective-permute-start.50 = (bf16[1024,256]{1,0:T(8,128)(2,1)S(1)}, bf16[1024,256]{1,0:T(8,128)(2,1)S(1)}, u32[]{:S(2)}, u32[]{:S(2)}) collective-permute-start(bf16[1024,256]{1,0:T(8,128)(2,1)S(1)} %get-tuple-element.184.refs_1_), channel_id=1, source_target_pairs={{0,16},{16,0},{1,17},{17,1},{2,18},{18,2},{3,19},{19,3},{4,20},{20... | collective-permute-start | bytes 1572872 | tf_op jit(solution)/shard_map/ppermute | solution.py:849
  146.8 14.4 %collective-permute-start.49 = (bf16[352,512]{1,0:T(8,128)(2,1)S(1)}, bf16[352,512]{1,0:T(8,128)(2,1)S(1)}, u32[]{:S(2)}, u32[]{:S(2)}) collective-permute-start(bf16[352,512]{1,0:T(8,128)(2,1)S(1)} %get-tuple-element.191), channel_id=1, source_target_pairs={{0,0},{2,2},{4,8},{6,10},{8,4},{10,6},{12,12},{14,14},{1,1},{3,3},... | collective-permute-start | bytes 1081352 | tf_op jit(solution)/shard_map/ppermute | solution.py:980
  147.8 18.3 %collective-permute-start.44 = (bf16[512,640]{1,0:T(8,128)(2,1)S(1)}, bf16[512,640]{1,0:T(8,128)(2,1)S(1)}, u32[]{:S(2)}, u32[]{:S(2)}) collective-permute-start(bf16[512,640]{1,0:T(8,128)(2,1)S(1)} %copy-done.64), channel_id=1, source_target_pairs={{0,1},{1,0},{2,3},{3,2},{4,5},{5,4},{6,7},{7,6},{8,9},{9,8},{10,11... | collective-permute-start | bytes 1966088 | tf_op jit(solution)/shard_map/ppermute | solution.py:849
  162.5 22.1 %collective-permute-start.51 = (bf16[1088,256]{1,0:T(8,128)(2,1)}, bf16[1088,256]{1,0:T(8,128)(2,1)}, u32[]{:S(2)}, u32[]{:S(2)}) collective-permute-start(bf16[1088,256]{1,0:T(8,128)(2,1)} %get-tuple-element.195), channel_id=1, source_target_pairs={{0,1},{1,0},{2,3},{3,2},{4,5},{5,4},{6,7},{7,6},{8,9},{9,8},{10,11... | collective-permute-start | bytes 1671176 | tf_op jit(solution)/shard_map/ppermute | solution.py:849
  164.2 16.1 %collective-permute-start.53 = (bf16[576,256]{1,0:T(8,128)(2,1)}, bf16[576,256]{1,0:T(8,128)(2,1)}, u32[]{:S(2)}, u32[]{:S(2)}) collective-permute-start(bf16[576,256]{1,0:T(8,128)(2,1)} %get-tuple-element.197), channel_id=1, source_target_pairs={{0,17},{1,16},{16,1},{17,0},{2,19},{3,18},{18,3},{19,2},{4,21},{5,... | collective-permute-start | bytes 884744 | tf_op jit(solution)/shard_map/ppermute | solution.py:1020
  168.2 20.4 %collective-permute-start.46 = (bf16[128,768]{1,0:T(8,128)(2,1)}, bf16[128,768]{1,0:T(8,128)(2,1)}, u32[]{:S(2)}, u32[]{:S(2)}) collective-permute-start(bf16[128,768]{1,0:T(8,128)(2,1)} %get-tuple-element.186), channel_id=1, source_target_pairs={{0,2},{2,0},{4,6},{6,4},{1,3},{3,1},{5,7},{7,5},{8,10},{10,8},{12,... | collective-permute-start | bytes 589832 | tf_op jit(solution)/shard_map/ppermute | solution.py:853
  168.3 25.3 %collective-permute-start.47 = (bf16[128,768]{1,0:T(8,128)(2,1)}, bf16[128,768]{1,0:T(8,128)(2,1)S(1)}, u32[]{:S(2)}, u32[]{:S(2)}) collective-permute-start(bf16[128,768]{1,0:T(8,128)(2,1)} %copy-done.66), channel_id=1, source_target_pairs={{0,4},{2,6},{4,0},{6,2},{1,5},{3,7},{5,1},{7,3},{8,12},{10,14},{12... | collective-permute-start | bytes 589832 | tf_op jit(solution)/shard_map/ppermute | solution.py:853
  173.6 20.0 %collective-permute-start.48 = (bf16[128,768]{1,0:T(8,128)(2,1)}, bf16[128,768]{1,0:T(8,128)(2,1)S(1)}, u32[]{:S(2)}, u32[]{:S(2)}) collective-permute-start(bf16[128,768]{1,0:T(8,128)(2,1)} %copy-done.65), channel_id=1, source_target_pairs={{0,6},{2,4},{4,2},{6,0},{1,7},{3,5},{5,3},{7,1},{8,14},{10,12},{12... | collective-permute-start | bytes 589832 | tf_op jit(solution)/shard_map/ppermute | solution.py:853
  188.6 12.9 %collective-permute-start.55 = (bf16[272,256]{1,0:T(8,128)(2,1)S(1)}, bf16[272,256]{1,0:T(8,128)(2,1)S(1)}, u32[]{:S(2)}, u32[]{:S(2)}) collective-permute-start(bf16[272,256]{1,0:T(8,128)(2,1)S(1)} %get-tuple-element.201), channel_id=1, source_target_pairs={{0,4},{2,6},{4,0},{6,2},{1,5},{3,7},{5,1},{7,3},{8,12},{10,14},{12... | collective-permute-start | bytes 417800 | tf_op jit(solution)/shard_map/ppermute | solution.py:853
  188.6 12.9 %collective-permute-start.54 = (bf16[272,256]{1,0:T(8,128)(2,1)S(1)}, bf16[272,256]{1,0:T(8,128)(2,1)S(1)}, u32[]{:S(2)}, u32[]{:S(2)}) collective-permute-start(bf16[272,256]{1,0:T(8,128)(2,1)S(1)} %get-tuple-element.200), channel_id=1, source_target_pairs={{0,2},{2,0},{4,6},{6,4},{1,3},{3,1},{5,7},{7,5},{8,10},{10,8},{12,... | collective-permute-start | bytes 417800 | tf_op jit(solution)/shard_map/ppermute | solution.py:853
  (113 other events, 943.7 us)
